TPU v7x, 512 devices: a whole 4x8x8 slice. The times are simulated.
512 devices in a mesh: gx: 8 (over y), gy: 8 (over z), gz: 8 (over x, core).
Axes of the slice: x: 4, y: 8, z: 8, core: 2. Of those that a mesh axis runs over, the one named last changes fastest.
Arguments:
- kinematics: float32 [18, 131072], P(None, ('gx', 'gy', 'gz')), may hold values from -6 to 6
- pair_offsets: float32 [3, 16, 131072], P(None, None, ('gx', 'gy', 'gz')), may hold values from -1 to 1
- pair_index: int32 [16, 131072], P(None, ('gx', 'gy', 'gz')), may hold values from 0 to 687, as said below
- neighbour_count: int32 [131072], P(('gx', 'gy', 'gz')), may hold values from 1 to 16
- send_rows: int32 [27, 8192], P(None, ('gx', 'gy', 'gz')), may hold values from 0 to 255
- migrate_dir: int32 [131072], P(('gx', 'gy', 'gz')), may hold values from 0 to 26, as said below
- migrate_slot: int32 [131072], P(('gx', 'gy', 'gz')), may hold values from 0 to 3, as said below
- enc_node_w1: float32 [15, 128], replicated, may hold values from -1.5 to 1.5
- enc_node_w2: bfloat16 [128, 128], replicated, may hold values from -0.5 to 0.5
- enc_edge_w1: float32 [4, 128], replicated, may hold values from -3 to 3
- enc_edge_w2: bfloat16 [128, 128], replicated, may hold values from -0.5 to 0.5
- edge_w1: bfloat16 [3, 384, 128], replicated, may hold values from -0.3125 to 0.3125
- edge_w2: bfloat16 [3, 128, 128], replicated, may hold values from -0.5 to 0.5
- node_w1: bfloat16 [3, 256, 128], replicated, may hold values from -0.375 to 0.375
- node_w2: bfloat16 [3, 128, 128], replicated, may hold values from -0.5 to 0.5
- edge_gain: float32 [3, 128], replicated, may hold values from 0.25 to 1.75
- node_gain: float32 [3, 128], replicated, may hold values from 0.25 to 1.75
- dec_w1: bfloat16 [128, 128], replicated, may hold values from -0.5 to 0.5
- dec_w2: float32 [3, 128], replicated, may hold values from -0.5 to 0.5
Outputs:
- stayed: float32 [18, 131072], P(None, ('gx', 'gy', 'gz'))
- arrived: float32 [18, 55296], P(None, ('gx', 'gy', 'gz'))
Inputs may be any that keep to these rules, and one draw needn't show every extreme that they name: `pair_index`: A value below 256 names a row of the particle's own subdomain. A value v of 256 or more names ghost row v - 256; its direction (v - 256) // 16 is never 13 and points to a subdomain inside the grid. How many ghost rows of a direction are named differs between directions and subdomains. `migrate_dir`: A value other than 13 points to a subdomain inside the grid. On one subdomain at most 4 particles share a direction, and on every subdomain some direction has exactly 4. `migrate_slot`: among the particles of one subdomain that leave in one direction the slots are distinct; for staying particles the slot means nothing.
All inputs are finite; a program needn't handle non-finite values.
Results may differ from a plain program's by a relative error of at most 0.0085.
Values may be sent and summed in bfloat16 or wider, within the bound.
No kernel may reach another device: no remote copies, remote signals or barrier semaphores. Data moves between devices by JAX's collectives and lax.ppermute only.
A program may use at most 64 MiB of HBM per device.

v0:
```python
import jax
import jax.numpy as jnp
from jax import lax
from jax.sharding import PartitionSpec as P

MIG = 4


norm_eps = 1e-05


def shifted(value, axis, steps):
    count = lax.axis_size(axis)
    first, last = (max(0, -steps), min(count, count - steps))
    return lax.ppermute(value, axis, [(source, source + steps) for source in range(first, last)])


def with_halo(shard, sides, width):
    for axis, dim in sides:
        count, length = (lax.axis_size(axis), shard.shape[dim])
        up = [(i, (i + 1) % count) for i in range(count - 1)]
        down = [(j, i) for i, j in up]
        last = lax.slice_in_dim(shard, length - width, length, axis=dim)
        first = lax.slice_in_dim(shard, 0, width, axis=dim)
        before = lax.ppermute(last, axis, up)
        after = lax.ppermute(first, axis, down)
        shard = jnp.concatenate([before, shard, after], axis=dim)
    return shard


def layer_norm(values):
    center = values - jnp.mean(values, axis=-1, keepdims=True)
    spread = jnp.mean(center * center, axis=-1, keepdims=True)
    return center * lax.rsqrt(spread + norm_eps)


def encode_edges(offsets, first_weight, second_weight):
    squared = jnp.sum(offsets * offsets, axis=0, keepdims=True)
    features = jnp.concatenate([offsets, squared], axis=0)
    hidden = jnp.maximum(jnp.einsum("ckp,ch->kph", features, first_weight), 0.0).astype(
        jnp.bfloat16
    )
    pair_slots, particles, inner_width = hidden.shape
    result = jnp.dot(
        hidden.reshape(pair_slots * particles, inner_width),
        second_weight,
        preferred_element_type=jnp.float32,
    )
    return (
        layer_norm(result)
        .astype(jnp.bfloat16)
        .reshape(pair_slots, particles, second_weight.shape[1])
    )


def message_round(
    latent,
    extended,
    edge_latent,
    pair_index,
    neighbour_count,
    edge_first,
    edge_second,
    node_first,
    node_second,
    edge_scale,
    node_scale,
    block_pairs,
):
    latent_width = latent.shape[1]
    pair_slots, particles = pair_index.shape
    sender_proj = jnp.dot(
        extended, edge_first[2 * latent_width :], preferred_element_type=jnp.float32
    )
    receiver_proj = jnp.dot(
        latent, edge_first[latent_width : 2 * latent_width], preferred_element_type=jnp.float32
    )
    summed = jnp.zeros((particles, edge_second.shape[1]), jnp.float32)
    for first_pair in range(0, pair_slots, block_pairs):
        chosen = pair_index[first_pair : first_pair + block_pairs]
        edge_rows = edge_latent[first_pair : first_pair + block_pairs].reshape(
            block_pairs * particles, latent_width
        )
        pre_act = jnp.dot(
            edge_rows, edge_first[:latent_width], preferred_element_type=jnp.float32
        ).reshape(block_pairs, particles, -1)
        pre_act = pre_act + receiver_proj[None] + sender_proj[chosen]
        hidden = jnp.maximum(pre_act, 0.0).astype(jnp.bfloat16)
        message = (
            layer_norm(
                jnp.dot(
                    hidden.reshape(block_pairs * particles, -1),
                    edge_second,
                    preferred_element_type=jnp.float32,
                )
            )
            * edge_scale
        )
        message = message.reshape(block_pairs, particles, -1)
        usable = (first_pair + jnp.arange(block_pairs, dtype=jnp.int32))[:, None] < neighbour_count[
            None, :
        ]
        summed = summed + jnp.sum(jnp.where(usable[:, :, None], message, 0.0), axis=0)
    aggregate = summed.astype(jnp.bfloat16)
    node_pre = jnp.dot(
        latent, node_first[:latent_width], preferred_element_type=jnp.float32
    ) + jnp.dot(aggregate, node_first[latent_width:], preferred_element_type=jnp.float32)
    node_mid = jnp.maximum(node_pre, 0.0).astype(jnp.bfloat16)
    update = (
        layer_norm(jnp.dot(node_mid, node_second, preferred_element_type=jnp.float32)) * node_scale
    )
    return (latent.astype(jnp.float32) + update).astype(jnp.bfloat16)


def along_x(payload, offset):
    return shifted(payload, "gx", offset)


def along_y(payload, offset):
    return shifted(payload, "gy", offset)


def along_z(payload, offset):
    return shifted(payload, "gz", offset)


def forward_section(outbox, axis_dim, mover):
    higher = lax.index_in_dim(outbox, 2, axis_dim, keepdims=False)
    middle = lax.index_in_dim(outbox, 1, axis_dim, keepdims=False)
    lowest = lax.index_in_dim(outbox, 0, axis_dim, keepdims=False)
    return jnp.stack([mover(higher, 1), middle, mover(lowest, -1)], axis=axis_dim)


def on_device(
    kinematics,
    pair_offsets,
    pair_index,
    neighbour_count,
    send_rows,
    migrate_dir,
    migrate_slot,
    enc_node_w1,
    enc_node_w2,
    enc_edge_w1,
    enc_edge_w2,
    edge_w1,
    edge_w2,
    node_w1,
    node_w2,
    edge_gain,
    node_gain,
    dec_w1,
    dec_w2,
):
    latent_width = enc_node_w2.shape[1]
    pair_slots = pair_index.shape[0]
    ghost_count = send_rows.shape[1]
    state_rows = kinematics.shape[0]
    node_hidden = jnp.maximum(jnp.einsum("cn,ch->nh", kinematics[3:], enc_node_w1), 0.0).astype(
        jnp.bfloat16
    )
    latent = layer_norm(
        jnp.dot(node_hidden, enc_node_w2, preferred_element_type=jnp.float32)
    ).astype(jnp.bfloat16)
    edge_latent = jnp.concatenate(
        [
            encode_edges(pair_offsets[:, first_pair : first_pair + 2], enc_edge_w1, enc_edge_w2)
            for first_pair in range(0, pair_slots, 2)
        ],
        axis=0,
    )
    for round_index in range(edge_w1.shape[0]):
        outbox = latent[send_rows.reshape(-1)].reshape(3, 3, 3, ghost_count, latent_width)
        ghosts = forward_section(
            forward_section(forward_section(outbox, 0, along_x), 1, along_y), 2, along_z
        )
        extended = jnp.concatenate([latent, ghosts.reshape(27 * ghost_count, latent_width)], axis=0)
        latent = message_round(
            latent,
            extended,
            edge_latent,
            pair_index,
            neighbour_count,
            edge_w1[round_index],
            edge_w2[round_index],
            node_w1[round_index],
            node_w2[round_index],
            edge_gain[round_index],
            node_gain[round_index],
            2,
        )
    decode_hidden = jnp.maximum(
        jnp.dot(latent, dec_w1, preferred_element_type=jnp.float32), 0.0
    ).astype(jnp.bfloat16)
    acceleration = jnp.einsum("ch,nh->cn", dec_w2, decode_hidden.astype(jnp.float32))
    velocity = kinematics[state_rows - 3 :] + acceleration
    new_state = jnp.concatenate([kinematics[:3] + velocity, kinematics[6:], velocity], axis=0)
    staying = migrate_dir == 13
    stayed = jnp.where(staying[None, :], new_state, 0.0)
    target_code = jnp.where(staying, -1, migrate_dir * MIG + migrate_slot)
    picker = (target_code[None, :] == jnp.arange(27 * MIG, dtype=jnp.int32)[:, None]).astype(
        jnp.float32
    )
    outgoing = jnp.einsum("qp,sp->qs", picker, new_state).reshape(3, 3, 3, MIG, state_rows)
    landed = with_halo(outgoing, (("gx", 0), ("gy", 1), ("gz", 2)), 1)
    arrived = landed[0::2, 0::2, 0::2].reshape(27 * MIG, state_rows).T
    return (stayed, arrived)


def solution(mesh):
    return jax.shard_map(
        on_device,
        mesh=mesh,
        in_specs=(
            P(None, ("gx", "gy", "gz")),
            P(None, None, ("gx", "gy", "gz")),
            P(None, ("gx", "gy", "gz")),
            P(("gx", "gy", "gz")),
            P(None, ("gx", "gy", "gz")),
            P(("gx", "gy", "gz")),
            P(("gx", "gy", "gz")),
            P(),
            P(),
            P(),
            P(),
            P(),
            P(),
            P(),
            P(),
            P(),
            P(),
            P(),
            P(),
        ),
        out_specs=(P(None, ("gx", "gy", "gz")), P(None, ("gx", "gy", "gz"))),
        check_vma=False,
    )
```

profile of v0, /device:TPU:1, one launch (start us, length us, event | category | flops | bytes accessed | tf_op | source)
XLA Modules:
  0.0 229.0 jit_solution(2907848693452456751)
XLA Ops:
  6.7 4.7 %collective-permute-start = (bf16[3,3,16,128]{3,2,1,0:T(8,128)(2,1)S(1)}, bf16[3,3,16,128]{3,2,1,0:T(8,128)(2,1)S(1)}, u32[]{:S(2)}, u32[]{:S(2)}) collective-permute-start(bf16[3,3,16,128]{3,2,1,0:T(8,128)(2,1)S(1)} %bitcast.701), channel_id=1, source_target_pairs={{0,64},{64,128},{128,192},{192,256},{256,320},{320,384},{384,448},... | collective-permute-start | bytes 110600 | tf_op jit(solution)/shard_map/ppermute | solution.py:15
  26.2 4.2 %collective-permute-start.2 = (bf16[3,3,16,128]{3,2,0,1:T(8,128)(2,1)S(1)}, bf16[3,3,16,128]{3,2,0,1:T(8,128)(2,1)S(1)}, u32[]{:S(2)}, u32[]{:S(2)}) collective-permute-start(bf16[3,3,16,128]{3,2,0,1:T(8,128)(2,1)S(1)} %get-tuple-element.27), channel_id=1, source_target_pairs={{0,8},{8,16},{16,24},{24,32},{32,40},{40,48},{48,56},{1,9},{9,17},... | collective-permute-start | bytes 110600 | tf_op jit(solution)/shard_map/ppermute | solution.py:15
  31.7 4.0 %collective-permute-done.3 = bf16[3,3,16,128]{3,2,0,1:T(8,128)(2,1)S(1)} collective-permute-done((bf16[3,3,16,128]{3,2,0,1:T(8,128)(2,1)S(1)}, bf16[3,3,16,128]{3,2,0,1:T(8,128)(2,1)S(1)}, u32[]{:S(2)}, u32[]{:S(2)}) %collective-permute-start.3) | collective-permute-done | bytes 36896 | tf_op jit(solution)/shard_map/ppermute | solution.py:15
  35.7 5.4 %collective-permute-start.4 = (bf16[3,3,16,128]{3,2,1,0:T(8,128)(2,1)S(1)}, bf16[3,3,16,128]{3,2,1,0:T(8,128)(2,1)S(1)}, u32[]{:S(2)}, u32[]{:S(2)}) collective-permute-start(bf16[3,3,16,128]{3,2,1,0:T(8,128)(2,1)S(1)} %get-tuple-element.24), channel_id=1, source_target_pairs={{0,1},{1,2},{2,3},{3,4},{4,5},{5,6},{6,7},{8,9},{9,10},{10,11},{11... | collective-permute-start | bytes 110600 | tf_op jit(solution)/shard_map/ppermute | solution.py:15
  41.1 2.4 %collective-permute-start.5 = (bf16[3,3,16,128]{3,2,1,0:T(8,128)(2,1)S(1)}, bf16[3,3,16,128]{3,2,1,0:T(8,128)(2,1)S(1)}, u32[]{:S(2)}, u32[]{:S(2)}) collective-permute-start(bf16[3,3,16,128]{3,2,1,0:T(8,128)(2,1)S(1)} %get-tuple-element.25), channel_id=1, source_target_pairs={{1,0},{2,1},{3,2},{4,3},{5,4},{6,5},{7,6},{9,8},{10,9},{11,10},{12... | collective-permute-start | bytes 110600 | tf_op jit(solution)/shard_map/ppermute | solution.py:15
  44.2 2.3 collective-permute-done.5
  83.1 3.2 %collective-permute-start.6 = (bf16[3,3,16,128]{3,2,1,0:T(8,128)(2,1)S(1)}, bf16[3,3,16,128]{3,2,1,0:T(8,128)(2,1)S(1)}, u32[]{:S(2)}, u32[]{:S(2)}) collective-permute-start(bf16[3,3,16,128]{3,2,1,0:T(8,128)(2,1)S(1)} %bitcast.723), channel_id=1, source_target_pairs={{0,64},{64,128},{128,192},{192,256},{256,320},{320,384},{384,448},... | collective-permute-start | bytes 110600 | tf_op jit(solution)/shard_map/ppermute | solution.py:15
  87.7 3.4 %collective-permute-done.7 = bf16[3,3,16,128]{3,2,1,0:T(8,128)(2,1)S(1)} collective-permute-done((bf16[3,3,16,128]{3,2,1,0:T(8,128)(2,1)S(1)}, bf16[3,3,16,128]{3,2,1,0:T(8,128)(2,1)S(1)}, u32[]{:S(2)}, u32[]{:S(2)}) %collective-permute-start.7) | collective-permute-done | bytes 36896 | tf_op jit(solution)/shard_map/ppermute | solution.py:15
  91.1 4.0 %collective-permute-start.8 = (bf16[3,3,16,128]{3,2,0,1:T(8,128)(2,1)S(1)}, bf16[3,3,16,128]{3,2,0,1:T(8,128)(2,1)S(1)}, u32[]{:S(2)}, u32[]{:S(2)}) collective-permute-start(bf16[3,3,16,128]{3,2,0,1:T(8,128)(2,1)S(1)} %get-tuple-element.18), channel_id=1, source_target_pairs={{0,8},{8,16},{16,24},{24,32},{32,40},{40,48},{48,56},{1,9},{9,17},... | collective-permute-start | bytes 110600 | tf_op jit(solution)/shard_map/ppermute | solution.py:15
  96.6 5.2 %collective-permute-done.9 = bf16[3,3,16,128]{3,2,0,1:T(8,128)(2,1)S(1)} collective-permute-done((bf16[3,3,16,128]{3,2,0,1:T(8,128)(2,1)S(1)}, bf16[3,3,16,128]{3,2,0,1:T(8,128)(2,1)S(1)}, u32[]{:S(2)}, u32[]{:S(2)}) %collective-permute-start.9) | collective-permute-done | bytes 36896 | tf_op jit(solution)/shard_map/ppermute | solution.py:15
  101.8 4.5 %collective-permute-start.10 = (bf16[3,3,16,128]{3,2,1,0:T(8,128)(2,1)S(1)}, bf16[3,3,16,128]{3,2,1,0:T(8,128)(2,1)S(1)}, u32[]{:S(2)}, u32[]{:S(2)}) collective-permute-start(bf16[3,3,16,128]{3,2,1,0:T(8,128)(2,1)S(1)} %get-tuple-element.15), channel_id=1, source_target_pairs={{0,1},{1,2},{2,3},{3,4},{4,5},{5,6},{6,7},{8,9},{9,10},{10,11},{11... | collective-permute-start | bytes 110600 | tf_op jit(solution)/shard_map/ppermute | solution.py:15
  109.4 2.2 collective-permute-done.11
  142.6 3.8 %collective-permute-start.12 = (bf16[3,3,16,128]{3,2,1,0:T(8,128)(2,1)S(1)}, bf16[3,3,16,128]{3,2,1,0:T(8,128)(2,1)S(1)}, u32[]{:S(2)}, u32[]{:S(2)}) collective-permute-start(bf16[3,3,16,128]{3,2,1,0:T(8,128)(2,1)S(1)} %bitcast.717), channel_id=1, source_target_pairs={{0,64},{64,128},{128,192},{192,256},{256,320},{320,384},{384,448},... | collective-permute-start | bytes 110600 | tf_op jit(solution)/shard_map/ppermute | solution.py:15
  147.8 3.8 %collective-permute-done.13 = bf16[3,3,16,128]{3,2,1,0:T(8,128)(2,1)S(1)} collective-permute-done((bf16[3,3,16,128]{3,2,1,0:T(8,128)(2,1)S(1)}, bf16[3,3,16,128]{3,2,1,0:T(8,128)(2,1)S(1)}, u32[]{:S(2)}, u32[]{:S(2)}) %collective-permute-start.13) | collective-permute-done | bytes 36896 | tf_op jit(solution)/shard_map/ppermute | solution.py:15
  151.6 4.8 %collective-permute-start.14 = (bf16[3,3,16,128]{3,2,0,1:T(8,128)(2,1)S(1)}, bf16[3,3,16,128]{3,2,0,1:T(8,128)(2,1)S(1)}, u32[]{:S(2)}, u32[]{:S(2)}) collective-permute-start(bf16[3,3,16,128]{3,2,0,1:T(8,128)(2,1)S(1)} %get-tuple-element.9), channel_id=1, source_target_pairs={{0,8},{8,16},{16,24},{24,32},{32,40},{40,48},{48,56},{1,9},{9,17},... | collective-permute-start | bytes 110600 | tf_op jit(solution)/shard_map/ppermute | solution.py:15
  157.9 3.5 %collective-permute-done.15 = bf16[3,3,16,128]{3,2,0,1:T(8,128)(2,1)S(1)} collective-permute-done((bf16[3,3,16,128]{3,2,0,1:T(8,128)(2,1)S(1)}, bf16[3,3,16,128]{3,2,0,1:T(8,128)(2,1)S(1)}, u32[]{:S(2)}, u32[]{:S(2)}) %collective-permute-start.15) | collective-permute-done | bytes 36896 | tf_op jit(solution)/shard_map/ppermute | solution.py:15
  161.5 4.3 %collective-permute-start.16 = (bf16[3,3,16,128]{3,2,1,0:T(8,128)(2,1)S(1)}, bf16[3,3,16,128]{3,2,1,0:T(8,128)(2,1)S(1)}, u32[]{:S(2)}, u32[]{:S(2)}) collective-permute-start(bf16[3,3,16,128]{3,2,1,0:T(8,128)(2,1)S(1)} %get-tuple-element.6), channel_id=1, source_target_pairs={{0,1},{1,2},{2,3},{3,4},{4,5},{5,6},{6,7},{8,9},{9,10},{10,11},{11... | collective-permute-start | bytes 110600 | tf_op jit(solution)/shard_map/ppermute | solution.py:15
  165.7 2.2 collective-permute-start.17
  200.5 4.4 %collective-permute-start.18 = (f32[1,3,3,4,18]{4,3,2,1,0:T(4,128)S(1)}, f32[1,3,3,4,18]{4,3,2,1,0:T(4,128)S(1)}, u32[]{:S(2)}, u32[]{:S(2)}) collective-permute-start(f32[1,3,3,4,18]{4,3,2,1,0:T(4,128)S(1)} %slice.460), channel_id=1, source_target_pairs={{0,64},{64,128},{128,192},{192,256},{256,320},{320,384},{384,448},... | collective-permute-start | bytes 7784 | tf_op jit(solution)/shard_map/ppermute | solution.py:25
  206.6 3.4 %collective-permute-done.19 = f32[1,3,3,4,18]{4,3,2,1,0:T(4,128)S(1)} collective-permute-done((f32[1,3,3,4,18]{4,3,2,1,0:T(4,128)S(1)}, f32[1,3,3,4,18]{4,3,2,1,0:T(4,128)S(1)}, u32[]{:S(2)}, u32[]{:S(2)}) %collective-permute-start.19) | collective-permute-done | bytes 2624 | tf_op jit(solution)/shard_map/ppermute | solution.py:26
  210.0 3.6 %collective-permute-start.20 = (f32[5,1,3,4,18]{4,3,2,1,0:T(4,128)S(1)}, f32[5,1,3,4,18]{4,3,2,1,0:T(4,128)S(1)}, u32[]{:S(2)}, u32[]{:S(2)}) collective-permute-start(f32[5,1,3,4,18]{4,3,2,1,0:T(4,128)S(1)} %get-tuple-element.33), channel_id=1, source_target_pairs={{0,8},{8,16},{16,24},{24,32},{32,40},{40,48},{48,56},{1,9},{9,17},... | collective-permute-start | bytes 12968 | tf_op jit(solution)/shard_map/ppermute | solution.py:25
  214.9 3.4 %collective-permute-done.21 = f32[5,1,3,4,18]{4,3,2,1,0:T(4,128)S(1)} collective-permute-done((f32[5,1,3,4,18]{4,3,2,1,0:T(4,128)S(1)}, f32[5,1,3,4,18]{4,3,2,1,0:T(4,128)S(1)}, u32[]{:S(2)}, u32[]{:S(2)}) %collective-permute-start.21) | collective-permute-done | bytes 4352 | tf_op jit(solution)/shard_map/ppermute | solution.py:26
  218.4 4.4 %collective-permute-start.22 = (f32[5,5,1,4,18]{4,3,2,1,0:T(4,128)S(1)}, f32[5,5,1,4,18]{4,3,2,1,0:T(4,128)S(1)}, u32[]{:S(2)}, u32[]{:S(2)}) collective-permute-start(f32[5,5,1,4,18]{4,3,2,1,0:T(4,128)S(1)} %get-tuple-element.4), channel_id=1, source_target_pairs={{0,1},{1,2},{2,3},{3,4},{4,5},{5,6},{6,7},{8,9},{9,10},{10,11},{11... | collective-permute-start | bytes 21608 | tf_op jit(solution)/shard_map/ppermute | solution.py:25
  225.3 2.9 %collective-permute-done.23 = f32[5,5,1,4,18]{4,3,2,1,0:T(4,128)S(1)} collective-permute-done((f32[5,5,1,4,18]{4,3,2,1,0:T(4,128)S(1)}, f32[5,5,1,4,18]{4,3,2,1,0:T(4,128)S(1)}, u32[]{:S(2)}, u32[]{:S(2)}) %collective-permute-start.23) | collective-permute-done | bytes 7232 | tf_op jit(solution)/shard_map/ppermute | solution.py:26
  (539 shorter events, 135.8 us)
Async XLA Ops:
  5.4 20.7 %collective-permute-start.1 = (bf16[3,3,16,128]{3,2,1,0:T(8,128)(2,1)S(1)}, bf16[3,3,16,128]{3,2,1,0:T(8,128)(2,1)S(1)}, u32[]{:S(2)}, u32[]{:S(2)}) collective-permute-start(bf16[3,3,16,128]{3,2,1,0:T(8,128)(2,1)S(1)} %bitcast.703), channel_id=1, source_target_pairs={{64,0},{128,64},{192,128},{256,192},{320,256},{384,320},{448,384},... | collective-permute-start | bytes 110600 | tf_op jit(solution)/shard_map/ppermute | solution.py:15
  6.7 19.4 %collective-permute-start = (bf16[3,3,16,128]{3,2,1,0:T(8,128)(2,1)S(1)}, bf16[3,3,16,128]{3,2,1,0:T(8,128)(2,1)S(1)}, u32[]{:S(2)}, u32[]{:S(2)}) collective-permute-start(bf16[3,3,16,128]{3,2,1,0:T(8,128)(2,1)S(1)} %bitcast.701), channel_id=1, source_target_pairs={{0,64},{64,128},{128,192},{192,256},{256,320},{320,384},{384,448},... | collective-permute-start | bytes 110600 | tf_op jit(solution)/shard_map/ppermute | solution.py:15
  26.2 5.5 %collective-permute-start.2 = (bf16[3,3,16,128]{3,2,0,1:T(8,128)(2,1)S(1)}, bf16[3,3,16,128]{3,2,0,1:T(8,128)(2,1)S(1)}, u32[]{:S(2)}, u32[]{:S(2)}) collective-permute-start(bf16[3,3,16,128]{3,2,0,1:T(8,128)(2,1)S(1)} %get-tuple-element.27), channel_id=1, source_target_pairs={{0,8},{8,16},{16,24},{24,32},{32,40},{40,48},{48,56},{1,9},{9,17},... | collective-permute-start | bytes 110600 | tf_op jit(solution)/shard_map/ppermute | solution.py:15
  30.4 5.3 %collective-permute-start.3 = (bf16[3,3,16,128]{3,2,0,1:T(8,128)(2,1)S(1)}, bf16[3,3,16,128]{3,2,0,1:T(8,128)(2,1)S(1)}, u32[]{:S(2)}, u32[]{:S(2)}) collective-permute-start(bf16[3,3,16,128]{3,2,0,1:T(8,128)(2,1)S(1)} %get-tuple-element.28), channel_id=1, source_target_pairs={{8,0},{16,8},{24,16},{32,24},{40,32},{48,40},{56,48},{9,1},{17,9},... | collective-permute-start | bytes 110600 | tf_op jit(solution)/shard_map/ppermute | solution.py:15
  35.7 8.4 %collective-permute-start.4 = (bf16[3,3,16,128]{3,2,1,0:T(8,128)(2,1)S(1)}, bf16[3,3,16,128]{3,2,1,0:T(8,128)(2,1)S(1)}, u32[]{:S(2)}, u32[]{:S(2)}) collective-permute-start(bf16[3,3,16,128]{3,2,1,0:T(8,128)(2,1)S(1)} %get-tuple-element.24), channel_id=1, source_target_pairs={{0,1},{1,2},{2,3},{3,4},{4,5},{5,6},{6,7},{8,9},{9,10},{10,11},{11... | collective-permute-start | bytes 110600 | tf_op jit(solution)/shard_map/ppermute | solution.py:15
  41.1 5.3 %collective-permute-start.5 = (bf16[3,3,16,128]{3,2,1,0:T(8,128)(2,1)S(1)}, bf16[3,3,16,128]{3,2,1,0:T(8,128)(2,1)S(1)}, u32[]{:S(2)}, u32[]{:S(2)}) collective-permute-start(bf16[3,3,16,128]{3,2,1,0:T(8,128)(2,1)S(1)} %get-tuple-element.25), channel_id=1, source_target_pairs={{1,0},{2,1},{3,2},{4,3},{5,4},{6,5},{7,6},{9,8},{10,9},{11,10},{12... | collective-permute-start | bytes 110600 | tf_op jit(solution)/shard_map/ppermute | solution.py:15
  83.1 4.5 %collective-permute-start.6 = (bf16[3,3,16,128]{3,2,1,0:T(8,128)(2,1)S(1)}, bf16[3,3,16,128]{3,2,1,0:T(8,128)(2,1)S(1)}, u32[]{:S(2)}, u32[]{:S(2)}) collective-permute-start(bf16[3,3,16,128]{3,2,1,0:T(8,128)(2,1)S(1)} %bitcast.723), channel_id=1, source_target_pairs={{0,64},{64,128},{128,192},{192,256},{256,320},{320,384},{384,448},... | collective-permute-start | bytes 110600 | tf_op jit(solution)/shard_map/ppermute | solution.py:15
  86.4 4.7 %collective-permute-start.7 = (bf16[3,3,16,128]{3,2,1,0:T(8,128)(2,1)S(1)}, bf16[3,3,16,128]{3,2,1,0:T(8,128)(2,1)S(1)}, u32[]{:S(2)}, u32[]{:S(2)}) collective-permute-start(bf16[3,3,16,128]{3,2,1,0:T(8,128)(2,1)S(1)} %bitcast.715), channel_id=1, source_target_pairs={{64,0},{128,64},{192,128},{256,192},{320,256},{384,320},{448,384},... | collective-permute-start | bytes 110600 | tf_op jit(solution)/shard_map/ppermute | solution.py:15
  91.1 5.5 %collective-permute-start.8 = (bf16[3,3,16,128]{3,2,0,1:T(8,128)(2,1)S(1)}, bf16[3,3,16,128]{3,2,0,1:T(8,128)(2,1)S(1)}, u32[]{:S(2)}, u32[]{:S(2)}) collective-permute-start(bf16[3,3,16,128]{3,2,0,1:T(8,128)(2,1)S(1)} %get-tuple-element.18), channel_id=1, source_target_pairs={{0,8},{8,16},{16,24},{24,32},{32,40},{40,48},{48,56},{1,9},{9,17},... | collective-permute-start | bytes 110600 | tf_op jit(solution)/shard_map/ppermute | solution.py:15
  95.1 6.7 %collective-permute-start.9 = (bf16[3,3,16,128]{3,2,0,1:T(8,128)(2,1)S(1)}, bf16[3,3,16,128]{3,2,0,1:T(8,128)(2,1)S(1)}, u32[]{:S(2)}, u32[]{:S(2)}) collective-permute-start(bf16[3,3,16,128]{3,2,0,1:T(8,128)(2,1)S(1)} %get-tuple-element.19), channel_id=1, source_target_pairs={{8,0},{16,8},{24,16},{32,24},{40,32},{48,40},{56,48},{9,1},{17,9},... | collective-permute-start | bytes 110600 | tf_op jit(solution)/shard_map/ppermute | solution.py:15
  101.8 7.5 %collective-permute-start.10 = (bf16[3,3,16,128]{3,2,1,0:T(8,128)(2,1)S(1)}, bf16[3,3,16,128]{3,2,1,0:T(8,128)(2,1)S(1)}, u32[]{:S(2)}, u32[]{:S(2)}) collective-permute-start(bf16[3,3,16,128]{3,2,1,0:T(8,128)(2,1)S(1)} %get-tuple-element.15), channel_id=1, source_target_pairs={{0,1},{1,2},{2,3},{3,4},{4,5},{5,6},{6,7},{8,9},{9,10},{10,11},{11... | collective-permute-start | bytes 110600 | tf_op jit(solution)/shard_map/ppermute | solution.py:15
  106.3 5.3 %collective-permute-start.11 = (bf16[3,3,16,128]{3,2,1,0:T(8,128)(2,1)S(1)}, bf16[3,3,16,128]{3,2,1,0:T(8,128)(2,1)S(1)}, u32[]{:S(2)}, u32[]{:S(2)}) collective-permute-start(bf16[3,3,16,128]{3,2,1,0:T(8,128)(2,1)S(1)} %get-tuple-element.16), channel_id=1, source_target_pairs={{1,0},{2,1},{3,2},{4,3},{5,4},{6,5},{7,6},{9,8},{10,9},{11,10},{12... | collective-permute-start | bytes 110600 | tf_op jit(solution)/shard_map/ppermute | solution.py:15
  142.6 5.2 %collective-permute-start.12 = (bf16[3,3,16,128]{3,2,1,0:T(8,128)(2,1)S(1)}, bf16[3,3,16,128]{3,2,1,0:T(8,128)(2,1)S(1)}, u32[]{:S(2)}, u32[]{:S(2)}) collective-permute-start(bf16[3,3,16,128]{3,2,1,0:T(8,128)(2,1)S(1)} %bitcast.717), channel_id=1, source_target_pairs={{0,64},{64,128},{128,192},{192,256},{256,320},{320,384},{384,448},... | collective-permute-start | bytes 110600 | tf_op jit(solution)/shard_map/ppermute | solution.py:15
  146.4 5.1 %collective-permute-start.13 = (bf16[3,3,16,128]{3,2,1,0:T(8,128)(2,1)S(1)}, bf16[3,3,16,128]{3,2,1,0:T(8,128)(2,1)S(1)}, u32[]{:S(2)}, u32[]{:S(2)}) collective-permute-start(bf16[3,3,16,128]{3,2,1,0:T(8,128)(2,1)S(1)} %bitcast.709), channel_id=1, source_target_pairs={{64,0},{128,64},{192,128},{256,192},{320,256},{384,320},{448,384},... | collective-permute-start | bytes 110600 | tf_op jit(solution)/shard_map/ppermute | solution.py:15
  151.6 6.3 %collective-permute-start.14 = (bf16[3,3,16,128]{3,2,0,1:T(8,128)(2,1)S(1)}, bf16[3,3,16,128]{3,2,0,1:T(8,128)(2,1)S(1)}, u32[]{:S(2)}, u32[]{:S(2)}) collective-permute-start(bf16[3,3,16,128]{3,2,0,1:T(8,128)(2,1)S(1)} %get-tuple-element.9), channel_id=1, source_target_pairs={{0,8},{8,16},{16,24},{24,32},{32,40},{40,48},{48,56},{1,9},{9,17},... | collective-permute-start | bytes 110600 | tf_op jit(solution)/shard_map/ppermute | solution.py:15
  156.4 5.0 %collective-permute-start.15 = (bf16[3,3,16,128]{3,2,0,1:T(8,128)(2,1)S(1)}, bf16[3,3,16,128]{3,2,0,1:T(8,128)(2,1)S(1)}, u32[]{:S(2)}, u32[]{:S(2)}) collective-permute-start(bf16[3,3,16,128]{3,2,0,1:T(8,128)(2,1)S(1)} %get-tuple-element.10), channel_id=1, source_target_pairs={{8,0},{16,8},{24,16},{32,24},{40,32},{48,40},{56,48},{9,1},{17,9},... | collective-permute-start | bytes 110600 | tf_op jit(solution)/shard_map/ppermute | solution.py:15
  161.5 7.4 %collective-permute-start.16 = (bf16[3,3,16,128]{3,2,1,0:T(8,128)(2,1)S(1)}, bf16[3,3,16,128]{3,2,1,0:T(8,128)(2,1)S(1)}, u32[]{:S(2)}, u32[]{:S(2)}) collective-permute-start(bf16[3,3,16,128]{3,2,1,0:T(8,128)(2,1)S(1)} %get-tuple-element.6), channel_id=1, source_target_pairs={{0,1},{1,2},{2,3},{3,4},{4,5},{5,6},{6,7},{8,9},{9,10},{10,11},{11... | collective-permute-start | bytes 110600 | tf_op jit(solution)/shard_map/ppermute | solution.py:15
  165.7 5.3 %collective-permute-start.17 = (bf16[3,3,16,128]{3,2,1,0:T(8,128)(2,1)S(1)}, bf16[3,3,16,128]{3,2,1,0:T(8,128)(2,1)S(1)}, u32[]{:S(2)}, u32[]{:S(2)}) collective-permute-start(bf16[3,3,16,128]{3,2,1,0:T(8,128)(2,1)S(1)} %get-tuple-element.7), channel_id=1, source_target_pairs={{1,0},{2,1},{3,2},{4,3},{5,4},{6,5},{7,6},{9,8},{10,9},{11,10},{12... | collective-permute-start | bytes 110600 | tf_op jit(solution)/shard_map/ppermute | solution.py:15
  200.5 6.0 %collective-permute-start.18 = (f32[1,3,3,4,18]{4,3,2,1,0:T(4,128)S(1)}, f32[1,3,3,4,18]{4,3,2,1,0:T(4,128)S(1)}, u32[]{:S(2)}, u32[]{:S(2)}) collective-permute-start(f32[1,3,3,4,18]{4,3,2,1,0:T(4,128)S(1)} %slice.460), channel_id=1, source_target_pairs={{0,64},{64,128},{128,192},{192,256},{256,320},{320,384},{384,448},... | collective-permute-start | bytes 7784 | tf_op jit(solution)/shard_map/ppermute | solution.py:25
  205.2 4.7 %collective-permute-start.19 = (f32[1,3,3,4,18]{4,3,2,1,0:T(4,128)S(1)}, f32[1,3,3,4,18]{4,3,2,1,0:T(4,128)S(1)}, u32[]{:S(2)}, u32[]{:S(2)}) collective-permute-start(f32[1,3,3,4,18]{4,3,2,1,0:T(4,128)S(1)} %slice.462), channel_id=1, source_target_pairs={{64,0},{128,64},{192,128},{256,192},{320,256},{384,320},{448,384},... | collective-permute-start | bytes 7784 | tf_op jit(solution)/shard_map/ppermute | solution.py:26
  210.0 5.0 %collective-permute-start.20 = (f32[5,1,3,4,18]{4,3,2,1,0:T(4,128)S(1)}, f32[5,1,3,4,18]{4,3,2,1,0:T(4,128)S(1)}, u32[]{:S(2)}, u32[]{:S(2)}) collective-permute-start(f32[5,1,3,4,18]{4,3,2,1,0:T(4,128)S(1)} %get-tuple-element.33), channel_id=1, source_target_pairs={{0,8},{8,16},{16,24},{24,32},{32,40},{40,48},{48,56},{1,9},{9,17},... | collective-permute-start | bytes 12968 | tf_op jit(solution)/shard_map/ppermute | solution.py:25
  213.6 4.7 %collective-permute-start.21 = (f32[5,1,3,4,18]{4,3,2,1,0:T(4,128)S(1)}, f32[5,1,3,4,18]{4,3,2,1,0:T(4,128)S(1)}, u32[]{:S(2)}, u32[]{:S(2)}) collective-permute-start(f32[5,1,3,4,18]{4,3,2,1,0:T(4,128)S(1)} %get-tuple-element.34), channel_id=1, source_target_pairs={{8,0},{16,8},{24,16},{32,24},{40,32},{48,40},{56,48},{9,1},{17,9},... | collective-permute-start | bytes 12968 | tf_op jit(solution)/shard_map/ppermute | solution.py:26
  218.4 7.0 %collective-permute-start.22 = (f32[5,5,1,4,18]{4,3,2,1,0:T(4,128)S(1)}, f32[5,5,1,4,18]{4,3,2,1,0:T(4,128)S(1)}, u32[]{:S(2)}, u32[]{:S(2)}) collective-permute-start(f32[5,5,1,4,18]{4,3,2,1,0:T(4,128)S(1)} %get-tuple-element.4), channel_id=1, source_target_pairs={{0,1},{1,2},{2,3},{3,4},{4,5},{5,6},{6,7},{8,9},{9,10},{10,11},{11... | collective-permute-start | bytes 21608 | tf_op jit(solution)/shard_map/ppermute | solution.py:25
  222.8 5.4 %collective-permute-start.23 = (f32[5,5,1,4,18]{4,3,2,1,0:T(4,128)S(1)}, f32[5,5,1,4,18]{4,3,2,1,0:T(4,128)S(1)}, u32[]{:S(2)}, u32[]{:S(2)}) collective-permute-start(f32[5,5,1,4,18]{4,3,2,1,0:T(4,128)S(1)} %get-tuple-element.5), channel_id=1, source_target_pairs={{1,0},{2,1},{3,2},{4,3},{5,4},{6,5},{7,6},{9,8},{10,9},{11,10},{12... | collective-permute-start | bytes 21608 | tf_op jit(solution)/shard_map/ppermute | solution.py:26
  (88 other events, 270.0 us)
where the time goes:
time: 231 us; the launch traced here: 229 us
  starting transfers between devices  70.3 us (30%)
  local copies, waits for them, and re-layouts  66.9 us (29%)
  waiting for transfers between devices  36.3 us (16%)
  matrix products  27.6 us (12%)
  other arithmetic  24.7 us (11%)
  between operations  3.27 us (1%)
    ppermute x18, starting transfers between devices, shifted(): lax.ppermute(value, axis, [(source, source + steps) for source in range(f...  53.3 us
    unnamed x196, local copies, waits for them, and re-layouts  32.5 us
    gather x24, local copies, waits for them, and re-layouts, message_round(): pre_act = pre_act + receiver_proj[None] + sender_proj[chosen]  28 us
    ppermute x18, waiting for transfers between devices, shifted(): lax.ppermute(value, axis, [(source, source + steps) for source in range(f...  26.6 us
    ppermute x3, starting transfers between devices, with_halo(): before = lax.ppermute(last, axis, up)  12.5 us
    ppermute x3, waiting for transfers between devices, with_halo(): after = lax.ppermute(first, axis, down)  9.68 us
    reduce_sum x36, other arithmetic, layer_norm(): spread = jnp.mean(center * center, axis=-1, keepdims=True)  8.29 us
    dot_general x24, matrix products, message_round(): jnp.dot(hidden.reshape(block_pairs * particles, -1), edge_second, preferr...  7.12 us
  transfers between devices with their start and end apart: 24, of which 11 were waited for; matrix products, arithmetic and copies ran while one was open for 6% of the time, Pallas kernels for 0%

commit v1 on v0

v1 whole, which is shorter than its diff:
```python
import functools

import jax
import jax.numpy as jnp
from jax import lax
from jax.experimental import pallas as pl
from jax.experimental.pallas import tpu as pltpu
from jax.sharding import PartitionSpec as P

MIG = 4
EPS = 1e-05
F32 = jnp.float32
BF16 = jnp.bfloat16
VMEM_LIMIT = 48 * 1024 * 1024


def shifted(value, axis, steps):
    count = lax.axis_size(axis)
    first, last = (max(0, -steps), min(count, count - steps))
    return lax.ppermute(value, axis, [(source, source + steps) for source in range(first, last)])


def mm(a, b):
    return jnp.dot(a, b, preferred_element_type=F32)


def halves(value):
    high = value.astype(BF16)
    return high, (value - high.astype(F32)).astype(BF16)


def centred(weight):
    wide = weight.astype(F32)
    wide = wide - jnp.mean(wide, axis=-1, keepdims=True)
    return jnp.concatenate(halves(wide), axis=1)


def normalised(rows, weight):
    both = mm(rows, weight)
    width = both.shape[1] // 2
    center = both[:, :width] + both[:, width:]
    spread = jnp.mean(center * center, axis=-1, keepdims=True)
    return center, lax.rsqrt(spread + EPS)


def send_rows_of(latent, rows_ref, outs):
    particles = latent.shape[0]
    count = rows_ref.shape[0]
    picked = rows_ref[...] == lax.broadcasted_iota(jnp.int32, (count, particles), 1)
    chosen = mm(jnp.where(picked, 1.0, 0.0).astype(BF16), latent).astype(BF16)
    step = count // 3
    for index, out in enumerate(outs):
        out[...] = chosen[index * step : (index + 1) * step]


def node_kernel(kin_ref, w1_ref, w2_ref, rows_ref, latent_ref, low_ref, mid_ref, high_ref):
    features = kin_ref[3:, :]
    hidden = lax.dot_general(
        features,
        w1_ref[...],
        (((0,), (0,)), ((), ())),
        precision=lax.Precision.HIGHEST,
        preferred_element_type=F32,
    )
    hidden = jnp.maximum(hidden, 0.0).astype(BF16)
    center, scale = normalised(hidden, centred(w2_ref[...]))
    latent = (center * scale).astype(BF16)
    latent_ref[...] = latent
    send_rows_of(latent, rows_ref, (low_ref, mid_ref, high_ref))


def edge_kernel(off_ref, index_ref, count_ref, w1_ref, w2_ref, edge_ref, column_ref):
    slots, particles = index_ref.shape
    index = index_ref[...]
    place = index - particles
    slot = place & 15
    direction = place >> 4
    dx = (direction * 57) >> 9
    rest = direction - dx * 9
    dy = (rest * 11) >> 5
    dz = rest - dy * 3
    moved = particles + (dz * 9 + dx * 3 + dy) * 16 + slot
    index = jnp.where(index < particles, index, moved).astype(F32)
    count = count_ref[...].astype(F32)
    filler = jnp.zeros((128 - slots - count.shape[0], particles), F32)
    column_ref[...] = jnp.concatenate([index, count, filler], axis=0).T.astype(jnp.int32)

    offsets = [off_ref[c] for c in range(3)]
    square = offsets[0] * offsets[0] + offsets[1] * offsets[1] + offsets[2] * offsets[2]
    stack = jnp.concatenate(offsets + [square], axis=0)
    high = stack.astype(BF16).astype(F32)
    low = stack - high
    wide = jnp.concatenate([high, low, high, jnp.zeros_like(high)], axis=0).T.astype(BF16)
    first = w1_ref[...]
    width = first.shape[1]
    first_high = first.astype(BF16).astype(F32)
    first_low = first - first_high
    rows = [
        jnp.broadcast_to(part[c : c + 1], (slots, width))
        for part in (first_high, first_high, first_low, jnp.zeros_like(first))
        for c in range(4)
    ]
    table = jnp.concatenate(rows, axis=0)
    owner = lax.broadcasted_iota(jnp.int32, table.shape, 0) & (slots - 1)
    second = centred(w2_ref[...])
    for k in range(slots):
        chosen = jnp.where(owner == k, table, 0.0).astype(BF16)
        hidden = jnp.maximum(mm(wide, chosen), 0.0).astype(BF16)
        center, scale = normalised(hidden, second)
        edge_ref[k] = (center * scale).astype(BF16)


def updated_latent(
    round_index,
    slots,
    latent_ref,
    ghost_refs,
    edge_ref,
    column_ref,
    ew1_ref,
    ew2_ref,
    nw1_ref,
    nw2_ref,
    eg_ref,
    ng_ref,
):
    latent = latent_ref[...]
    particles, width = latent.shape
    total = particles + sum(ref.shape[0] for ref in ghost_refs)
    padded = -(-total // 256) * 256
    filler = jnp.zeros((padded - total, width), BF16)
    extended = jnp.concatenate([latent] + [ref[...] for ref in ghost_refs] + [filler], axis=0)
    receiver = mm(latent, ew1_ref[0, width : 2 * width])
    joint = jnp.concatenate([ew1_ref[0, :width], ew1_ref[0, 2 * width :]], axis=0)
    second = centred(ew2_ref[0])
    lanes = lax.broadcasted_iota(jnp.int32, (particles, padded), 1)
    counts = column_ref[:, slots : slots + 1]
    summed = jnp.zeros((particles, width), F32)
    for k in range(slots):
        picked = column_ref[:, k : k + 1] == lanes
        sender = mm(jnp.where(picked, 1.0, 0.0).astype(BF16), extended).astype(BF16)
        pre = mm(jnp.concatenate([edge_ref[k], sender], axis=1), joint) + receiver
        hidden = jnp.maximum(pre, 0.0).astype(BF16)
        center, scale = normalised(hidden, second)
        summed = summed + center * jnp.where(counts > k, scale, 0.0)
    aggregate = (summed * eg_ref[round_index : round_index + 1]).astype(BF16)
    node_pre = mm(jnp.concatenate([latent, aggregate], axis=1), nw1_ref[0])
    node_mid = jnp.maximum(node_pre, 0.0).astype(BF16)
    center, scale = normalised(node_mid, centred(nw2_ref[0]))
    update = center * scale * ng_ref[round_index : round_index + 1]
    return (latent.astype(F32) + update).astype(BF16)


def round_kernel(round_index, slots, latent_ref, g0, g1, g2, *refs):
    (edge, column, ew1, ew2, nw1, nw2, eg, ng, rows_ref, out_ref, low, mid, high) = refs
    latent = updated_latent(
        round_index, slots, latent_ref, (g0, g1, g2), edge, column, ew1, ew2, nw1, nw2, eg, ng
    )
    out_ref[...] = latent
    send_rows_of(latent, rows_ref, (low, mid, high))


def last_kernel(round_index, slots, latent_ref, g0, g1, g2, *refs):
    (edge, column, ew1, ew2, nw1, nw2, eg, ng) = refs[:8]
    (kin_ref, leave_ref, dw1_ref, dw2_ref, stayed_ref, low, mid, high) = refs[8:]
    latent = updated_latent(
        round_index, slots, latent_ref, (g0, g1, g2), edge, column, ew1, ew2, nw1, nw2, eg, ng
    )
    decoded = jnp.maximum(mm(latent, dw1_ref[...]), 0.0)
    decoded = decoded.astype(BF16).astype(F32)
    acceleration = lax.dot_general(
        dw2_ref[...],
        decoded,
        (((1,), (1,)), ((), ())),
        precision=lax.Precision.HIGHEST,
        preferred_element_type=F32,
    )
    state_rows, particles = kin_ref.shape
    velocity = kin_ref[state_rows - 3 :, :] + acceleration
    state = jnp.concatenate([kin_ref[:3, :] + velocity, kin_ref[6:, :], velocity], axis=0)
    direction = leave_ref[0:1, :]
    staying = direction == 13
    stayed_ref[...] = jnp.where(staying, state, 0.0)
    code = jnp.where(staying, -1, direction * MIG + leave_ref[1:2, :])
    picker = jnp.where(
        code == lax.broadcasted_iota(jnp.int32, (27 * MIG, particles), 0), 1.0, 0.0
    )
    outgoing = lax.dot_general(
        picker,
        state,
        (((1,), (1,)), ((), ())),
        precision=lax.Precision.HIGHEST,
        preferred_element_type=F32,
    )
    step = 9 * MIG
    for index, out in enumerate((low, mid, high)):
        out[...] = outgoing[index * step : (index + 1) * step]


def whole(shape):
    return pl.BlockSpec(shape, lambda i: (0,) * len(shape))


def call(body, args, specs, outs, name, flops=0, moved=0):
    return pl.pallas_call(
        body,
        grid=(1,),
        in_specs=[spec if spec is not None else whole(a.shape) for a, spec in zip(args, specs)],
        out_specs=[whole(s.shape) for s in outs],
        out_shape=outs,
        compiler_params=pltpu.CompilerParams(vmem_limit_bytes=VMEM_LIMIT),
        cost_estimate=pl.CostEstimate(flops=flops, bytes_accessed=moved, transcendentals=0),
        name=name,
    )(*args)


def shape(dims, dtype):
    return jax.ShapeDtypeStruct(dims, dtype)


def exchanged(low, mid, high, rows):
    tail = low.shape[-1]
    parts = [shifted(high, "gx", 1), mid, shifted(low, "gx", -1)]
    parts = [part.reshape(3, 3 * rows, tail) for part in parts]
    low, mid, high = (
        jnp.concatenate([part[y] for part in parts], axis=0) for y in range(3)
    )
    parts = [shifted(high, "gy", 1), mid, shifted(low, "gy", -1)]
    parts = [part.reshape(3, 3, rows, tail) for part in parts]
    low, mid, high = (
        jnp.stack([part[:, z] for part in parts], axis=1).reshape(9 * rows, tail)
        for z in range(3)
    )
    return [shifted(high, "gz", 1), mid, shifted(low, "gz", -1)]


def on_device(
    kinematics,
    pair_offsets,
    pair_index,
    neighbour_count,
    send_rows,
    migrate_dir,
    migrate_slot,
    enc_node_w1,
    enc_node_w2,
    enc_edge_w1,
    enc_edge_w2,
    edge_w1,
    edge_w2,
    node_w1,
    node_w2,
    edge_gain,
    node_gain,
    dec_w1,
    dec_w2,
):
    width = enc_node_w2.shape[1]
    slots, particles = pair_index.shape
    ghost_rows = send_rows.shape[1]
    rounds = edge_w1.shape[0]
    state_rows = kinematics.shape[0]
    rows = send_rows.reshape(-1, 1)
    part = shape((9 * ghost_rows, width), BF16)
    latent, low, mid, high = call(
        node_kernel,
        (kinematics, enc_node_w1, enc_node_w2, rows),
        (None,) * 4,
        [shape((particles, width), BF16), part, part, part],
        "node_encoder",
    )
    edges, columns = call(
        edge_kernel,
        (
            pair_offsets,
            pair_index,
            neighbour_count.reshape(1, particles),
            enc_edge_w1,
            enc_edge_w2,
        ),
        (None,) * 5,
        [shape((slots, particles, width), BF16), shape((particles, 128), jnp.int32)],
        "edge_encoder",
        flops=2 * slots * particles * 256 * 384,
        moved=4 * slots * particles * width,
    )
    leaving = jnp.stack([migrate_dir, migrate_slot], axis=0)
    for r in range(rounds):
        ghosts = exchanged(low, mid, high, ghost_rows)

        def of_round(array):
            return pl.BlockSpec((1,) + array.shape[1:], lambda i: (r, 0, 0))

        args = [latent, *ghosts, edges, columns, edge_w1, edge_w2, node_w1, node_w2]
        specs = [None] * 6 + [of_round(a) for a in args[6:]]
        args += [edge_gain, node_gain]
        specs += [None, None]
        if r < rounds - 1:
            latent, low, mid, high = call(
                functools.partial(round_kernel, r, slots),
                args + [rows],
                specs + [None],
                [shape((particles, width), BF16), part, part, part],
                "message_round",
            )
        else:
            out = shape((9 * MIG, state_rows), F32)
            stayed, low, mid, high = call(
                functools.partial(last_kernel, r, slots),
                args + [kinematics, leaving, dec_w1, dec_w2],
                specs + [None] * 4,
                [shape((state_rows, particles), F32), out, out, out],
                "last_round",
            )
    landed = exchanged(low, mid, high, MIG)
    landed = jnp.stack([g.reshape(9, MIG, state_rows) for g in landed], axis=1)
    arrived = landed.reshape(27 * MIG, state_rows).T
    return (stayed, arrived)


def solution(mesh):
    axes = ("gx", "gy", "gz")
    return jax.shard_map(
        on_device,
        mesh=mesh,
        in_specs=(
            P(None, axes),
            P(None, None, axes),
            P(None, axes),
            P(axes),
            P(None, axes),
            P(axes),
            P(axes),
        )
        + (P(),) * 12,
        out_specs=(P(None, axes), P(None, axes)),
        check_vma=False,
    )
```

time: 231 us -> 139 us (0.60)
  the two profiles are of different devices: /device:TPU:1 before, /device:TPU:35 now
where the time goes in v1:
time: 139 us; the launch traced here: 138 us
  starting transfers between devices  82.3 us (59%)
  waiting for transfers between devices  27.9 us (20%)
  Pallas kernels  21.4 us (15%)
  local copies, waits for them, and re-layouts  4.5 us (3%)
  between operations  1.45 us (1%)
    ppermute x24, starting transfers between devices, shifted(): lax.ppermute(value, axis, [(source, source + steps) for source in range(f...  82.3 us
    ppermute x24, waiting for transfers between devices, shifted(): lax.ppermute(value, axis, [(source, source + steps) for source in range(f...  27.9 us
    pallas_call x5, Pallas kernels, call(): pl.pallas_call(body, grid=(1,), in_specs=[spec if spec is not None else w...  21.4 us
    unnamed x38, local copies, waits for them, and re-layouts  4.13 us
  transfers between devices with their start and end apart: 24, of which 11 were waited for; matrix products, arithmetic and copies ran while one was open for 0% of the time, Pallas kernels for 1%

profile of v1, /device:TPU:35, one launch (start us, length us, event | category | flops | bytes accessed | tf_op | source)
XLA Modules:
  0.0 137.7 jit_solution(290353507751606808)
XLA Ops:
  5.6 4.2 %collective-permute-start.1 = (bf16[144,128]{1,0:T(8,128)(2,1)S(1)}, bf16[144,128]{1,0:T(8,128)(2,1)S(1)}, u32[]{:S(2)}, u32[]{:S(2)}) collective-permute-start(bf16[144,128]{1,0:T(8,128)(2,1)S(1)} %get-tuple-element.23), channel_id=1, source_target_pairs={{64,0},{128,64},{192,128},{256,192},{320,256},{384,320},{448,384},... | collective-permute-start | bytes 110600 | tf_op jit(solution)/shard_map/ppermute | solution.py:20
  12.8 4.1 %collective-permute-start.2 = (bf16[144,128]{1,0:T(8,128)(2,1)S(1)}, bf16[144,128]{1,0:T(8,128)(2,1)S(1)}, u32[]{:S(2)}, u32[]{:S(2)}) collective-permute-start(bf16[144,128]{1,0:T(8,128)(2,1)S(1)} %pad_maximum_fusion.1), channel_id=1, source_target_pairs={{0,8},{8,16},{16,24},{24,32},{32,40},{40,48},{48,56},{1,9},{9,17},... | collective-permute-start | bytes 110600 | tf_op jit(solution)/shard_map/ppermute | solution.py:20
  18.5 4.0 %collective-permute-done.3 = bf16[144,128]{1,0:T(8,128)(2,1)S(1)} collective-permute-done((bf16[144,128]{1,0:T(8,128)(2,1)S(1)}, bf16[144,128]{1,0:T(8,128)(2,1)S(1)}, u32[]{:S(2)}, u32[]{:S(2)}) %collective-permute-start.3) | collective-permute-done | bytes 36896 | tf_op jit(solution)/shard_map/ppermute | solution.py:20
  22.5 4.3 %collective-permute-start.5 = (bf16[144,128]{1,0:T(8,128)(2,1)S(1)}, bf16[144,128]{1,0:T(8,128)(2,1)S(1)}, u32[]{:S(2)}, u32[]{:S(2)}) collective-permute-start(bf16[144,128]{1,0:T(8,128)(2,1)S(1)} %bitcast.35), channel_id=1, source_target_pairs={{1,0},{2,1},{3,2},{4,3},{5,4},{6,5},{7,6},{9,8},{10,9},{11,10},{12... | collective-permute-start | bytes 110600 | tf_op jit(solution)/shard_map/ppermute | solution.py:20
  26.8 3.0 %collective-permute-start.4 = (bf16[144,128]{1,0:T(8,128)(2,1)S(1)}, bf16[144,128]{1,0:T(8,128)(2,1)S(1)}, u32[]{:S(2)}, u32[]{:S(2)}) collective-permute-start(bf16[144,128]{1,0:T(8,128)(2,1)S(1)} %bitcast.38), channel_id=1, source_target_pairs={{0,1},{1,2},{2,3},{3,4},{4,5},{5,6},{6,7},{8,9},{9,10},{10,11},{11... | collective-permute-start | bytes 110600 | tf_op jit(solution)/shard_map/ppermute | solution.py:20
  31.6 6.0 %message_round.2 = (bf16[256,128]{1,0:T(8,128)(2,1)S(1)}, bf16[144,128]{1,0:T(8,128)(2,1)S(1)}, bf16[144,128]{1,0:T(8,128)(2,1)S(1)}, bf16[144,128]{1,0:T(8,128)(2,1)S(1)}) custom-call(bf16[256,128]{1,0:T(8,128)(2,1)S(1)} %get-tuple-element.20.latent_ref, bf16[144,128]{1,0:T(8,128)(2,1)S(1)} %collective-permute-done.4.g0, bf16[144,128]{1,0:T(8,128)(2,1)S(1)} %bitcast.24, ...), custom_call_target="tpu_custom_call" | custom-call | tf_op jit(solution)/shard_map/message_round/pallas_call | solution.py:205
  39.6 4.6 %collective-permute-start.7 = (bf16[144,128]{1,0:T(8,128)(2,1)S(1)}, bf16[144,128]{1,0:T(8,128)(2,1)S(1)}, u32[]{:S(2)}, u32[]{:S(2)}) collective-permute-start(bf16[144,128]{1,0:T(8,128)(2,1)S(1)} %get-tuple-element.29), channel_id=1, source_target_pairs={{64,0},{128,64},{192,128},{256,192},{320,256},{384,320},{448,384},... | collective-permute-start | bytes 110600 | tf_op jit(solution)/shard_map/ppermute | solution.py:20
  45.2 4.0 %collective-permute-start.8 = (bf16[144,128]{1,0:T(8,128)(2,1)S(1)}, bf16[144,128]{1,0:T(8,128)(2,1)S(1)}, u32[]{:S(2)}, u32[]{:S(2)}) collective-permute-start(bf16[144,128]{1,0:T(8,128)(2,1)S(1)} %pad_maximum_fusion.7), channel_id=1, source_target_pairs={{0,8},{8,16},{16,24},{24,32},{32,40},{40,48},{48,56},{1,9},{9,17},... | collective-permute-start | bytes 110600 | tf_op jit(solution)/shard_map/ppermute | solution.py:20
  50.6 5.2 %collective-permute-done.9 = bf16[144,128]{1,0:T(8,128)(2,1)S(1)} collective-permute-done((bf16[144,128]{1,0:T(8,128)(2,1)S(1)}, bf16[144,128]{1,0:T(8,128)(2,1)S(1)}, u32[]{:S(2)}, u32[]{:S(2)}) %collective-permute-start.9) | collective-permute-done | bytes 36896 | tf_op jit(solution)/shard_map/ppermute | solution.py:20
  55.8 5.4 %collective-permute-start.11 = (bf16[144,128]{1,0:T(8,128)(2,1)S(1)}, bf16[144,128]{1,0:T(8,128)(2,1)S(1)}, u32[]{:S(2)}, u32[]{:S(2)}) collective-permute-start(bf16[144,128]{1,0:T(8,128)(2,1)S(1)} %bitcast.36), channel_id=1, source_target_pairs={{1,0},{2,1},{3,2},{4,3},{5,4},{6,5},{7,6},{9,8},{10,9},{11,10},{12... | collective-permute-start | bytes 110600 | tf_op jit(solution)/shard_map/ppermute | solution.py:20
  61.3 3.2 %collective-permute-start.10 = (bf16[144,128]{1,0:T(8,128)(2,1)S(1)}, bf16[144,128]{1,0:T(8,128)(2,1)S(1)}, u32[]{:S(2)}, u32[]{:S(2)}) collective-permute-start(bf16[144,128]{1,0:T(8,128)(2,1)S(1)} %bitcast.39), channel_id=1, source_target_pairs={{0,1},{1,2},{2,3},{3,4},{4,5},{5,6},{6,7},{8,9},{9,10},{10,11},{11... | collective-permute-start | bytes 110600 | tf_op jit(solution)/shard_map/ppermute | solution.py:20
  65.3 6.0 %message_round.3 = (bf16[256,128]{1,0:T(8,128)(2,1)S(1)}, bf16[144,128]{1,0:T(8,128)(2,1)S(1)}, bf16[144,128]{1,0:T(8,128)(2,1)S(1)}, bf16[144,128]{1,0:T(8,128)(2,1)S(1)}) custom-call(bf16[256,128]{1,0:T(8,128)(2,1)S(1)} %get-tuple-element.26.latent_ref, bf16[144,128]{1,0:T(8,128)(2,1)S(1)} %collective-permute-done.10.g0, bf16[144,128]{1,0:T(8,128)(2,1)S(1)} %bitcast.25, ...), custom_call_target="tpu_custom_call" | custom-call | tf_op jit(solution)/shard_map/message_round/pallas_call | solution.py:205
  73.3 5.2 %collective-permute-start.13 = (bf16[144,128]{1,0:T(8,128)(2,1)S(1)}, bf16[144,128]{1,0:T(8,128)(2,1)S(1)}, u32[]{:S(2)}, u32[]{:S(2)}) collective-permute-start(bf16[144,128]{1,0:T(8,128)(2,1)S(1)} %get-tuple-element.33), channel_id=1, source_target_pairs={{64,0},{128,64},{192,128},{256,192},{320,256},{384,320},{448,384},... | collective-permute-start | bytes 110600 | tf_op jit(solution)/shard_map/ppermute | solution.py:20
  79.5 4.8 %collective-permute-start.14 = (bf16[144,128]{1,0:T(8,128)(2,1)S(1)}, bf16[144,128]{1,0:T(8,128)(2,1)S(1)}, u32[]{:S(2)}, u32[]{:S(2)}) collective-permute-start(bf16[144,128]{1,0:T(8,128)(2,1)S(1)} %pad_maximum_fusion.13), channel_id=1, source_target_pairs={{0,8},{8,16},{16,24},{24,32},{32,40},{40,48},{48,56},{1,9},{9,17},... | collective-permute-start | bytes 110600 | tf_op jit(solution)/shard_map/ppermute | solution.py:20
  85.7 3.7 %collective-permute-done.15 = bf16[144,128]{1,0:T(8,128)(2,1)S(1)} collective-permute-done((bf16[144,128]{1,0:T(8,128)(2,1)S(1)}, bf16[144,128]{1,0:T(8,128)(2,1)S(1)}, u32[]{:S(2)}, u32[]{:S(2)}) %collective-permute-start.15) | collective-permute-done | bytes 36896 | tf_op jit(solution)/shard_map/ppermute | solution.py:20
  89.4 5.1 %collective-permute-start.17 = (bf16[144,128]{1,0:T(8,128)(2,1)S(1)}, bf16[144,128]{1,0:T(8,128)(2,1)S(1)}, u32[]{:S(2)}, u32[]{:S(2)}) collective-permute-start(bf16[144,128]{1,0:T(8,128)(2,1)S(1)} %bitcast.37), channel_id=1, source_target_pairs={{1,0},{2,1},{3,2},{4,3},{5,4},{6,5},{7,6},{9,8},{10,9},{11,10},{12... | collective-permute-start | bytes 110600 | tf_op jit(solution)/shard_map/ppermute | solution.py:20
  94.6 3.0 %collective-permute-start.16 = (bf16[144,128]{1,0:T(8,128)(2,1)S(1)}, bf16[144,128]{1,0:T(8,128)(2,1)S(1)}, u32[]{:S(2)}, u32[]{:S(2)}) collective-permute-start(bf16[144,128]{1,0:T(8,128)(2,1)S(1)} %bitcast.40), channel_id=1, source_target_pairs={{0,1},{1,2},{2,3},{3,4},{4,5},{5,6},{6,7},{8,9},{9,10},{10,11},{11... | collective-permute-start | bytes 110600 | tf_op jit(solution)/shard_map/ppermute | solution.py:20
  98.7 6.8 %last_round.1 = (f32[18,256]{1,0:T(8,128)}, f32[36,18]{1,0:T(8,128)S(1)}, f32[36,18]{1,0:T(8,128)S(1)}, f32[36,18]{1,0:T(8,128)S(1)}) custom-call(bf16[256,128]{1,0:T(8,128)(2,1)S(1)} %get-tuple-element.30.latent_ref, bf16[144,128]{1,0:T(8,128)(2,1)S(1)} %collective-permute-done.16.g0, bf16[144,128]{1,0:T(8,128)(2,1)S(1)} %bitcast.23, ...), custom_call_target="tpu_custom_call" | custom-call | tf_op jit(solution)/shard_map/last_round/pallas_call | solution.py:205
  105.5 5.2 %collective-permute-start.19 = (f32[36,18]{1,0:T(8,128)S(1)}, f32[36,18]{1,0:T(8,128)S(1)}, u32[]{:S(2)}, u32[]{:S(2)}) collective-permute-start(f32[36,18]{1,0:T(8,128)S(1)} %get-tuple-element.37), channel_id=1, source_target_pairs={{64,0},{128,64},{192,128},{256,192},{320,256},{384,320},{448,384},... | collective-permute-start | bytes 7784 | tf_op jit(solution)/shard_map/ppermute | solution.py:20
  112.6 3.8 %collective-permute-done.18 = f32[36,18]{1,0:T(8,128)S(1)} collective-permute-done((f32[36,18]{1,0:T(8,128)S(1)}, f32[36,18]{1,0:T(8,128)S(1)}, u32[]{:S(2)}, u32[]{:S(2)}) %collective-permute-start.18) | collective-permute-done | bytes 2624 | tf_op jit(solution)/shard_map/ppermute | solution.py:20
  116.4 3.6 %collective-permute-start.20 = (f32[36,18]{1,0:T(8,128)S(1)}, f32[36,18]{1,0:T(8,128)S(1)}, u32[]{:S(2)}, u32[]{:S(2)}) collective-permute-start(f32[36,18]{1,0:T(8,128)S(1)} %pad_maximum_fusion.19), channel_id=1, source_target_pairs={{0,8},{8,16},{16,24},{24,32},{32,40},{40,48},{48,56},{1,9},{9,17},... | collective-permute-start | bytes 7784 | tf_op jit(solution)/shard_map/ppermute | solution.py:20
  121.5 3.2 %collective-permute-done.21 = f32[36,18]{1,0:T(8,128)S(1)} collective-permute-done((f32[36,18]{1,0:T(8,128)S(1)}, f32[36,18]{1,0:T(8,128)S(1)}, u32[]{:S(2)}, u32[]{:S(2)}) %collective-permute-start.21) | collective-permute-done | bytes 2624 | tf_op jit(solution)/shard_map/ppermute | solution.py:20
  124.7 7.1 %collective-permute-start.22 = (f32[36,18]{1,0:T(8,128)S(1)}, f32[36,18]{1,0:T(8,128)S(1)}, u32[]{:S(2)}, u32[]{:S(2)}) collective-permute-start(f32[36,18]{1,0:T(8,128)S(1)} %reshape.189), channel_id=1, source_target_pairs={{0,1},{1,2},{2,3},{3,4},{4,5},{5,6},{6,7},{8,9},{9,10},{10,11},{11... | collective-permute-start | bytes 7784 | tf_op jit(solution)/shard_map/ppermute | solution.py:20
  133.8 3.1 %collective-permute-done.23 = f32[36,18]{1,0:T(8,128)S(1)} collective-permute-done((f32[36,18]{1,0:T(8,128)S(1)}, f32[36,18]{1,0:T(8,128)S(1)}, u32[]{:S(2)}, u32[]{:S(2)}) %collective-permute-start.23) | collective-permute-done | bytes 2624 | tf_op jit(solution)/shard_map/ppermute | solution.py:20
  (127 shorter events, 27.5 us)
Async XLA Ops:
  3.1 9.7 %collective-permute-start = (bf16[144,128]{1,0:T(8,128)(2,1)S(1)}, bf16[144,128]{1,0:T(8,128)(2,1)S(1)}, u32[]{:S(2)}, u32[]{:S(2)}) collective-permute-start(bf16[144,128]{1,0:T(8,128)(2,1)S(1)} %get-tuple-element.21), channel_id=1, source_target_pairs={{0,64},{64,128},{128,192},{192,256},{256,320},{320,384},{384,448},... | collective-permute-start | bytes 110600 | tf_op jit(solution)/shard_map/ppermute | solution.py:20
  5.6 7.2 %collective-permute-start.1 = (bf16[144,128]{1,0:T(8,128)(2,1)S(1)}, bf16[144,128]{1,0:T(8,128)(2,1)S(1)}, u32[]{:S(2)}, u32[]{:S(2)}) collective-permute-start(bf16[144,128]{1,0:T(8,128)(2,1)S(1)} %get-tuple-element.23), channel_id=1, source_target_pairs={{64,0},{128,64},{192,128},{256,192},{320,256},{384,320},{448,384},... | collective-permute-start | bytes 110600 | tf_op jit(solution)/shard_map/ppermute | solution.py:20
  12.8 5.6 %collective-permute-start.2 = (bf16[144,128]{1,0:T(8,128)(2,1)S(1)}, bf16[144,128]{1,0:T(8,128)(2,1)S(1)}, u32[]{:S(2)}, u32[]{:S(2)}) collective-permute-start(bf16[144,128]{1,0:T(8,128)(2,1)S(1)} %pad_maximum_fusion.1), channel_id=1, source_target_pairs={{0,8},{8,16},{16,24},{24,32},{32,40},{40,48},{48,56},{1,9},{9,17},... | collective-permute-start | bytes 110600 | tf_op jit(solution)/shard_map/ppermute | solution.py:20
  17.0 5.5 %collective-permute-start.3 = (bf16[144,128]{1,0:T(8,128)(2,1)S(1)}, bf16[144,128]{1,0:T(8,128)(2,1)S(1)}, u32[]{:S(2)}, u32[]{:S(2)}) collective-permute-start(bf16[144,128]{1,0:T(8,128)(2,1)S(1)} %pad_maximum_fusion.3), channel_id=1, source_target_pairs={{8,0},{16,8},{24,16},{32,24},{40,32},{48,40},{56,48},{9,1},{17,9},... | collective-permute-start | bytes 110600 | tf_op jit(solution)/shard_map/ppermute | solution.py:20
  22.5 7.4 %collective-permute-start.5 = (bf16[144,128]{1,0:T(8,128)(2,1)S(1)}, bf16[144,128]{1,0:T(8,128)(2,1)S(1)}, u32[]{:S(2)}, u32[]{:S(2)}) collective-permute-start(bf16[144,128]{1,0:T(8,128)(2,1)S(1)} %bitcast.35), channel_id=1, source_target_pairs={{1,0},{2,1},{3,2},{4,3},{5,4},{6,5},{7,6},{9,8},{10,9},{11,10},{12... | collective-permute-start | bytes 110600 | tf_op jit(solution)/shard_map/ppermute | solution.py:20
  26.8 4.1 %collective-permute-start.4 = (bf16[144,128]{1,0:T(8,128)(2,1)S(1)}, bf16[144,128]{1,0:T(8,128)(2,1)S(1)}, u32[]{:S(2)}, u32[]{:S(2)}) collective-permute-start(bf16[144,128]{1,0:T(8,128)(2,1)S(1)} %bitcast.38), channel_id=1, source_target_pairs={{0,1},{1,2},{2,3},{3,4},{4,5},{5,6},{6,7},{8,9},{9,10},{10,11},{11... | collective-permute-start | bytes 110600 | tf_op jit(solution)/shard_map/ppermute | solution.py:20
  37.7 6.5 %collective-permute-start.6 = (bf16[144,128]{1,0:T(8,128)(2,1)S(1)}, bf16[144,128]{1,0:T(8,128)(2,1)S(1)}, u32[]{:S(2)}, u32[]{:S(2)}) collective-permute-start(bf16[144,128]{1,0:T(8,128)(2,1)S(1)} %get-tuple-element.27), channel_id=1, source_target_pairs={{0,64},{64,128},{128,192},{192,256},{256,320},{320,384},{384,448},... | collective-permute-start | bytes 110600 | tf_op jit(solution)/shard_map/ppermute | solution.py:20
  39.6 5.6 %collective-permute-start.7 = (bf16[144,128]{1,0:T(8,128)(2,1)S(1)}, bf16[144,128]{1,0:T(8,128)(2,1)S(1)}, u32[]{:S(2)}, u32[]{:S(2)}) collective-permute-start(bf16[144,128]{1,0:T(8,128)(2,1)S(1)} %get-tuple-element.29), channel_id=1, source_target_pairs={{64,0},{128,64},{192,128},{256,192},{320,256},{384,320},{448,384},... | collective-permute-start | bytes 110600 | tf_op jit(solution)/shard_map/ppermute | solution.py:20
  45.2 5.3 %collective-permute-start.8 = (bf16[144,128]{1,0:T(8,128)(2,1)S(1)}, bf16[144,128]{1,0:T(8,128)(2,1)S(1)}, u32[]{:S(2)}, u32[]{:S(2)}) collective-permute-start(bf16[144,128]{1,0:T(8,128)(2,1)S(1)} %pad_maximum_fusion.7), channel_id=1, source_target_pairs={{0,8},{8,16},{16,24},{24,32},{32,40},{40,48},{48,56},{1,9},{9,17},... | collective-permute-start | bytes 110600 | tf_op jit(solution)/shard_map/ppermute | solution.py:20
  49.3 6.6 %collective-permute-start.9 = (bf16[144,128]{1,0:T(8,128)(2,1)S(1)}, bf16[144,128]{1,0:T(8,128)(2,1)S(1)}, u32[]{:S(2)}, u32[]{:S(2)}) collective-permute-start(bf16[144,128]{1,0:T(8,128)(2,1)S(1)} %pad_maximum_fusion.9), channel_id=1, source_target_pairs={{8,0},{16,8},{24,16},{32,24},{40,32},{48,40},{56,48},{9,1},{17,9},... | collective-permute-start | bytes 110600 | tf_op jit(solution)/shard_map/ppermute | solution.py:20
  55.8 8.7 %collective-permute-start.11 = (bf16[144,128]{1,0:T(8,128)(2,1)S(1)}, bf16[144,128]{1,0:T(8,128)(2,1)S(1)}, u32[]{:S(2)}, u32[]{:S(2)}) collective-permute-start(bf16[144,128]{1,0:T(8,128)(2,1)S(1)} %bitcast.36), channel_id=1, source_target_pairs={{1,0},{2,1},{3,2},{4,3},{5,4},{6,5},{7,6},{9,8},{10,9},{11,10},{12... | collective-permute-start | bytes 110600 | tf_op jit(solution)/shard_map/ppermute | solution.py:20
  61.3 4.1 %collective-permute-start.10 = (bf16[144,128]{1,0:T(8,128)(2,1)S(1)}, bf16[144,128]{1,0:T(8,128)(2,1)S(1)}, u32[]{:S(2)}, u32[]{:S(2)}) collective-permute-start(bf16[144,128]{1,0:T(8,128)(2,1)S(1)} %bitcast.39), channel_id=1, source_target_pairs={{0,1},{1,2},{2,3},{3,4},{4,5},{5,6},{6,7},{8,9},{9,10},{10,11},{11... | collective-permute-start | bytes 110600 | tf_op jit(solution)/shard_map/ppermute | solution.py:20
  71.4 7.1 %collective-permute-start.12 = (bf16[144,128]{1,0:T(8,128)(2,1)S(1)}, bf16[144,128]{1,0:T(8,128)(2,1)S(1)}, u32[]{:S(2)}, u32[]{:S(2)}) collective-permute-start(bf16[144,128]{1,0:T(8,128)(2,1)S(1)} %get-tuple-element.31), channel_id=1, source_target_pairs={{0,64},{64,128},{128,192},{192,256},{256,320},{320,384},{384,448},... | collective-permute-start | bytes 110600 | tf_op jit(solution)/shard_map/ppermute | solution.py:20
  73.3 6.2 %collective-permute-start.13 = (bf16[144,128]{1,0:T(8,128)(2,1)S(1)}, bf16[144,128]{1,0:T(8,128)(2,1)S(1)}, u32[]{:S(2)}, u32[]{:S(2)}) collective-permute-start(bf16[144,128]{1,0:T(8,128)(2,1)S(1)} %get-tuple-element.33), channel_id=1, source_target_pairs={{64,0},{128,64},{192,128},{256,192},{320,256},{384,320},{448,384},... | collective-permute-start | bytes 110600 | tf_op jit(solution)/shard_map/ppermute | solution.py:20
  79.5 6.2 %collective-permute-start.14 = (bf16[144,128]{1,0:T(8,128)(2,1)S(1)}, bf16[144,128]{1,0:T(8,128)(2,1)S(1)}, u32[]{:S(2)}, u32[]{:S(2)}) collective-permute-start(bf16[144,128]{1,0:T(8,128)(2,1)S(1)} %pad_maximum_fusion.13), channel_id=1, source_target_pairs={{0,8},{8,16},{16,24},{24,32},{32,40},{40,48},{48,56},{1,9},{9,17},... | collective-permute-start | bytes 110600 | tf_op jit(solution)/shard_map/ppermute | solution.py:20
  84.4 5.0 %collective-permute-start.15 = (bf16[144,128]{1,0:T(8,128)(2,1)S(1)}, bf16[144,128]{1,0:T(8,128)(2,1)S(1)}, u32[]{:S(2)}, u32[]{:S(2)}) collective-permute-start(bf16[144,128]{1,0:T(8,128)(2,1)S(1)} %pad_maximum_fusion.15), channel_id=1, source_target_pairs={{8,0},{16,8},{24,16},{32,24},{40,32},{48,40},{56,48},{9,1},{17,9},... | collective-permute-start | bytes 110600 | tf_op jit(solution)/shard_map/ppermute | solution.py:20
  89.4 8.2 %collective-permute-start.17 = (bf16[144,128]{1,0:T(8,128)(2,1)S(1)}, bf16[144,128]{1,0:T(8,128)(2,1)S(1)}, u32[]{:S(2)}, u32[]{:S(2)}) collective-permute-start(bf16[144,128]{1,0:T(8,128)(2,1)S(1)} %bitcast.37), channel_id=1, source_target_pairs={{1,0},{2,1},{3,2},{4,3},{5,4},{6,5},{7,6},{9,8},{10,9},{11,10},{12... | collective-permute-start | bytes 110600 | tf_op jit(solution)/shard_map/ppermute | solution.py:20
  94.6 4.1 %collective-permute-start.16 = (bf16[144,128]{1,0:T(8,128)(2,1)S(1)}, bf16[144,128]{1,0:T(8,128)(2,1)S(1)}, u32[]{:S(2)}, u32[]{:S(2)}) collective-permute-start(bf16[144,128]{1,0:T(8,128)(2,1)S(1)} %bitcast.40), channel_id=1, source_target_pairs={{0,1},{1,2},{2,3},{3,4},{4,5},{5,6},{6,7},{8,9},{9,10},{10,11},{11... | collective-permute-start | bytes 110600 | tf_op jit(solution)/shard_map/ppermute | solution.py:20
  105.5 7.1 %collective-permute-start.19 = (f32[36,18]{1,0:T(8,128)S(1)}, f32[36,18]{1,0:T(8,128)S(1)}, u32[]{:S(2)}, u32[]{:S(2)}) collective-permute-start(f32[36,18]{1,0:T(8,128)S(1)} %get-tuple-element.37), channel_id=1, source_target_pairs={{64,0},{128,64},{192,128},{256,192},{320,256},{384,320},{448,384},... | collective-permute-start | bytes 7784 | tf_op jit(solution)/shard_map/ppermute | solution.py:20
  110.7 5.7 %collective-permute-start.18 = (f32[36,18]{1,0:T(8,128)S(1)}, f32[36,18]{1,0:T(8,128)S(1)}, u32[]{:S(2)}, u32[]{:S(2)}) collective-permute-start(f32[36,18]{1,0:T(8,128)S(1)} %get-tuple-element.35), channel_id=1, source_target_pairs={{0,64},{64,128},{128,192},{192,256},{256,320},{320,384},{384,448},... | collective-permute-start | bytes 7784 | tf_op jit(solution)/shard_map/ppermute | solution.py:20
  116.4 5.0 %collective-permute-start.20 = (f32[36,18]{1,0:T(8,128)S(1)}, f32[36,18]{1,0:T(8,128)S(1)}, u32[]{:S(2)}, u32[]{:S(2)}) collective-permute-start(f32[36,18]{1,0:T(8,128)S(1)} %pad_maximum_fusion.19), channel_id=1, source_target_pairs={{0,8},{8,16},{16,24},{24,32},{32,40},{40,48},{48,56},{1,9},{9,17},... | collective-permute-start | bytes 7784 | tf_op jit(solution)/shard_map/ppermute | solution.py:20
  120.1 4.5 %collective-permute-start.21 = (f32[36,18]{1,0:T(8,128)S(1)}, f32[36,18]{1,0:T(8,128)S(1)}, u32[]{:S(2)}, u32[]{:S(2)}) collective-permute-start(f32[36,18]{1,0:T(8,128)S(1)} %pad_maximum_fusion.21), channel_id=1, source_target_pairs={{8,0},{16,8},{24,16},{32,24},{40,32},{48,40},{56,48},{9,1},{17,9},... | collective-permute-start | bytes 7784 | tf_op jit(solution)/shard_map/ppermute | solution.py:20
  124.7 9.1 %collective-permute-start.22 = (f32[36,18]{1,0:T(8,128)S(1)}, f32[36,18]{1,0:T(8,128)S(1)}, u32[]{:S(2)}, u32[]{:S(2)}) collective-permute-start(f32[36,18]{1,0:T(8,128)S(1)} %reshape.189), channel_id=1, source_target_pairs={{0,1},{1,2},{2,3},{3,4},{4,5},{5,6},{6,7},{8,9},{9,10},{10,11},{11... | collective-permute-start | bytes 7784 | tf_op jit(solution)/shard_map/ppermute | solution.py:20
  131.8 5.1 %collective-permute-start.23 = (f32[36,18]{1,0:T(8,128)S(1)}, f32[36,18]{1,0:T(8,128)S(1)}, u32[]{:S(2)}, u32[]{:S(2)}) collective-permute-start(f32[36,18]{1,0:T(8,128)S(1)} %reshape.190), channel_id=1, source_target_pairs={{1,0},{2,1},{3,2},{4,3},{5,4},{6,5},{7,6},{9,8},{10,9},{11,10},{12... | collective-permute-start | bytes 7784 | tf_op jit(solution)/shard_map/ppermute | solution.py:20
  (18 other events, 90.2 us)

commit v2 on v1

--- a/solution.py
+++ b/solution.py
@@ -8,6 +8,7 @@
 from jax.sharding import PartitionSpec as P
 
 MIG = 4
+BLOCK = 8
 EPS = 1e-05
 F32 = jnp.float32
 BF16 = jnp.bfloat16
@@ -45,12 +46,22 @@
 
 def send_rows_of(latent, rows_ref, outs):
     particles = latent.shape[0]
-    count = rows_ref.shape[0]
-    picked = rows_ref[...] == lax.broadcasted_iota(jnp.int32, (count, particles), 1)
-    chosen = mm(jnp.where(picked, 1.0, 0.0).astype(BF16), latent).astype(BF16)
-    step = count // 3
-    for index, out in enumerate(outs):
-        out[...] = chosen[index * step : (index + 1) * step]
+    depth = rows_ref.shape[0]
+    lanes = lax.broadcasted_iota(jnp.int32, (depth, particles), 1)
+    for z, out in enumerate(outs):
+        picked = [
+            jnp.where(rows_ref[:, d : d + 1] == lanes, 1.0, 0.0)
+            for d in [x * 9 + y * 3 + z for x in range(3) for y in range(3)]
+        ]
+        picked = jnp.concatenate(picked, axis=0).astype(BF16)
+        out[...] = mm(picked, latent).astype(BF16)
+
+
+def split_direction(direction):
+    dx = (direction * 57) >> 9
+    rest = direction - dx * 9
+    dy = (rest * 11) >> 5
+    return dx, dy, rest - dy * 3
 
 
 def node_kernel(kin_ref, w1_ref, w2_ref, rows_ref, latent_ref, low_ref, mid_ref, high_ref):
@@ -74,12 +85,8 @@
     index = index_ref[...]
     place = index - particles
     slot = place & 15
-    direction = place >> 4
-    dx = (direction * 57) >> 9
-    rest = direction - dx * 9
-    dy = (rest * 11) >> 5
-    dz = rest - dy * 3
-    moved = particles + (dz * 9 + dx * 3 + dy) * 16 + slot
+    dx, dy, dz = split_direction(place >> 4)
+    moved = particles + (dy * 9 + dz * 3 + dx) * 16 + slot
     index = jnp.where(index < particles, index, moved).astype(F32)
     count = count_ref[...].astype(F32)
     filler = jnp.zeros((128 - slots - count.shape[0], particles), F32)
@@ -110,62 +117,69 @@
         edge_ref[k] = (center * scale).astype(BF16)
 
 
-def updated_latent(
-    round_index,
-    slots,
-    latent_ref,
-    ghost_refs,
-    edge_ref,
-    column_ref,
-    ew1_ref,
-    ew2_ref,
-    nw1_ref,
-    nw2_ref,
-    eg_ref,
-    ng_ref,
-):
+def one_hot(column_ref, first, count, lanes):
+    picked = [
+        jnp.where(column_ref[:, k : k + 1] == lanes, 1.0, 0.0).astype(BF16)
+        for k in range(first, first + count)
+    ]
+    return jnp.concatenate(picked, axis=0)
+
+
+def local_kernel(latent_ref, edge_ref, column_ref, w1_ref, out_ref):
+    slots, particles, width = edge_ref.shape
     latent = latent_ref[...]
-    particles, width = latent.shape
-    total = particles + sum(ref.shape[0] for ref in ghost_refs)
+    receiver = mm(latent, w1_ref[0, width : 2 * width])
+    sender = jnp.concatenate(halves(mm(latent, w1_ref[0, 2 * width :])), axis=1)
+    first = w1_ref[0, :width]
+    lanes = lax.broadcasted_iota(jnp.int32, (particles, particles), 1)
+    for k in range(0, slots, BLOCK):
+        both = mm(one_hot(column_ref, k, BLOCK, lanes), sender)
+        pre = mm(edge_ref[k : k + BLOCK].reshape(BLOCK * particles, width), first)
+        pre = pre + both[:, :width] + both[:, width:]
+        for j in range(BLOCK):
+            out_ref[k + j] = pre[j * particles : (j + 1) * particles] + receiver
+
+
+def updated_latent(r, latent_ref, ghost_refs, part_ref, column_ref, refs):
+    ew1_ref, ew2_ref, nw1_ref, nw2_ref, eg_ref, ng_ref = refs
+    latent = latent_ref[...]
+    slots, particles, width = part_ref.shape
+    total = sum(ref.shape[0] for ref in ghost_refs)
     padded = -(-total // 256) * 256
     filler = jnp.zeros((padded - total, width), BF16)
-    extended = jnp.concatenate([latent] + [ref[...] for ref in ghost_refs] + [filler], axis=0)
-    receiver = mm(latent, ew1_ref[0, width : 2 * width])
-    joint = jnp.concatenate([ew1_ref[0, :width], ew1_ref[0, 2 * width :]], axis=0)
+    ghosts = jnp.concatenate([ref[...] for ref in ghost_refs] + [filler], axis=0)
+    sender = jnp.concatenate(halves(mm(ghosts, ew1_ref[0, 2 * width :])), axis=1)
     second = centred(ew2_ref[0])
-    lanes = lax.broadcasted_iota(jnp.int32, (particles, padded), 1)
+    lanes = lax.broadcasted_iota(jnp.int32, (particles, padded), 1) + particles
     counts = column_ref[:, slots : slots + 1]
     summed = jnp.zeros((particles, width), F32)
-    for k in range(slots):
-        picked = column_ref[:, k : k + 1] == lanes
-        sender = mm(jnp.where(picked, 1.0, 0.0).astype(BF16), extended).astype(BF16)
-        pre = mm(jnp.concatenate([edge_ref[k], sender], axis=1), joint) + receiver
+    for k in range(0, slots, BLOCK):
+        both = mm(one_hot(column_ref, k, BLOCK, lanes), sender)
+        pre = part_ref[k : k + BLOCK].reshape(BLOCK * particles, width)
+        pre = pre + both[:, :width] + both[:, width:]
         hidden = jnp.maximum(pre, 0.0).astype(BF16)
         center, scale = normalised(hidden, second)
-        summed = summed + center * jnp.where(counts > k, scale, 0.0)
-    aggregate = (summed * eg_ref[round_index : round_index + 1]).astype(BF16)
+        for j in range(BLOCK):
+            rows = slice(j * particles, (j + 1) * particles)
+            summed = summed + center[rows] * jnp.where(counts > k + j, scale[rows], 0.0)
+    aggregate = (summed * eg_ref[r : r + 1]).astype(BF16)
     node_pre = mm(jnp.concatenate([latent, aggregate], axis=1), nw1_ref[0])
     node_mid = jnp.maximum(node_pre, 0.0).astype(BF16)
     center, scale = normalised(node_mid, centred(nw2_ref[0]))
-    update = center * scale * ng_ref[round_index : round_index + 1]
+    update = center * scale * ng_ref[r : r + 1]
     return (latent.astype(F32) + update).astype(BF16)
 
 
-def round_kernel(round_index, slots, latent_ref, g0, g1, g2, *refs):
-    (edge, column, ew1, ew2, nw1, nw2, eg, ng, rows_ref, out_ref, low, mid, high) = refs
-    latent = updated_latent(
-        round_index, slots, latent_ref, (g0, g1, g2), edge, column, ew1, ew2, nw1, nw2, eg, ng
-    )
+def round_kernel(r, latent_ref, g0, g1, g2, part_ref, column_ref, *refs):
+    rows_ref, out_ref, low, mid, high = refs[6:]
+    latent = updated_latent(r, latent_ref, (g0, g1, g2), part_ref, column_ref, refs[:6])
     out_ref[...] = latent
     send_rows_of(latent, rows_ref, (low, mid, high))
 
 
-def last_kernel(round_index, slots, latent_ref, g0, g1, g2, *refs):
-    (edge, column, ew1, ew2, nw1, nw2, eg, ng) = refs[:8]
-    (kin_ref, leave_ref, dw1_ref, dw2_ref, stayed_ref, low, mid, high) = refs[8:]
-    latent = updated_latent(
-        round_index, slots, latent_ref, (g0, g1, g2), edge, column, ew1, ew2, nw1, nw2, eg, ng
-    )
+def last_kernel(r, latent_ref, g0, g1, g2, part_ref, column_ref, *refs):
+    kin_ref, leave_ref, dw1_ref, dw2_ref, stayed_ref, low, mid, high = refs[6:]
+    latent = updated_latent(r, latent_ref, (g0, g1, g2), part_ref, column_ref, refs[:6])
     decoded = jnp.maximum(mm(latent, dw1_ref[...]), 0.0)
     decoded = decoded.astype(BF16).astype(F32)
     acceleration = lax.dot_general(
@@ -181,7 +195,9 @@
     direction = leave_ref[0:1, :]
     staying = direction == 13
     stayed_ref[...] = jnp.where(staying, state, 0.0)
-    code = jnp.where(staying, -1, direction * MIG + leave_ref[1:2, :])
+    dx, dy, dz = split_direction(direction)
+    code = (dz * 9 + dx * 3 + dy) * MIG + leave_ref[1:2, :]
+    code = jnp.where(staying, -1, code)
     picker = jnp.where(
         code == lax.broadcasted_iota(jnp.int32, (27 * MIG, particles), 0), 1.0, 0.0
     )
@@ -218,20 +234,37 @@
     return jax.ShapeDtypeStruct(dims, dtype)
 
 
+def swapped(value, axis, first):
+    pairs = []
+    for low in range(first, lax.axis_size(axis) - 1, 2):
+        pairs += [(low, low + 1), (low + 1, low)]
+    return lax.ppermute(value, axis, pairs)
+
+
+def moved_in_pairs(low, mid, high, axis):
+    even = lax.axis_index(axis) % 2 == 0
+    odd_pairs = swapped(jnp.where(even, low, high), axis, 1)
+    even_pairs = swapped(jnp.where(even, high, low), axis, 0)
+    from_below = jnp.where(even, odd_pairs, even_pairs)
+    from_above = jnp.where(even, even_pairs, odd_pairs)
+    return [from_below, mid, from_above]
+
+
+def moved(low, mid, high, axis):
+    return [shifted(high, axis, 1), mid, shifted(low, axis, -1)]
+
+
 def exchanged(low, mid, high, rows):
     tail = low.shape[-1]
-    parts = [shifted(high, "gx", 1), mid, shifted(low, "gx", -1)]
+    parts = moved_in_pairs(low, mid, high, "gz")
     parts = [part.reshape(3, 3 * rows, tail) for part in parts]
-    low, mid, high = (
-        jnp.concatenate([part[y] for part in parts], axis=0) for y in range(3)
-    )
-    parts = [shifted(high, "gy", 1), mid, shifted(low, "gy", -1)]
+    parts = moved(*(jnp.concatenate([part[x] for part in parts], axis=0) for x in range(3)), "gx")
     parts = [part.reshape(3, 3, rows, tail) for part in parts]
     low, mid, high = (
-        jnp.stack([part[:, z] for part in parts], axis=1).reshape(9 * rows, tail)
-        for z in range(3)
-    )
-    return [shifted(high, "gz", 1), mid, shifted(low, "gz", -1)]
+        jnp.stack([part[:, y] for part in parts], axis=1).reshape(9 * rows, tail)
+        for y in range(3)
+    )
+    return moved(low, mid, high, "gy")
 
 
 def on_device(
@@ -260,7 +293,7 @@
     ghost_rows = send_rows.shape[1]
     rounds = edge_w1.shape[0]
     state_rows = kinematics.shape[0]
-    rows = send_rows.reshape(-1, 1)
+    rows = send_rows.T
     part = shape((9 * ghost_rows, width), BF16)
     latent, low, mid, high = call(
         node_kernel,
@@ -291,13 +324,21 @@
         def of_round(array):
             return pl.BlockSpec((1,) + array.shape[1:], lambda i: (r, 0, 0))
 
-        args = [latent, *ghosts, edges, columns, edge_w1, edge_w2, node_w1, node_w2]
-        specs = [None] * 6 + [of_round(a) for a in args[6:]]
-        args += [edge_gain, node_gain]
-        specs += [None, None]
+        (part_sum,) = call(
+            local_kernel,
+            (latent, edges, columns, edge_w1),
+            (None, None, None, of_round(edge_w1)),
+            [shape((slots, particles, width), F32)],
+            "local_pairs",
+            flops=2 * slots * particles * 256 * 512,
+            moved=8 * slots * particles * width,
+        )
+        weights = [edge_w1, edge_w2, node_w1, node_w2]
+        args = [latent, *ghosts, part_sum, columns, *weights, edge_gain, node_gain]
+        specs = [None] * 6 + [of_round(w) for w in weights] + [None, None]
         if r < rounds - 1:
             latent, low, mid, high = call(
-                functools.partial(round_kernel, r, slots),
+                functools.partial(round_kernel, r),
                 args + [rows],
                 specs + [None],
                 [shape((particles, width), BF16), part, part, part],
@@ -306,16 +347,15 @@
         else:
             out = shape((9 * MIG, state_rows), F32)
             stayed, low, mid, high = call(
-                functools.partial(last_kernel, r, slots),
+                functools.partial(last_kernel, r),
                 args + [kinematics, leaving, dec_w1, dec_w2],
                 specs + [None] * 4,
                 [shape((state_rows, particles), F32), out, out, out],
                 "last_round",
             )
-    landed = exchanged(low, mid, high, MIG)
-    landed = jnp.stack([g.reshape(9, MIG, state_rows) for g in landed], axis=1)
-    arrived = landed.reshape(27 * MIG, state_rows).T
-    return (stayed, arrived)
+    landed = jnp.stack(exchanged(low, mid, high, MIG), axis=0)
+    landed = landed.reshape(3, 3, 3, MIG, state_rows).transpose(4, 2, 0, 1, 3)
+    return (stayed, landed.reshape(state_rows, 27 * MIG))
 
 
 def solution(mesh):

time: 139 us -> 141 us (1.014)
  the two profiles are of different devices: /device:TPU:35 before, /device:TPU:192 now
where the time goes in v2:
time: 141 us; the launch traced here: 140 us
  starting transfers between devices  70.9 us (50%)
  Pallas kernels  30 us (21%)
  waiting for transfers between devices  28.7 us (20%)
  local copies, waits for them, and re-layouts  7.52 us (5%)
  between operations  1.49 us (1%)
    ppermute x16, starting transfers between devices, shifted(): lax.ppermute(value, axis, [(source, source + steps) for source in range(f...  50.9 us
    pallas_call x8, Pallas kernels, call(): pl.pallas_call(body, grid=(1,), in_specs=[spec if spec is not None else w...  30 us
    ppermute x16, waiting for transfers between devices, shifted(): lax.ppermute(value, axis, [(source, source + steps) for source in range(f...  27.9 us
    ppermute x8, starting transfers between devices, swapped(): return lax.ppermute(value, axis, pairs)  20.1 us
    unnamed x39, local copies, waits for them, and re-layouts  7.3 us
  transfers between devices with their start and end apart: 24, of which 13 were waited for; matrix products, arithmetic and copies ran while one was open for 1% of the time, Pallas kernels for 4%

profile of v2, /device:TPU:192, one launch (start us, length us, event | category | flops | bytes accessed | tf_op | source)
XLA Modules:
  0.0 139.6 jit_solution(3685400004284107646)
XLA Ops:
  5.2 4.8 %collective-permute-start.1 = (bf16[144,128]{1,0:T(8,128)(2,1)S(1)}, bf16[144,128]{1,0:T(8,128)(2,1)S(1)}, u32[]{:S(2)}, u32[]{:S(2)}) collective-permute-start(bf16[144,128]{1,0:T(8,128)(2,1)S(1)} %get-tuple-element.51), channel_id=1, source_target_pairs={{0,1},{1,0},{2,3},{3,2},{4,5},{5,4},{6,7},{7,6},{8,9},{9,8},{10,11... | collective-permute-start | bytes 110600 | tf_op jit(solution)/shard_map/ppermute | solution.py:241
  17.2 3.5 %collective-permute-start.2 = (bf16[144,128]{1,0:T(8,128)(2,1)S(1)}, bf16[144,128]{1,0:T(8,128)(2,1)S(1)}, u32[]{:S(2)}, u32[]{:S(2)}) collective-permute-start(bf16[144,128]{1,0:T(8,128)(2,1)S(1)} %pad_maximum_fusion), channel_id=1, source_target_pairs={{0,64},{64,128},{128,192},{192,256},{256,320},{320,384},{384,448},... | collective-permute-start | bytes 110600 | tf_op jit(solution)/shard_map/ppermute | solution.py:21
  22.3 4.3 %collective-permute-done.3 = bf16[144,128]{1,0:T(8,128)(2,1)S(1)} collective-permute-done((bf16[144,128]{1,0:T(8,128)(2,1)S(1)}, bf16[144,128]{1,0:T(8,128)(2,1)S(1)}, u32[]{:S(2)}, u32[]{:S(2)}) %collective-permute-start.3) | collective-permute-done | bytes 36896 | tf_op jit(solution)/shard_map/ppermute | solution.py:21
  26.6 1.9 %collective-permute-start.5 = (bf16[144,128]{1,0:T(8,128)(2,1)S(1)}, bf16[144,128]{1,0:T(8,128)(2,1)S(1)}, u32[]{:S(2)}, u32[]{:S(2)}) collective-permute-start(bf16[144,128]{1,0:T(8,128)(2,1)S(1)} %bitcast.41), channel_id=1, source_target_pairs={{8,0},{16,8},{24,16},{32,24},{40,32},{48,40},{56,48},{9,1},{17,9},... | collective-permute-start | bytes 110600 | tf_op jit(solution)/shard_map/ppermute | solution.py:21
  28.6 5.5 %collective-permute-start.4 = (bf16[144,128]{1,0:T(8,128)(2,1)S(1)}, bf16[144,128]{1,0:T(8,128)(2,1)S(1)}, u32[]{:S(2)}, u32[]{:S(2)}) collective-permute-start(bf16[144,128]{1,0:T(8,128)(2,1)S(1)} %bitcast.44), channel_id=1, source_target_pairs={{0,8},{8,16},{16,24},{24,32},{32,40},{40,48},{48,56},{1,9},{9,17},... | collective-permute-start | bytes 110600 | tf_op jit(solution)/shard_map/ppermute | solution.py:21
  35.7 7.8 %message_round.2 = (bf16[256,128]{1,0:T(8,128)(2,1)S(1)}, bf16[144,128]{1,0:T(8,128)(2,1)S(1)}, bf16[144,128]{1,0:T(8,128)(2,1)S(1)}, bf16[144,128]{1,0:T(8,128)(2,1)S(1)}) custom-call(bf16[256,128]{1,0:T(8,128)(2,1)S(1)} %get-tuple-element.20.latent_ref, bf16[144,128]{1,0:T(8,128)(2,1)S(1)} %collective-permute-done.4.g0, bf16[144,128]{1,0:T(8,128)(2,1)S(1)} %bitcast.29, ...), custom_call_target="tpu_custom_call" | custom-call | tf_op jit(solution)/shard_map/message_round/pallas_call | solution.py:221
  44.2 4.8 %collective-permute-start.7 = (bf16[144,128]{1,0:T(8,128)(2,1)S(1)}, bf16[144,128]{1,0:T(8,128)(2,1)S(1)}, u32[]{:S(2)}, u32[]{:S(2)}) collective-permute-start(bf16[144,128]{1,0:T(8,128)(2,1)S(1)} %get-tuple-element.47), channel_id=1, source_target_pairs={{0,1},{1,0},{2,3},{3,2},{4,5},{5,4},{6,7},{7,6},{8,9},{9,8},{10,11... | collective-permute-start | bytes 110600 | tf_op jit(solution)/shard_map/ppermute | solution.py:241
  50.2 3.5 %collective-permute-start.8 = (bf16[144,128]{1,0:T(8,128)(2,1)S(1)}, bf16[144,128]{1,0:T(8,128)(2,1)S(1)}, u32[]{:S(2)}, u32[]{:S(2)}) collective-permute-start(bf16[144,128]{1,0:T(8,128)(2,1)S(1)} %pad_maximum_fusion.6), channel_id=1, source_target_pairs={{0,64},{64,128},{128,192},{192,256},{256,320},{320,384},{384,448},... | collective-permute-start | bytes 110600 | tf_op jit(solution)/shard_map/ppermute | solution.py:21
  55.3 4.6 %collective-permute-done.9 = bf16[144,128]{1,0:T(8,128)(2,1)S(1)} collective-permute-done((bf16[144,128]{1,0:T(8,128)(2,1)S(1)}, bf16[144,128]{1,0:T(8,128)(2,1)S(1)}, u32[]{:S(2)}, u32[]{:S(2)}) %collective-permute-start.9) | collective-permute-done | bytes 36896 | tf_op jit(solution)/shard_map/ppermute | solution.py:21
  59.9 1.9 %collective-permute-start.11 = (bf16[144,128]{1,0:T(8,128)(2,1)S(1)}, bf16[144,128]{1,0:T(8,128)(2,1)S(1)}, u32[]{:S(2)}, u32[]{:S(2)}) collective-permute-start(bf16[144,128]{1,0:T(8,128)(2,1)S(1)} %bitcast.42), channel_id=1, source_target_pairs={{8,0},{16,8},{24,16},{32,24},{40,32},{48,40},{56,48},{9,1},{17,9},... | collective-permute-start | bytes 110600 | tf_op jit(solution)/shard_map/ppermute | solution.py:21
  61.9 5.6 %collective-permute-start.10 = (bf16[144,128]{1,0:T(8,128)(2,1)S(1)}, bf16[144,128]{1,0:T(8,128)(2,1)S(1)}, u32[]{:S(2)}, u32[]{:S(2)}) collective-permute-start(bf16[144,128]{1,0:T(8,128)(2,1)S(1)} %bitcast.45), channel_id=1, source_target_pairs={{0,8},{8,16},{16,24},{24,32},{32,40},{40,48},{48,56},{1,9},{9,17},... | collective-permute-start | bytes 110600 | tf_op jit(solution)/shard_map/ppermute | solution.py:21
  68.9 7.8 %message_round.3 = (bf16[256,128]{1,0:T(8,128)(2,1)S(1)}, bf16[144,128]{1,0:T(8,128)(2,1)S(1)}, bf16[144,128]{1,0:T(8,128)(2,1)S(1)}, bf16[144,128]{1,0:T(8,128)(2,1)S(1)}) custom-call(bf16[256,128]{1,0:T(8,128)(2,1)S(1)} %get-tuple-element.26.latent_ref, bf16[144,128]{1,0:T(8,128)(2,1)S(1)} %collective-permute-done.10.g0, bf16[144,128]{1,0:T(8,128)(2,1)S(1)} %bitcast.30, ...), custom_call_target="tpu_custom_call" | custom-call | tf_op jit(solution)/shard_map/message_round/pallas_call | solution.py:221
  77.4 4.5 %collective-permute-start.13 = (bf16[144,128]{1,0:T(8,128)(2,1)S(1)}, bf16[144,128]{1,0:T(8,128)(2,1)S(1)}, u32[]{:S(2)}, u32[]{:S(2)}) collective-permute-start(bf16[144,128]{1,0:T(8,128)(2,1)S(1)} %get-tuple-element.43), channel_id=1, source_target_pairs={{0,1},{1,0},{2,3},{3,2},{4,5},{5,4},{6,7},{7,6},{8,9},{9,8},{10,11... | collective-permute-start | bytes 110600 | tf_op jit(solution)/shard_map/ppermute | solution.py:241
  83.1 5.1 %collective-permute-start.14 = (bf16[144,128]{1,0:T(8,128)(2,1)S(1)}, bf16[144,128]{1,0:T(8,128)(2,1)S(1)}, u32[]{:S(2)}, u32[]{:S(2)}) collective-permute-start(bf16[144,128]{1,0:T(8,128)(2,1)S(1)} %pad_maximum_fusion.12), channel_id=1, source_target_pairs={{0,64},{64,128},{128,192},{192,256},{256,320},{320,384},{384,448},... | collective-permute-start | bytes 110600 | tf_op jit(solution)/shard_map/ppermute | solution.py:21
  89.9 4.3 %collective-permute-done.15 = bf16[144,128]{1,0:T(8,128)(2,1)S(1)} collective-permute-done((bf16[144,128]{1,0:T(8,128)(2,1)S(1)}, bf16[144,128]{1,0:T(8,128)(2,1)S(1)}, u32[]{:S(2)}, u32[]{:S(2)}) %collective-permute-start.15) | collective-permute-done | bytes 36896 | tf_op jit(solution)/shard_map/ppermute | solution.py:21
  94.2 1.9 %collective-permute-start.17 = (bf16[144,128]{1,0:T(8,128)(2,1)S(1)}, bf16[144,128]{1,0:T(8,128)(2,1)S(1)}, u32[]{:S(2)}, u32[]{:S(2)}) collective-permute-start(bf16[144,128]{1,0:T(8,128)(2,1)S(1)} %bitcast.43), channel_id=1, source_target_pairs={{8,0},{16,8},{24,16},{32,24},{40,32},{48,40},{56,48},{9,1},{17,9},... | collective-permute-start | bytes 110600 | tf_op jit(solution)/shard_map/ppermute | solution.py:21
  96.1 5.4 %collective-permute-start.16 = (bf16[144,128]{1,0:T(8,128)(2,1)S(1)}, bf16[144,128]{1,0:T(8,128)(2,1)S(1)}, u32[]{:S(2)}, u32[]{:S(2)}) collective-permute-start(bf16[144,128]{1,0:T(8,128)(2,1)S(1)} %bitcast.46), channel_id=1, source_target_pairs={{0,8},{8,16},{16,24},{24,32},{32,40},{40,48},{48,56},{1,9},{9,17},... | collective-permute-start | bytes 110600 | tf_op jit(solution)/shard_map/ppermute | solution.py:21
  103.2 8.5 %last_round.1 = (f32[18,256]{1,0:T(8,128)}, f32[36,18]{1,0:T(8,128)S(1)}, f32[36,18]{1,0:T(8,128)S(1)}, f32[36,18]{1,0:T(8,128)S(1)}) custom-call(bf16[256,128]{1,0:T(8,128)(2,1)S(1)} %get-tuple-element.30.latent_ref, bf16[144,128]{1,0:T(8,128)(2,1)S(1)} %collective-permute-done.16.g0, bf16[144,128]{1,0:T(8,128)(2,1)S(1)} %bitcast.28, ...), custom_call_target="tpu_custom_call" | custom-call | tf_op jit(solution)/shard_map/last_round/pallas_call | solution.py:221
  112.4 3.4 %collective-permute-start.19 = (f32[36,18]{1,0:T(8,128)S(1)}, f32[36,18]{1,0:T(8,128)S(1)}, u32[]{:S(2)}, u32[]{:S(2)}) collective-permute-start(f32[36,18]{1,0:T(8,128)S(1)} %get-tuple-element.55), channel_id=1, source_target_pairs={{0,1},{1,0},{2,3},{3,2},{4,5},{5,4},{6,7},{7,6},{8,9},{9,8},{10,11... | collective-permute-start | bytes 7784 | tf_op jit(solution)/shard_map/ppermute | solution.py:241
  116.7 3.9 %collective-permute-start.20 = (f32[36,18]{1,0:T(8,128)S(1)}, f32[36,18]{1,0:T(8,128)S(1)}, u32[]{:S(2)}, u32[]{:S(2)}) collective-permute-start(f32[36,18]{1,0:T(8,128)S(1)} %pad_maximum_fusion.18), channel_id=1, source_target_pairs={{0,64},{64,128},{128,192},{192,256},{256,320},{320,384},{384,448},... | collective-permute-start | bytes 7784 | tf_op jit(solution)/shard_map/ppermute | solution.py:21
  122.1 4.3 %collective-permute-done.21 = f32[36,18]{1,0:T(8,128)S(1)} collective-permute-done((f32[36,18]{1,0:T(8,128)S(1)}, f32[36,18]{1,0:T(8,128)S(1)}, u32[]{:S(2)}, u32[]{:S(2)}) %collective-permute-start.21) | collective-permute-done | bytes 2624 | tf_op jit(solution)/shard_map/ppermute | solution.py:21
  126.4 5.5 %collective-permute-start.22 = (f32[36,18]{1,0:T(8,128)S(1)}, f32[36,18]{1,0:T(8,128)S(1)}, u32[]{:S(2)}, u32[]{:S(2)}) collective-permute-start(f32[36,18]{1,0:T(8,128)S(1)} %reshape.192), channel_id=1, source_target_pairs={{0,8},{8,16},{16,24},{24,32},{32,40},{40,48},{48,56},{1,9},{9,17},... | collective-permute-start | bytes 7784 | tf_op jit(solution)/shard_map/ppermute | solution.py:21
  131.9 1.9 %collective-permute-start.23 = (f32[36,18]{1,0:T(8,128)S(1)}, f32[36,18]{1,0:T(8,128)S(1)}, u32[]{:S(2)}, u32[]{:S(2)}) collective-permute-start(f32[36,18]{1,0:T(8,128)S(1)} %reshape.193), channel_id=1, source_target_pairs={{8,0},{16,8},{24,16},{32,24},{40,32},{48,40},{56,48},{9,1},{17,9},... | collective-permute-start | bytes 7784 | tf_op jit(solution)/shard_map/ppermute | solution.py:21
  133.9 4.9 %collective-permute-done.23 = f32[36,18]{1,0:T(8,128)S(1)} collective-permute-done((f32[36,18]{1,0:T(8,128)S(1)}, f32[36,18]{1,0:T(8,128)S(1)}, u32[]{:S(2)}, u32[]{:S(2)}) %collective-permute-start.23) | collective-permute-done | bytes 2624 | tf_op jit(solution)/shard_map/ppermute | solution.py:21
  (137 shorter events, 28.6 us)
Async XLA Ops:
  4.5 12.6 %collective-permute-start = (bf16[144,128]{1,0:T(8,128)(2,1)S(1)}, bf16[144,128]{1,0:T(8,128)(2,1)S(1)}, u32[]{:S(2)}, u32[]{:S(2)}) collective-permute-start(bf16[144,128]{1,0:T(8,128)(2,1)S(1)} %get-tuple-element.50), channel_id=1, source_target_pairs={{1,2},{2,1},{3,4},{4,3},{5,6},{6,5},{9,10},{10,9},{11,12},{12,11},... | collective-permute-start | bytes 110600 | tf_op jit(solution)/shard_map/ppermute | solution.py:241
  5.2 12.0 %collective-permute-start.1 = (bf16[144,128]{1,0:T(8,128)(2,1)S(1)}, bf16[144,128]{1,0:T(8,128)(2,1)S(1)}, u32[]{:S(2)}, u32[]{:S(2)}) collective-permute-start(bf16[144,128]{1,0:T(8,128)(2,1)S(1)} %get-tuple-element.51), channel_id=1, source_target_pairs={{0,1},{1,0},{2,3},{3,2},{4,5},{5,4},{6,7},{7,6},{8,9},{9,8},{10,11... | collective-permute-start | bytes 110600 | tf_op jit(solution)/shard_map/ppermute | solution.py:241
  17.2 5.1 %collective-permute-start.2 = (bf16[144,128]{1,0:T(8,128)(2,1)S(1)}, bf16[144,128]{1,0:T(8,128)(2,1)S(1)}, u32[]{:S(2)}, u32[]{:S(2)}) collective-permute-start(bf16[144,128]{1,0:T(8,128)(2,1)S(1)} %pad_maximum_fusion), channel_id=1, source_target_pairs={{0,64},{64,128},{128,192},{192,256},{256,320},{320,384},{384,448},... | collective-permute-start | bytes 110600 | tf_op jit(solution)/shard_map/ppermute | solution.py:21
  20.7 5.9 %collective-permute-start.3 = (bf16[144,128]{1,0:T(8,128)(2,1)S(1)}, bf16[144,128]{1,0:T(8,128)(2,1)S(1)}, u32[]{:S(2)}, u32[]{:S(2)}) collective-permute-start(bf16[144,128]{1,0:T(8,128)(2,1)S(1)} %pad_maximum_fusion.2), channel_id=1, source_target_pairs={{64,0},{128,64},{192,128},{256,192},{320,256},{384,320},{448,384},... | collective-permute-start | bytes 110600 | tf_op jit(solution)/shard_map/ppermute | solution.py:21
  26.6 7.5 %collective-permute-start.5 = (bf16[144,128]{1,0:T(8,128)(2,1)S(1)}, bf16[144,128]{1,0:T(8,128)(2,1)S(1)}, u32[]{:S(2)}, u32[]{:S(2)}) collective-permute-start(bf16[144,128]{1,0:T(8,128)(2,1)S(1)} %bitcast.41), channel_id=1, source_target_pairs={{8,0},{16,8},{24,16},{32,24},{40,32},{48,40},{56,48},{9,1},{17,9},... | collective-permute-start | bytes 110600 | tf_op jit(solution)/shard_map/ppermute | solution.py:21
  28.6 7.1 %collective-permute-start.4 = (bf16[144,128]{1,0:T(8,128)(2,1)S(1)}, bf16[144,128]{1,0:T(8,128)(2,1)S(1)}, u32[]{:S(2)}, u32[]{:S(2)}) collective-permute-start(bf16[144,128]{1,0:T(8,128)(2,1)S(1)} %bitcast.44), channel_id=1, source_target_pairs={{0,8},{8,16},{16,24},{24,32},{32,40},{40,48},{48,56},{1,9},{9,17},... | collective-permute-start | bytes 110600 | tf_op jit(solution)/shard_map/ppermute | solution.py:21
  43.5 6.6 %collective-permute-start.6 = (bf16[144,128]{1,0:T(8,128)(2,1)S(1)}, bf16[144,128]{1,0:T(8,128)(2,1)S(1)}, u32[]{:S(2)}, u32[]{:S(2)}) collective-permute-start(bf16[144,128]{1,0:T(8,128)(2,1)S(1)} %get-tuple-element.46), channel_id=1, source_target_pairs={{1,2},{2,1},{3,4},{4,3},{5,6},{6,5},{9,10},{10,9},{11,12},{12,11},... | collective-permute-start | bytes 110600 | tf_op jit(solution)/shard_map/ppermute | solution.py:241
  44.2 5.9 %collective-permute-start.7 = (bf16[144,128]{1,0:T(8,128)(2,1)S(1)}, bf16[144,128]{1,0:T(8,128)(2,1)S(1)}, u32[]{:S(2)}, u32[]{:S(2)}) collective-permute-start(bf16[144,128]{1,0:T(8,128)(2,1)S(1)} %get-tuple-element.47), channel_id=1, source_target_pairs={{0,1},{1,0},{2,3},{3,2},{4,5},{5,4},{6,7},{7,6},{8,9},{9,8},{10,11... | collective-permute-start | bytes 110600 | tf_op jit(solution)/shard_map/ppermute | solution.py:241
  50.2 5.1 %collective-permute-start.8 = (bf16[144,128]{1,0:T(8,128)(2,1)S(1)}, bf16[144,128]{1,0:T(8,128)(2,1)S(1)}, u32[]{:S(2)}, u32[]{:S(2)}) collective-permute-start(bf16[144,128]{1,0:T(8,128)(2,1)S(1)} %pad_maximum_fusion.6), channel_id=1, source_target_pairs={{0,64},{64,128},{128,192},{192,256},{256,320},{320,384},{384,448},... | collective-permute-start | bytes 110600 | tf_op jit(solution)/shard_map/ppermute | solution.py:21
  53.7 6.2 %collective-permute-start.9 = (bf16[144,128]{1,0:T(8,128)(2,1)S(1)}, bf16[144,128]{1,0:T(8,128)(2,1)S(1)}, u32[]{:S(2)}, u32[]{:S(2)}) collective-permute-start(bf16[144,128]{1,0:T(8,128)(2,1)S(1)} %pad_maximum_fusion.8), channel_id=1, source_target_pairs={{64,0},{128,64},{192,128},{256,192},{320,256},{384,320},{448,384},... | collective-permute-start | bytes 110600 | tf_op jit(solution)/shard_map/ppermute | solution.py:21
  59.9 7.6 %collective-permute-start.11 = (bf16[144,128]{1,0:T(8,128)(2,1)S(1)}, bf16[144,128]{1,0:T(8,128)(2,1)S(1)}, u32[]{:S(2)}, u32[]{:S(2)}) collective-permute-start(bf16[144,128]{1,0:T(8,128)(2,1)S(1)} %bitcast.42), channel_id=1, source_target_pairs={{8,0},{16,8},{24,16},{32,24},{40,32},{48,40},{56,48},{9,1},{17,9},... | collective-permute-start | bytes 110600 | tf_op jit(solution)/shard_map/ppermute | solution.py:21
  61.9 7.1 %collective-permute-start.10 = (bf16[144,128]{1,0:T(8,128)(2,1)S(1)}, bf16[144,128]{1,0:T(8,128)(2,1)S(1)}, u32[]{:S(2)}, u32[]{:S(2)}) collective-permute-start(bf16[144,128]{1,0:T(8,128)(2,1)S(1)} %bitcast.45), channel_id=1, source_target_pairs={{0,8},{8,16},{16,24},{24,32},{32,40},{40,48},{48,56},{1,9},{9,17},... | collective-permute-start | bytes 110600 | tf_op jit(solution)/shard_map/ppermute | solution.py:21
  76.7 6.3 %collective-permute-start.12 = (bf16[144,128]{1,0:T(8,128)(2,1)S(1)}, bf16[144,128]{1,0:T(8,128)(2,1)S(1)}, u32[]{:S(2)}, u32[]{:S(2)}) collective-permute-start(bf16[144,128]{1,0:T(8,128)(2,1)S(1)} %get-tuple-element.42), channel_id=1, source_target_pairs={{1,2},{2,1},{3,4},{4,3},{5,6},{6,5},{9,10},{10,9},{11,12},{12,11},... | collective-permute-start | bytes 110600 | tf_op jit(solution)/shard_map/ppermute | solution.py:241
  77.4 5.7 %collective-permute-start.13 = (bf16[144,128]{1,0:T(8,128)(2,1)S(1)}, bf16[144,128]{1,0:T(8,128)(2,1)S(1)}, u32[]{:S(2)}, u32[]{:S(2)}) collective-permute-start(bf16[144,128]{1,0:T(8,128)(2,1)S(1)} %get-tuple-element.43), channel_id=1, source_target_pairs={{0,1},{1,0},{2,3},{3,2},{4,5},{5,4},{6,7},{7,6},{8,9},{9,8},{10,11... | collective-permute-start | bytes 110600 | tf_op jit(solution)/shard_map/ppermute | solution.py:241
  83.1 6.8 %collective-permute-start.14 = (bf16[144,128]{1,0:T(8,128)(2,1)S(1)}, bf16[144,128]{1,0:T(8,128)(2,1)S(1)}, u32[]{:S(2)}, u32[]{:S(2)}) collective-permute-start(bf16[144,128]{1,0:T(8,128)(2,1)S(1)} %pad_maximum_fusion.12), channel_id=1, source_target_pairs={{0,64},{64,128},{128,192},{192,256},{256,320},{320,384},{384,448},... | collective-permute-start | bytes 110600 | tf_op jit(solution)/shard_map/ppermute | solution.py:21
  88.3 5.9 %collective-permute-start.15 = (bf16[144,128]{1,0:T(8,128)(2,1)S(1)}, bf16[144,128]{1,0:T(8,128)(2,1)S(1)}, u32[]{:S(2)}, u32[]{:S(2)}) collective-permute-start(bf16[144,128]{1,0:T(8,128)(2,1)S(1)} %pad_maximum_fusion.14), channel_id=1, source_target_pairs={{64,0},{128,64},{192,128},{256,192},{320,256},{384,320},{448,384},... | collective-permute-start | bytes 110600 | tf_op jit(solution)/shard_map/ppermute | solution.py:21
  94.2 7.4 %collective-permute-start.17 = (bf16[144,128]{1,0:T(8,128)(2,1)S(1)}, bf16[144,128]{1,0:T(8,128)(2,1)S(1)}, u32[]{:S(2)}, u32[]{:S(2)}) collective-permute-start(bf16[144,128]{1,0:T(8,128)(2,1)S(1)} %bitcast.43), channel_id=1, source_target_pairs={{8,0},{16,8},{24,16},{32,24},{40,32},{48,40},{56,48},{9,1},{17,9},... | collective-permute-start | bytes 110600 | tf_op jit(solution)/shard_map/ppermute | solution.py:21
  96.1 7.1 %collective-permute-start.16 = (bf16[144,128]{1,0:T(8,128)(2,1)S(1)}, bf16[144,128]{1,0:T(8,128)(2,1)S(1)}, u32[]{:S(2)}, u32[]{:S(2)}) collective-permute-start(bf16[144,128]{1,0:T(8,128)(2,1)S(1)} %bitcast.46), channel_id=1, source_target_pairs={{0,8},{8,16},{16,24},{24,32},{32,40},{40,48},{48,56},{1,9},{9,17},... | collective-permute-start | bytes 110600 | tf_op jit(solution)/shard_map/ppermute | solution.py:21
  111.7 4.1 %collective-permute-start.18 = (f32[36,18]{1,0:T(8,128)S(1)}, f32[36,18]{1,0:T(8,128)S(1)}, u32[]{:S(2)}, u32[]{:S(2)}) collective-permute-start(f32[36,18]{1,0:T(8,128)S(1)} %get-tuple-element.54), channel_id=1, source_target_pairs={{1,2},{2,1},{3,4},{4,3},{5,6},{6,5},{9,10},{10,9},{11,12},{12,11},... | collective-permute-start | bytes 7784 | tf_op jit(solution)/shard_map/ppermute | solution.py:241
  112.4 4.3 %collective-permute-start.19 = (f32[36,18]{1,0:T(8,128)S(1)}, f32[36,18]{1,0:T(8,128)S(1)}, u32[]{:S(2)}, u32[]{:S(2)}) collective-permute-start(f32[36,18]{1,0:T(8,128)S(1)} %get-tuple-element.55), channel_id=1, source_target_pairs={{0,1},{1,0},{2,3},{3,2},{4,5},{5,4},{6,7},{7,6},{8,9},{9,8},{10,11... | collective-permute-start | bytes 7784 | tf_op jit(solution)/shard_map/ppermute | solution.py:241
  116.7 5.4 %collective-permute-start.20 = (f32[36,18]{1,0:T(8,128)S(1)}, f32[36,18]{1,0:T(8,128)S(1)}, u32[]{:S(2)}, u32[]{:S(2)}) collective-permute-start(f32[36,18]{1,0:T(8,128)S(1)} %pad_maximum_fusion.18), channel_id=1, source_target_pairs={{0,64},{64,128},{128,192},{192,256},{256,320},{320,384},{384,448},... | collective-permute-start | bytes 7784 | tf_op jit(solution)/shard_map/ppermute | solution.py:21
  120.7 5.7 %collective-permute-start.21 = (f32[36,18]{1,0:T(8,128)S(1)}, f32[36,18]{1,0:T(8,128)S(1)}, u32[]{:S(2)}, u32[]{:S(2)}) collective-permute-start(f32[36,18]{1,0:T(8,128)S(1)} %pad_maximum_fusion.20), channel_id=1, source_target_pairs={{64,0},{128,64},{192,128},{256,192},{320,256},{384,320},{448,384},... | collective-permute-start | bytes 7784 | tf_op jit(solution)/shard_map/ppermute | solution.py:21
  126.4 7.4 %collective-permute-start.22 = (f32[36,18]{1,0:T(8,128)S(1)}, f32[36,18]{1,0:T(8,128)S(1)}, u32[]{:S(2)}, u32[]{:S(2)}) collective-permute-start(f32[36,18]{1,0:T(8,128)S(1)} %reshape.192), channel_id=1, source_target_pairs={{0,8},{8,16},{16,24},{24,32},{32,40},{40,48},{48,56},{1,9},{9,17},... | collective-permute-start | bytes 7784 | tf_op jit(solution)/shard_map/ppermute | solution.py:21
  131.9 6.9 %collective-permute-start.23 = (f32[36,18]{1,0:T(8,128)S(1)}, f32[36,18]{1,0:T(8,128)S(1)}, u32[]{:S(2)}, u32[]{:S(2)}) collective-permute-start(f32[36,18]{1,0:T(8,128)S(1)} %reshape.193), channel_id=1, source_target_pairs={{8,0},{16,8},{24,16},{32,24},{40,32},{48,40},{56,48},{9,1},{17,9},... | collective-permute-start | bytes 7784 | tf_op jit(solution)/shard_map/ppermute | solution.py:21
  (19 other events, 204.2 us)

commit v3 on v2

--- a/solution.py
+++ b/solution.py
@@ -13,6 +13,7 @@
 F32 = jnp.float32
 BF16 = jnp.bfloat16
 VMEM_LIMIT = 48 * 1024 * 1024
+FETCH_LIMIT = 60 * 1024 * 1024
 
 
 def shifted(value, axis, steps):
@@ -125,7 +126,8 @@
     return jnp.concatenate(picked, axis=0)
 
 
-def local_kernel(latent_ref, edge_ref, column_ref, w1_ref, out_ref):
+def local_kernel(latent_ref, edge_ref, column_ref, w1_ref, *refs):
+    out_ref = refs[-1]
     slots, particles, width = edge_ref.shape
     latent = latent_ref[...]
     receiver = mm(latent, w1_ref[0, width : 2 * width])
@@ -151,7 +153,7 @@
     sender = jnp.concatenate(halves(mm(ghosts, ew1_ref[0, 2 * width :])), axis=1)
     second = centred(ew2_ref[0])
     lanes = lax.broadcasted_iota(jnp.int32, (particles, padded), 1) + particles
-    counts = column_ref[:, slots : slots + 1]
+    counts = jnp.broadcast_to(column_ref[:, slots : slots + 1], (particles, width))
     summed = jnp.zeros((particles, width), F32)
     for k in range(0, slots, BLOCK):
         both = mm(one_hot(column_ref, k, BLOCK, lanes), sender)
@@ -159,9 +161,10 @@
         pre = pre + both[:, :width] + both[:, width:]
         hidden = jnp.maximum(pre, 0.0).astype(BF16)
         center, scale = normalised(hidden, second)
+        message = center * scale
         for j in range(BLOCK):
             rows = slice(j * particles, (j + 1) * particles)
-            summed = summed + center[rows] * jnp.where(counts > k + j, scale[rows], 0.0)
+            summed = summed + jnp.where(counts > k + j, message[rows], 0.0)
     aggregate = (summed * eg_ref[r : r + 1]).astype(BF16)
     node_pre = mm(jnp.concatenate([latent, aggregate], axis=1), nw1_ref[0])
     node_mid = jnp.maximum(node_pre, 0.0).astype(BF16)
@@ -178,7 +181,7 @@
 
 
 def last_kernel(r, latent_ref, g0, g1, g2, part_ref, column_ref, *refs):
-    kin_ref, leave_ref, dw1_ref, dw2_ref, stayed_ref, low, mid, high = refs[6:]
+    kin_ref, dir_ref, slot_ref, dw1_ref, dw2_ref, stayed_ref, low, mid, high = refs[6:]
     latent = updated_latent(r, latent_ref, (g0, g1, g2), part_ref, column_ref, refs[:6])
     decoded = jnp.maximum(mm(latent, dw1_ref[...]), 0.0)
     decoded = decoded.astype(BF16).astype(F32)
@@ -192,11 +195,11 @@
     state_rows, particles = kin_ref.shape
     velocity = kin_ref[state_rows - 3 :, :] + acceleration
     state = jnp.concatenate([kin_ref[:3, :] + velocity, kin_ref[6:, :], velocity], axis=0)
-    direction = leave_ref[0:1, :]
+    direction = dir_ref[...]
     staying = direction == 13
     stayed_ref[...] = jnp.where(staying, state, 0.0)
     dx, dy, dz = split_direction(direction)
-    code = (dz * 9 + dx * 3 + dy) * MIG + leave_ref[1:2, :]
+    code = (dz * 9 + dx * 3 + dy) * MIG + slot_ref[...]
     code = jnp.where(staying, -1, code)
     picker = jnp.where(
         code == lax.broadcasted_iota(jnp.int32, (27 * MIG, particles), 0), 1.0, 0.0
@@ -230,6 +233,34 @@
     )(*args)
 
 
+def fetching(body, count, *refs):
+    sources, outs = refs[:count], refs[count : -count - 1]
+    targets, sems = refs[-count - 1 : -1], refs[-1]
+    copies = [
+        pltpu.make_async_copy(source, target, sems.at[i])
+        for i, (source, target) in enumerate(zip(sources, targets))
+    ]
+    for copy in copies:
+        copy.start()
+    for copy in copies:
+        copy.wait()
+    body(*targets, *outs)
+
+
+def call_fetching(body, args, outs, name, flops=0, moved=0):
+    return pl.pallas_call(
+        functools.partial(fetching, body, len(args)),
+        in_specs=[pl.BlockSpec(memory_space=pltpu.HBM)] * len(args),
+        out_specs=[pl.BlockSpec(memory_space=pltpu.VMEM)] * len(outs),
+        out_shape=outs,
+        scratch_shapes=[pltpu.VMEM(a.shape, a.dtype) for a in args]
+        + [pltpu.SemaphoreType.DMA((len(args),))],
+        compiler_params=pltpu.CompilerParams(vmem_limit_bytes=FETCH_LIMIT),
+        cost_estimate=pl.CostEstimate(flops=flops, bytes_accessed=moved, transcendentals=0),
+        name=name,
+    )(*args)
+
+
 def shape(dims, dtype):
     return jax.ShapeDtypeStruct(dims, dtype)
 
@@ -257,6 +288,7 @@
 def exchanged(low, mid, high, rows):
     tail = low.shape[-1]
     parts = moved_in_pairs(low, mid, high, "gz")
+    hold = parts[0]
     parts = [part.reshape(3, 3 * rows, tail) for part in parts]
     parts = moved(*(jnp.concatenate([part[x] for part in parts], axis=0) for x in range(3)), "gx")
     parts = [part.reshape(3, 3, rows, tail) for part in parts]
@@ -264,7 +296,7 @@
         jnp.stack([part[:, y] for part in parts], axis=1).reshape(9 * rows, tail)
         for y in range(3)
     )
-    return moved(low, mid, high, "gy")
+    return moved(low, mid, high, "gy"), hold
 
 
 def on_device(
@@ -295,14 +327,13 @@
     state_rows = kinematics.shape[0]
     rows = send_rows.T
     part = shape((9 * ghost_rows, width), BF16)
-    latent, low, mid, high = call(
+    latent, low, mid, high = call_fetching(
         node_kernel,
         (kinematics, enc_node_w1, enc_node_w2, rows),
-        (None,) * 4,
         [shape((particles, width), BF16), part, part, part],
         "node_encoder",
     )
-    edges, columns = call(
+    edges, columns = call_fetching(
         edge_kernel,
         (
             pair_offsets,
@@ -311,23 +342,23 @@
             enc_edge_w1,
             enc_edge_w2,
         ),
-        (None,) * 5,
         [shape((slots, particles, width), BF16), shape((particles, 128), jnp.int32)],
         "edge_encoder",
         flops=2 * slots * particles * 256 * 384,
         moved=4 * slots * particles * width,
     )
-    leaving = jnp.stack([migrate_dir, migrate_slot], axis=0)
+    leaving = [migrate_dir.reshape(1, particles), migrate_slot.reshape(1, particles)]
     for r in range(rounds):
-        ghosts = exchanged(low, mid, high, ghost_rows)
+        ghosts, hold = exchanged(low, mid, high, ghost_rows)
 
         def of_round(array):
             return pl.BlockSpec((1,) + array.shape[1:], lambda i: (r, 0, 0))
 
+        held = (hold,) if r == 0 else ()
         (part_sum,) = call(
             local_kernel,
-            (latent, edges, columns, edge_w1),
-            (None, None, None, of_round(edge_w1)),
+            (latent, edges, columns, edge_w1) + held,
+            (None, None, None, of_round(edge_w1)) + (None,) * len(held),
             [shape((slots, particles, width), F32)],
             "local_pairs",
             flops=2 * slots * particles * 256 * 512,
@@ -348,12 +379,12 @@
             out = shape((9 * MIG, state_rows), F32)
             stayed, low, mid, high = call(
                 functools.partial(last_kernel, r),
-                args + [kinematics, leaving, dec_w1, dec_w2],
-                specs + [None] * 4,
+                args + [kinematics, *leaving, dec_w1, dec_w2],
+                specs + [None] * 5,
                 [shape((state_rows, particles), F32), out, out, out],
                 "last_round",
             )
-    landed = jnp.stack(exchanged(low, mid, high, MIG), axis=0)
+    landed = jnp.stack(exchanged(low, mid, high, MIG)[0], axis=0)
     landed = landed.reshape(3, 3, 3, MIG, state_rows).transpose(4, 2, 0, 1, 3)
     return (stayed, landed.reshape(state_rows, 27 * MIG))
 

time: 141 us -> 124 us (0.88)
  the two profiles are of different devices: /device:TPU:192 before, /device:TPU:48 now
where the time goes in v3:
time: 124 us; the launch traced here: 123 us
  starting transfers between devices  67 us (54%)
  waiting for transfers between devices  28.6 us (23%)
  Pallas kernels  20.5 us (17%)
  local copies, waits for them, and re-layouts  3.84 us (3%)
  between operations  1.55 us (1%)
    ppermute x16, starting transfers between devices, shifted(): lax.ppermute(value, axis, [(source, source + steps) for source in range(f...  47 us
    ppermute x16, waiting for transfers between devices, shifted(): lax.ppermute(value, axis, [(source, source + steps) for source in range(f...  27.8 us
    ppermute x8, starting transfers between devices, swapped(): return lax.ppermute(value, axis, pairs)  20.1 us
    pallas_call x6, Pallas kernels, call(): pl.pallas_call(body, grid=(1,), in_specs=[spec if spec is not None else w...  14.6 us
    pallas_call x2, Pallas kernels, call_fetching(): pl.pallas_call(functools.partial(fetching, body, len(args)), in_specs=[pl...  5.88 us
    unnamed x31, local copies, waits for them, and re-layouts  2.87 us
  transfers between devices with their start and end apart: 24, of which 11 were waited for; matrix products, arithmetic and copies ran while one was open for 1% of the time, Pallas kernels for 6%

profile of v3, /device:TPU:48, one launch (start us, length us, event | category | flops | bytes accessed | tf_op | source)
XLA Modules:
  0.0 122.7 jit_solution(8963959960379612214)
XLA Ops:
  4.5 4.8 %collective-permute-start.1 = (bf16[144,128]{1,0:T(8,128)(2,1)S(1)}, bf16[144,128]{1,0:T(8,128)(2,1)S(1)}, u32[]{:S(2)}, u32[]{:S(2)}) collective-permute-start(bf16[144,128]{1,0:T(8,128)(2,1)S(1)} %get-tuple-element.51), channel_id=1, source_target_pairs={{0,1},{1,0},{2,3},{3,2},{4,5},{5,4},{6,7},{7,6},{8,9},{9,8},{10,11... | collective-permute-start | bytes 110600 | tf_op jit(solution)/shard_map/ppermute | solution.py:272
  10.1 3.5 %edge_encoder.1 = (bf16[16,256,128]{2,1,0:T(8,128)(2,1)}, s32[256,128]{1,0:T(8,128)}) custom-call(f32[3,16,256]{2,1,0:T(8,128)} %refs_0_.6, s32[16,256]{1,0:T(8,128)} %refs_1_.6, s32[1,256]{1,0:T(1,128)} %bitcast.51, f32[4,128]{1,0:T(4,128)} %refs_3_.4, bf16[128,128]{1,0:T(8,128)(2,1)} %refs_4_.4), custom_call_target="tpu_custom_call" | custom-call | flops 805306368 | bytes 2097152 | tf_op jit(solution)/shard_map/edge_encoder/pallas_call | solution.py:251
  13.7 3.3 %collective-permute-start.3 = (bf16[144,128]{1,0:T(8,128)(2,1)S(1)}, bf16[144,128]{1,0:T(8,128)(2,1)S(1)}, u32[]{:S(2)}, u32[]{:S(2)}) collective-permute-start(bf16[144,128]{1,0:T(8,128)(2,1)S(1)} %pad_maximum_fusion.2), channel_id=1, source_target_pairs={{64,0},{128,64},{192,128},{256,192},{320,256},{384,320},{448,384},... | collective-permute-start | bytes 110600 | tf_op jit(solution)/shard_map/ppermute | solution.py:22
  16.9 2.6 %collective-permute-start.2 = (bf16[144,128]{1,0:T(8,128)(2,1)S(1)}, bf16[144,128]{1,0:T(8,128)(2,1)S(1)}, u32[]{:S(2)}, u32[]{:S(2)}) collective-permute-start(bf16[144,128]{1,0:T(8,128)(2,1)S(1)} %pad_maximum_fusion), channel_id=1, source_target_pairs={{0,64},{64,128},{128,192},{192,256},{256,320},{320,384},{384,448},... | collective-permute-start | bytes 110600 | tf_op jit(solution)/shard_map/ppermute | solution.py:22
  22.9 4.3 %collective-permute-start.4 = (bf16[144,128]{1,0:T(8,128)(2,1)S(1)}, bf16[144,128]{1,0:T(8,128)(2,1)S(1)}, u32[]{:S(2)}, u32[]{:S(2)}) collective-permute-start(bf16[144,128]{1,0:T(8,128)(2,1)S(1)} %bitcast.40), channel_id=1, source_target_pairs={{0,8},{8,16},{16,24},{24,32},{32,40},{40,48},{48,56},{1,9},{9,17},... | collective-permute-start | bytes 110600 | tf_op jit(solution)/shard_map/ppermute | solution.py:22
  28.8 4.6 %collective-permute-done.5.g2 = bf16[144,128]{1,0:T(8,128)(2,1)S(1)} collective-permute-done((bf16[144,128]{1,0:T(8,128)(2,1)S(1)}, bf16[144,128]{1,0:T(8,128)(2,1)S(1)}, u32[]{:S(2)}, u32[]{:S(2)}) %collective-permute-start.5) | collective-permute-done | bytes 36896 | tf_op jit(solution)/shard_map/ppermute | solution.py:22
  33.5 3.5 %message_round.2 = (bf16[256,128]{1,0:T(8,128)(2,1)S(1)}, bf16[144,128]{1,0:T(8,128)(2,1)S(1)}, bf16[144,128]{1,0:T(8,128)(2,1)S(1)}, bf16[144,128]{1,0:T(8,128)(2,1)S(1)}) custom-call(bf16[256,128]{1,0:T(8,128)(2,1)S(1)} %copy-done.7, bf16[144,128]{1,0:T(8,128)(2,1)S(1)} %collective-permute-done.4.g0, bf16[144,128]{1,0:T(8,128)(2,1)S(1)} %bitcast.29, ...), custom_call_target="tpu_custom_call" | custom-call | tf_op jit(solution)/shard_map/message_round/pallas_call | solution.py:224
  37.7 4.8 %collective-permute-start.7 = (bf16[144,128]{1,0:T(8,128)(2,1)S(1)}, bf16[144,128]{1,0:T(8,128)(2,1)S(1)}, u32[]{:S(2)}, u32[]{:S(2)}) collective-permute-start(bf16[144,128]{1,0:T(8,128)(2,1)S(1)} %get-tuple-element.47), channel_id=1, source_target_pairs={{0,1},{1,0},{2,3},{3,2},{4,5},{5,4},{6,7},{7,6},{8,9},{9,8},{10,11... | collective-permute-start | bytes 110600 | tf_op jit(solution)/shard_map/ppermute | solution.py:272
  43.7 3.3 %collective-permute-start.9 = (bf16[144,128]{1,0:T(8,128)(2,1)S(1)}, bf16[144,128]{1,0:T(8,128)(2,1)S(1)}, u32[]{:S(2)}, u32[]{:S(2)}) collective-permute-start(bf16[144,128]{1,0:T(8,128)(2,1)S(1)} %pad_maximum_fusion.8), channel_id=1, source_target_pairs={{64,0},{128,64},{192,128},{256,192},{320,256},{384,320},{448,384},... | collective-permute-start | bytes 110600 | tf_op jit(solution)/shard_map/ppermute | solution.py:22
  47.0 2.6 %collective-permute-start.8 = (bf16[144,128]{1,0:T(8,128)(2,1)S(1)}, bf16[144,128]{1,0:T(8,128)(2,1)S(1)}, u32[]{:S(2)}, u32[]{:S(2)}) collective-permute-start(bf16[144,128]{1,0:T(8,128)(2,1)S(1)} %pad_maximum_fusion.6), channel_id=1, source_target_pairs={{0,64},{64,128},{128,192},{192,256},{256,320},{320,384},{384,448},... | collective-permute-start | bytes 110600 | tf_op jit(solution)/shard_map/ppermute | solution.py:22
  49.6 3.2 %collective-permute-done.8 = bf16[144,128]{1,0:T(8,128)(2,1)S(1)} collective-permute-done((bf16[144,128]{1,0:T(8,128)(2,1)S(1)}, bf16[144,128]{1,0:T(8,128)(2,1)S(1)}, u32[]{:S(2)}, u32[]{:S(2)}) %collective-permute-start.8) | collective-permute-done | bytes 36896 | tf_op jit(solution)/shard_map/ppermute | solution.py:22
  52.8 4.3 %collective-permute-start.10 = (bf16[144,128]{1,0:T(8,128)(2,1)S(1)}, bf16[144,128]{1,0:T(8,128)(2,1)S(1)}, u32[]{:S(2)}, u32[]{:S(2)}) collective-permute-start(bf16[144,128]{1,0:T(8,128)(2,1)S(1)} %bitcast.41), channel_id=1, source_target_pairs={{0,8},{8,16},{16,24},{24,32},{32,40},{40,48},{48,56},{1,9},{9,17},... | collective-permute-start | bytes 110600 | tf_op jit(solution)/shard_map/ppermute | solution.py:22
  58.7 5.8 %collective-permute-done.11.g2 = bf16[144,128]{1,0:T(8,128)(2,1)S(1)} collective-permute-done((bf16[144,128]{1,0:T(8,128)(2,1)S(1)}, bf16[144,128]{1,0:T(8,128)(2,1)S(1)}, u32[]{:S(2)}, u32[]{:S(2)}) %collective-permute-start.11) | collective-permute-done | bytes 36896 | tf_op jit(solution)/shard_map/ppermute | solution.py:22
  64.5 3.5 %message_round.3 = (bf16[256,128]{1,0:T(8,128)(2,1)S(1)}, bf16[144,128]{1,0:T(8,128)(2,1)S(1)}, bf16[144,128]{1,0:T(8,128)(2,1)S(1)}, bf16[144,128]{1,0:T(8,128)(2,1)S(1)}) custom-call(bf16[256,128]{1,0:T(8,128)(2,1)S(1)} %get-tuple-element.26.latent_ref, bf16[144,128]{1,0:T(8,128)(2,1)S(1)} %collective-permute-done.10.g0, bf16[144,128]{1,0:T(8,128)(2,1)S(1)} %bitcast.30, ...), custom_call_target="tpu_custom_call" | custom-call | tf_op jit(solution)/shard_map/message_round/pallas_call | solution.py:224
  68.7 4.5 %collective-permute-start.13 = (bf16[144,128]{1,0:T(8,128)(2,1)S(1)}, bf16[144,128]{1,0:T(8,128)(2,1)S(1)}, u32[]{:S(2)}, u32[]{:S(2)}) collective-permute-start(bf16[144,128]{1,0:T(8,128)(2,1)S(1)} %get-tuple-element.43), channel_id=1, source_target_pairs={{0,1},{1,0},{2,3},{3,2},{4,5},{5,4},{6,7},{7,6},{8,9},{9,8},{10,11... | collective-permute-start | bytes 110600 | tf_op jit(solution)/shard_map/ppermute | solution.py:272
  74.5 3.5 %collective-permute-start.15 = (bf16[144,128]{1,0:T(8,128)(2,1)S(1)}, bf16[144,128]{1,0:T(8,128)(2,1)S(1)}, u32[]{:S(2)}, u32[]{:S(2)}) collective-permute-start(bf16[144,128]{1,0:T(8,128)(2,1)S(1)} %pad_maximum_fusion.14), channel_id=1, source_target_pairs={{64,0},{128,64},{192,128},{256,192},{320,256},{384,320},{448,384},... | collective-permute-start | bytes 110600 | tf_op jit(solution)/shard_map/ppermute | solution.py:22
  80.4 4.1 %collective-permute-done.14 = bf16[144,128]{1,0:T(8,128)(2,1)S(1)} collective-permute-done((bf16[144,128]{1,0:T(8,128)(2,1)S(1)}, bf16[144,128]{1,0:T(8,128)(2,1)S(1)}, u32[]{:S(2)}, u32[]{:S(2)}) %collective-permute-start.14) | collective-permute-done | bytes 36896 | tf_op jit(solution)/shard_map/ppermute | solution.py:22
  84.5 5.1 %collective-permute-start.16 = (bf16[144,128]{1,0:T(8,128)(2,1)S(1)}, bf16[144,128]{1,0:T(8,128)(2,1)S(1)}, u32[]{:S(2)}, u32[]{:S(2)}) collective-permute-start(bf16[144,128]{1,0:T(8,128)(2,1)S(1)} %bitcast.42), channel_id=1, source_target_pairs={{0,8},{8,16},{16,24},{24,32},{32,40},{40,48},{48,56},{1,9},{9,17},... | collective-permute-start | bytes 110600 | tf_op jit(solution)/shard_map/ppermute | solution.py:22
  91.3 4.3 %collective-permute-done.17.g2 = bf16[144,128]{1,0:T(8,128)(2,1)S(1)} collective-permute-done((bf16[144,128]{1,0:T(8,128)(2,1)S(1)}, bf16[144,128]{1,0:T(8,128)(2,1)S(1)}, u32[]{:S(2)}, u32[]{:S(2)}) %collective-permute-start.17) | collective-permute-done | bytes 36896 | tf_op jit(solution)/shard_map/ppermute | solution.py:22
  95.6 4.3 %last_round.1 = (f32[18,256]{1,0:T(8,128)}, f32[36,18]{1,0:T(8,128)S(1)}, f32[36,18]{1,0:T(8,128)S(1)}, f32[36,18]{1,0:T(8,128)S(1)}) custom-call(bf16[256,128]{1,0:T(8,128)(2,1)S(1)} %get-tuple-element.30.latent_ref, bf16[144,128]{1,0:T(8,128)(2,1)S(1)} %collective-permute-done.16.g0, bf16[144,128]{1,0:T(8,128)(2,1)S(1)} %bitcast.28, ...), custom_call_target="tpu_custom_call" | custom-call | tf_op jit(solution)/shard_map/last_round/pallas_call | solution.py:224
  100.5 3.4 %collective-permute-start.19 = (f32[36,18]{1,0:T(8,128)S(1)}, f32[36,18]{1,0:T(8,128)S(1)}, u32[]{:S(2)}, u32[]{:S(2)}) collective-permute-start(f32[36,18]{1,0:T(8,128)S(1)} %get-tuple-element.55), channel_id=1, source_target_pairs={{0,1},{1,0},{2,3},{3,2},{4,5},{5,4},{6,7},{7,6},{8,9},{9,8},{10,11... | collective-permute-start | bytes 7784 | tf_op jit(solution)/shard_map/ppermute | solution.py:272
  104.9 3.9 %collective-permute-start.21 = (f32[36,18]{1,0:T(8,128)S(1)}, f32[36,18]{1,0:T(8,128)S(1)}, u32[]{:S(2)}, u32[]{:S(2)}) collective-permute-start(f32[36,18]{1,0:T(8,128)S(1)} %pad_maximum_fusion.20), channel_id=1, source_target_pairs={{64,0},{128,64},{192,128},{256,192},{320,256},{384,320},{448,384},... | collective-permute-start | bytes 7784 | tf_op jit(solution)/shard_map/ppermute | solution.py:22
  110.8 3.7 %collective-permute-done.20 = f32[36,18]{1,0:T(8,128)S(1)} collective-permute-done((f32[36,18]{1,0:T(8,128)S(1)}, f32[36,18]{1,0:T(8,128)S(1)}, u32[]{:S(2)}, u32[]{:S(2)}) %collective-permute-start.20) | collective-permute-done | bytes 2624 | tf_op jit(solution)/shard_map/ppermute | solution.py:22
  115.9 4.5 %collective-permute-start.22 = (f32[36,18]{1,0:T(8,128)S(1)}, f32[36,18]{1,0:T(8,128)S(1)}, u32[]{:S(2)}, u32[]{:S(2)}) collective-permute-start(f32[36,18]{1,0:T(8,128)S(1)} %reshape.200), channel_id=1, source_target_pairs={{0,8},{8,16},{16,24},{24,32},{32,40},{40,48},{48,56},{1,9},{9,17},... | collective-permute-start | bytes 7784 | tf_op jit(solution)/shard_map/ppermute | solution.py:22
  (128 shorter events, 25.9 us)
Async XLA Ops:
  3.9 9.7 %collective-permute-start = (bf16[144,128]{1,0:T(8,128)(2,1)S(1)}, bf16[144,128]{1,0:T(8,128)(2,1)S(1)}, u32[]{:S(2)}, u32[]{:S(2)}) collective-permute-start(bf16[144,128]{1,0:T(8,128)(2,1)S(1)} %get-tuple-element.50), channel_id=1, source_target_pairs={{1,2},{2,1},{3,4},{4,3},{5,6},{6,5},{9,10},{10,9},{11,12},{12,11},... | collective-permute-start | bytes 110600 | tf_op jit(solution)/shard_map/ppermute | solution.py:272
  4.5 9.0 %collective-permute-start.1 = (bf16[144,128]{1,0:T(8,128)(2,1)S(1)}, bf16[144,128]{1,0:T(8,128)(2,1)S(1)}, u32[]{:S(2)}, u32[]{:S(2)}) collective-permute-start(bf16[144,128]{1,0:T(8,128)(2,1)S(1)} %get-tuple-element.51), channel_id=1, source_target_pairs={{0,1},{1,0},{2,3},{3,2},{4,5},{5,4},{6,7},{7,6},{8,9},{9,8},{10,11... | collective-permute-start | bytes 110600 | tf_op jit(solution)/shard_map/ppermute | solution.py:272
  13.7 9.2 %collective-permute-start.3 = (bf16[144,128]{1,0:T(8,128)(2,1)S(1)}, bf16[144,128]{1,0:T(8,128)(2,1)S(1)}, u32[]{:S(2)}, u32[]{:S(2)}) collective-permute-start(bf16[144,128]{1,0:T(8,128)(2,1)S(1)} %pad_maximum_fusion.2), channel_id=1, source_target_pairs={{64,0},{128,64},{192,128},{256,192},{320,256},{384,320},{448,384},... | collective-permute-start | bytes 110600 | tf_op jit(solution)/shard_map/ppermute | solution.py:22
  16.9 5.9 %collective-permute-start.2 = (bf16[144,128]{1,0:T(8,128)(2,1)S(1)}, bf16[144,128]{1,0:T(8,128)(2,1)S(1)}, u32[]{:S(2)}, u32[]{:S(2)}) collective-permute-start(bf16[144,128]{1,0:T(8,128)(2,1)S(1)} %pad_maximum_fusion), channel_id=1, source_target_pairs={{0,64},{64,128},{128,192},{192,256},{256,320},{320,384},{384,448},... | collective-permute-start | bytes 110600 | tf_op jit(solution)/shard_map/ppermute | solution.py:22
  22.9 5.9 %collective-permute-start.4 = (bf16[144,128]{1,0:T(8,128)(2,1)S(1)}, bf16[144,128]{1,0:T(8,128)(2,1)S(1)}, u32[]{:S(2)}, u32[]{:S(2)}) collective-permute-start(bf16[144,128]{1,0:T(8,128)(2,1)S(1)} %bitcast.40), channel_id=1, source_target_pairs={{0,8},{8,16},{16,24},{24,32},{32,40},{40,48},{48,56},{1,9},{9,17},... | collective-permute-start | bytes 110600 | tf_op jit(solution)/shard_map/ppermute | solution.py:22
  27.2 6.2 %collective-permute-start.5 = (bf16[144,128]{1,0:T(8,128)(2,1)S(1)}, bf16[144,128]{1,0:T(8,128)(2,1)S(1)}, u32[]{:S(2)}, u32[]{:S(2)}) collective-permute-start(bf16[144,128]{1,0:T(8,128)(2,1)S(1)} %bitcast.46), channel_id=1, source_target_pairs={{8,0},{16,8},{24,16},{32,24},{40,32},{48,40},{56,48},{9,1},{17,9},... | collective-permute-start | bytes 110600 | tf_op jit(solution)/shard_map/ppermute | solution.py:22
  37.0 6.6 %collective-permute-start.6 = (bf16[144,128]{1,0:T(8,128)(2,1)S(1)}, bf16[144,128]{1,0:T(8,128)(2,1)S(1)}, u32[]{:S(2)}, u32[]{:S(2)}) collective-permute-start(bf16[144,128]{1,0:T(8,128)(2,1)S(1)} %get-tuple-element.46), channel_id=1, source_target_pairs={{1,2},{2,1},{3,4},{4,3},{5,6},{6,5},{9,10},{10,9},{11,12},{12,11},... | collective-permute-start | bytes 110600 | tf_op jit(solution)/shard_map/ppermute | solution.py:272
  37.7 5.9 %collective-permute-start.7 = (bf16[144,128]{1,0:T(8,128)(2,1)S(1)}, bf16[144,128]{1,0:T(8,128)(2,1)S(1)}, u32[]{:S(2)}, u32[]{:S(2)}) collective-permute-start(bf16[144,128]{1,0:T(8,128)(2,1)S(1)} %get-tuple-element.47), channel_id=1, source_target_pairs={{0,1},{1,0},{2,3},{3,2},{4,5},{5,4},{6,7},{7,6},{8,9},{9,8},{10,11... | collective-permute-start | bytes 110600 | tf_op jit(solution)/shard_map/ppermute | solution.py:272
  43.7 5.9 %collective-permute-start.9 = (bf16[144,128]{1,0:T(8,128)(2,1)S(1)}, bf16[144,128]{1,0:T(8,128)(2,1)S(1)}, u32[]{:S(2)}, u32[]{:S(2)}) collective-permute-start(bf16[144,128]{1,0:T(8,128)(2,1)S(1)} %pad_maximum_fusion.8), channel_id=1, source_target_pairs={{64,0},{128,64},{192,128},{256,192},{320,256},{384,320},{448,384},... | collective-permute-start | bytes 110600 | tf_op jit(solution)/shard_map/ppermute | solution.py:22
  47.0 5.9 %collective-permute-start.8 = (bf16[144,128]{1,0:T(8,128)(2,1)S(1)}, bf16[144,128]{1,0:T(8,128)(2,1)S(1)}, u32[]{:S(2)}, u32[]{:S(2)}) collective-permute-start(bf16[144,128]{1,0:T(8,128)(2,1)S(1)} %pad_maximum_fusion.6), channel_id=1, source_target_pairs={{0,64},{64,128},{128,192},{192,256},{256,320},{320,384},{384,448},... | collective-permute-start | bytes 110600 | tf_op jit(solution)/shard_map/ppermute | solution.py:22
  52.8 5.9 %collective-permute-start.10 = (bf16[144,128]{1,0:T(8,128)(2,1)S(1)}, bf16[144,128]{1,0:T(8,128)(2,1)S(1)}, u32[]{:S(2)}, u32[]{:S(2)}) collective-permute-start(bf16[144,128]{1,0:T(8,128)(2,1)S(1)} %bitcast.41), channel_id=1, source_target_pairs={{0,8},{8,16},{16,24},{24,32},{32,40},{40,48},{48,56},{1,9},{9,17},... | collective-permute-start | bytes 110600 | tf_op jit(solution)/shard_map/ppermute | solution.py:22
  57.1 7.4 %collective-permute-start.11 = (bf16[144,128]{1,0:T(8,128)(2,1)S(1)}, bf16[144,128]{1,0:T(8,128)(2,1)S(1)}, u32[]{:S(2)}, u32[]{:S(2)}) collective-permute-start(bf16[144,128]{1,0:T(8,128)(2,1)S(1)} %bitcast.47), channel_id=1, source_target_pairs={{8,0},{16,8},{24,16},{32,24},{40,32},{48,40},{56,48},{9,1},{17,9},... | collective-permute-start | bytes 110600 | tf_op jit(solution)/shard_map/ppermute | solution.py:22
  68.1 6.3 %collective-permute-start.12 = (bf16[144,128]{1,0:T(8,128)(2,1)S(1)}, bf16[144,128]{1,0:T(8,128)(2,1)S(1)}, u32[]{:S(2)}, u32[]{:S(2)}) collective-permute-start(bf16[144,128]{1,0:T(8,128)(2,1)S(1)} %get-tuple-element.42), channel_id=1, source_target_pairs={{1,2},{2,1},{3,4},{4,3},{5,6},{6,5},{9,10},{10,9},{11,12},{12,11},... | collective-permute-start | bytes 110600 | tf_op jit(solution)/shard_map/ppermute | solution.py:272
  68.7 5.7 %collective-permute-start.13 = (bf16[144,128]{1,0:T(8,128)(2,1)S(1)}, bf16[144,128]{1,0:T(8,128)(2,1)S(1)}, u32[]{:S(2)}, u32[]{:S(2)}) collective-permute-start(bf16[144,128]{1,0:T(8,128)(2,1)S(1)} %get-tuple-element.43), channel_id=1, source_target_pairs={{0,1},{1,0},{2,3},{3,2},{4,5},{5,4},{6,7},{7,6},{8,9},{9,8},{10,11... | collective-permute-start | bytes 110600 | tf_op jit(solution)/shard_map/ppermute | solution.py:272
  74.5 5.9 %collective-permute-start.15 = (bf16[144,128]{1,0:T(8,128)(2,1)S(1)}, bf16[144,128]{1,0:T(8,128)(2,1)S(1)}, u32[]{:S(2)}, u32[]{:S(2)}) collective-permute-start(bf16[144,128]{1,0:T(8,128)(2,1)S(1)} %pad_maximum_fusion.14), channel_id=1, source_target_pairs={{64,0},{128,64},{192,128},{256,192},{320,256},{384,320},{448,384},... | collective-permute-start | bytes 110600 | tf_op jit(solution)/shard_map/ppermute | solution.py:22
  78.0 6.5 %collective-permute-start.14 = (bf16[144,128]{1,0:T(8,128)(2,1)S(1)}, bf16[144,128]{1,0:T(8,128)(2,1)S(1)}, u32[]{:S(2)}, u32[]{:S(2)}) collective-permute-start(bf16[144,128]{1,0:T(8,128)(2,1)S(1)} %pad_maximum_fusion.12), channel_id=1, source_target_pairs={{0,64},{64,128},{128,192},{192,256},{256,320},{320,384},{384,448},... | collective-permute-start | bytes 110600 | tf_op jit(solution)/shard_map/ppermute | solution.py:22
  84.5 6.8 %collective-permute-start.16 = (bf16[144,128]{1,0:T(8,128)(2,1)S(1)}, bf16[144,128]{1,0:T(8,128)(2,1)S(1)}, u32[]{:S(2)}, u32[]{:S(2)}) collective-permute-start(bf16[144,128]{1,0:T(8,128)(2,1)S(1)} %bitcast.42), channel_id=1, source_target_pairs={{0,8},{8,16},{16,24},{24,32},{32,40},{40,48},{48,56},{1,9},{9,17},... | collective-permute-start | bytes 110600 | tf_op jit(solution)/shard_map/ppermute | solution.py:22
  89.7 5.9 %collective-permute-start.17 = (bf16[144,128]{1,0:T(8,128)(2,1)S(1)}, bf16[144,128]{1,0:T(8,128)(2,1)S(1)}, u32[]{:S(2)}, u32[]{:S(2)}) collective-permute-start(bf16[144,128]{1,0:T(8,128)(2,1)S(1)} %bitcast.48), channel_id=1, source_target_pairs={{8,0},{16,8},{24,16},{32,24},{40,32},{48,40},{56,48},{9,1},{17,9},... | collective-permute-start | bytes 110600 | tf_op jit(solution)/shard_map/ppermute | solution.py:22
  99.9 4.1 %collective-permute-start.18 = (f32[36,18]{1,0:T(8,128)S(1)}, f32[36,18]{1,0:T(8,128)S(1)}, u32[]{:S(2)}, u32[]{:S(2)}) collective-permute-start(f32[36,18]{1,0:T(8,128)S(1)} %get-tuple-element.54), channel_id=1, source_target_pairs={{1,2},{2,1},{3,4},{4,3},{5,6},{6,5},{9,10},{10,9},{11,12},{12,11},... | collective-permute-start | bytes 7784 | tf_op jit(solution)/shard_map/ppermute | solution.py:272
  100.5 4.3 %collective-permute-start.19 = (f32[36,18]{1,0:T(8,128)S(1)}, f32[36,18]{1,0:T(8,128)S(1)}, u32[]{:S(2)}, u32[]{:S(2)}) collective-permute-start(f32[36,18]{1,0:T(8,128)S(1)} %get-tuple-element.55), channel_id=1, source_target_pairs={{0,1},{1,0},{2,3},{3,2},{4,5},{5,4},{6,7},{7,6},{8,9},{9,8},{10,11... | collective-permute-start | bytes 7784 | tf_op jit(solution)/shard_map/ppermute | solution.py:272
  104.9 5.9 %collective-permute-start.21 = (f32[36,18]{1,0:T(8,128)S(1)}, f32[36,18]{1,0:T(8,128)S(1)}, u32[]{:S(2)}, u32[]{:S(2)}) collective-permute-start(f32[36,18]{1,0:T(8,128)S(1)} %pad_maximum_fusion.20), channel_id=1, source_target_pairs={{64,0},{128,64},{192,128},{256,192},{320,256},{384,320},{448,384},... | collective-permute-start | bytes 7784 | tf_op jit(solution)/shard_map/ppermute | solution.py:22
  108.8 5.7 %collective-permute-start.20 = (f32[36,18]{1,0:T(8,128)S(1)}, f32[36,18]{1,0:T(8,128)S(1)}, u32[]{:S(2)}, u32[]{:S(2)}) collective-permute-start(f32[36,18]{1,0:T(8,128)S(1)} %pad_maximum_fusion.18), channel_id=1, source_target_pairs={{0,64},{64,128},{128,192},{192,256},{256,320},{320,384},{384,448},... | collective-permute-start | bytes 7784 | tf_op jit(solution)/shard_map/ppermute | solution.py:22
  114.6 5.9 %collective-permute-start.23 = (f32[36,18]{1,0:T(8,128)S(1)}, f32[36,18]{1,0:T(8,128)S(1)}, u32[]{:S(2)}, u32[]{:S(2)}) collective-permute-start(f32[36,18]{1,0:T(8,128)S(1)} %reshape.201), channel_id=1, source_target_pairs={{8,0},{16,8},{24,16},{32,24},{40,32},{48,40},{56,48},{9,1},{17,9},... | collective-permute-start | bytes 7784 | tf_op jit(solution)/shard_map/ppermute | solution.py:22
  115.9 6.0 %collective-permute-start.22 = (f32[36,18]{1,0:T(8,128)S(1)}, f32[36,18]{1,0:T(8,128)S(1)}, u32[]{:S(2)}, u32[]{:S(2)}) collective-permute-start(f32[36,18]{1,0:T(8,128)S(1)} %reshape.200), channel_id=1, source_target_pairs={{0,8},{8,16},{16,24},{24,32},{32,40},{40,48},{48,56},{1,9},{9,17},... | collective-permute-start | bytes 7784 | tf_op jit(solution)/shard_map/ppermute | solution.py:22
  (15 other events, 219.5 us)

commit v4 on v3

--- a/solution.py
+++ b/solution.py
@@ -45,17 +45,36 @@
     return center, lax.rsqrt(spread + EPS)
 
 
+def by_parity(rows, outs):
+    even = lax.axis_index("gz") % 2 == 0
+    low, mid, high = rows
+    odd_ref, mid_ref, even_ref = outs
+    mid_ref[...] = mid
+
+    @pl.when(even)
+    def _():
+        odd_ref[...] = low
+        even_ref[...] = high
+
+    @pl.when(jnp.logical_not(even))
+    def _():
+        odd_ref[...] = high
+        even_ref[...] = low
+
+
 def send_rows_of(latent, rows_ref, outs):
     particles = latent.shape[0]
     depth = rows_ref.shape[0]
     lanes = lax.broadcasted_iota(jnp.int32, (depth, particles), 1)
-    for z, out in enumerate(outs):
+    chosen = []
+    for z in range(3):
         picked = [
             jnp.where(rows_ref[:, d : d + 1] == lanes, 1.0, 0.0)
             for d in [x * 9 + y * 3 + z for x in range(3) for y in range(3)]
         ]
         picked = jnp.concatenate(picked, axis=0).astype(BF16)
-        out[...] = mm(picked, latent).astype(BF16)
+        chosen.append(mm(picked, latent).astype(BF16))
+    by_parity(chosen, outs)
 
 
 def split_direction(direction):
@@ -173,14 +192,14 @@
     return (latent.astype(F32) + update).astype(BF16)
 
 
-def round_kernel(r, latent_ref, g0, g1, g2, part_ref, column_ref, *refs):
+def round_kernel(r, latent_ref, g2, g1, g0, part_ref, column_ref, *refs):
     rows_ref, out_ref, low, mid, high = refs[6:]
     latent = updated_latent(r, latent_ref, (g0, g1, g2), part_ref, column_ref, refs[:6])
     out_ref[...] = latent
     send_rows_of(latent, rows_ref, (low, mid, high))
 
 
-def last_kernel(r, latent_ref, g0, g1, g2, part_ref, column_ref, *refs):
+def last_kernel(r, latent_ref, g2, g1, g0, part_ref, column_ref, *refs):
     kin_ref, dir_ref, slot_ref, dw1_ref, dw2_ref, stayed_ref, low, mid, high = refs[6:]
     latent = updated_latent(r, latent_ref, (g0, g1, g2), part_ref, column_ref, refs[:6])
     decoded = jnp.maximum(mm(latent, dw1_ref[...]), 0.0)
@@ -212,8 +231,7 @@
         preferred_element_type=F32,
     )
     step = 9 * MIG
-    for index, out in enumerate((low, mid, high)):
-        out[...] = outgoing[index * step : (index + 1) * step]
+    by_parity([outgoing[i * step : (i + 1) * step] for i in range(3)], (low, mid, high))
 
 
 def whole(shape):
@@ -272,10 +290,10 @@
     return lax.ppermute(value, axis, pairs)
 
 
-def moved_in_pairs(low, mid, high, axis):
+def moved_in_pairs(to_odd, mid, to_even, axis):
     even = lax.axis_index(axis) % 2 == 0
-    odd_pairs = swapped(jnp.where(even, low, high), axis, 1)
-    even_pairs = swapped(jnp.where(even, high, low), axis, 0)
+    odd_pairs = swapped(to_odd, axis, 1)
+    even_pairs = swapped(to_even, axis, 0)
     from_below = jnp.where(even, odd_pairs, even_pairs)
     from_above = jnp.where(even, even_pairs, odd_pairs)
     return [from_below, mid, from_above]
@@ -365,7 +383,7 @@
             moved=8 * slots * particles * width,
         )
         weights = [edge_w1, edge_w2, node_w1, node_w2]
-        args = [latent, *ghosts, part_sum, columns, *weights, edge_gain, node_gain]
+        args = [latent, *ghosts[::-1], part_sum, columns, *weights, edge_gain, node_gain]
         specs = [None] * 6 + [of_round(w) for w in weights] + [None, None]
         if r < rounds - 1:
             latent, low, mid, high = call(

time: 124 us -> 119 us (0.960)
  the two profiles are of different devices: /device:TPU:48 before, /device:TPU:240 now
where the time goes in v4:
time: 119 us; the launch traced here: 118 us
  starting transfers between devices  73.1 us (61%)
  Pallas kernels  21.1 us (18%)
  waiting for transfers between devices  18.1 us (15%)
  local copies, waits for them, and re-layouts  3.84 us (3%)
  between operations  1.54 us (1%)
    ppermute x16, starting transfers between devices, shifted(): lax.ppermute(value, axis, [(source, source + steps) for source in range(f...  52.9 us
    ppermute x8, starting transfers between devices, swapped(): return lax.ppermute(value, axis, pairs)  20.2 us
    ppermute x16, waiting for transfers between devices, shifted(): lax.ppermute(value, axis, [(source, source + steps) for source in range(f...  17.2 us
    pallas_call x6, Pallas kernels, call(): pl.pallas_call(body, grid=(1,), in_specs=[spec if spec is not None else w...  15.1 us
    pallas_call x2, Pallas kernels, call_fetching(): pl.pallas_call(functools.partial(fetching, body, len(args)), in_specs=[pl...  5.99 us
    unnamed x31, local copies, waits for them, and re-layouts  2.87 us
  transfers between devices with their start and end apart: 24, of which 8 were waited for; matrix products, arithmetic and copies ran while one was open for 1% of the time, Pallas kernels for 6%

profile of v4, /device:TPU:240, one launch (start us, length us, event | category | flops | bytes accessed | tf_op | source)
XLA Modules:
  0.0 117.9 jit_solution(149856498088073951)
XLA Ops:
  0.6 2.5 %node_encoder.1 = (bf16[256,128]{1,0:T(8,128)(2,1)}, bf16[144,128]{1,0:T(8,128)(2,1)}, bf16[144,128]{1,0:T(8,128)(2,1)}, bf16[144,128]{1,0:T(8,128)(2,1)}) custom-call(f32[18,256]{1,0:T(8,128)} %refs_6_.1, f32[15,128]{1,0:T(8,128)} %refs_1_.5, bf16[128,128]{1,0:T(8,128)(2,1)} %refs_2_.4, s32[16,27]{1,0:T(8,128)} %bitcast.31), custom_call_target="tpu_custom_call" | custom-call | tf_op jit(solution)/shard_map/node_encoder/pallas_call | solution.py:269
  3.9 4.8 %collective-permute-start.1 = (bf16[144,128]{1,0:T(8,128)(2,1)}, bf16[144,128]{1,0:T(8,128)(2,1)S(1)}, u32[]{:S(2)}, u32[]{:S(2)}) collective-permute-start(bf16[144,128]{1,0:T(8,128)(2,1)} %get-tuple-element.22), channel_id=1, source_target_pairs={{0,1},{1,0},{2,3},{3,2},{4,5},{5,4},{6,7},{7,6},{8,9},{9,8},{10,11... | collective-permute-start | bytes 110600 | tf_op jit(solution)/shard_map/ppermute | solution.py:290
  9.4 3.5 %edge_encoder.1 = (bf16[16,256,128]{2,1,0:T(8,128)(2,1)}, s32[256,128]{1,0:T(8,128)}) custom-call(f32[3,16,256]{2,1,0:T(8,128)} %refs_0_.6, s32[16,256]{1,0:T(8,128)} %refs_1_.6, s32[1,256]{1,0:T(1,128)} %bitcast.51, f32[4,128]{1,0:T(4,128)} %refs_3_.4, bf16[128,128]{1,0:T(8,128)(2,1)} %refs_4_.4), custom_call_target="tpu_custom_call" | custom-call | flops 805306368 | bytes 2097152 | tf_op jit(solution)/shard_map/edge_encoder/pallas_call | solution.py:269
  13.1 3.3 %collective-permute-start.3 = (bf16[144,128]{1,0:T(8,128)(2,1)S(1)}, bf16[144,128]{1,0:T(8,128)(2,1)S(1)}, u32[]{:S(2)}, u32[]{:S(2)}) collective-permute-start(bf16[144,128]{1,0:T(8,128)(2,1)S(1)} %pad_maximum_fusion.2), channel_id=1, source_target_pairs={{64,0},{128,64},{192,128},{256,192},{320,256},{384,320},{448,384},... | collective-permute-start | bytes 110600 | tf_op jit(solution)/shard_map/ppermute | solution.py:22
  16.4 2.6 %collective-permute-start.2 = (bf16[144,128]{1,0:T(8,128)(2,1)S(1)}, bf16[144,128]{1,0:T(8,128)(2,1)S(1)}, u32[]{:S(2)}, u32[]{:S(2)}) collective-permute-start(bf16[144,128]{1,0:T(8,128)(2,1)S(1)} %pad_maximum_fusion), channel_id=1, source_target_pairs={{0,64},{64,128},{128,192},{192,256},{256,320},{320,384},{384,448},... | collective-permute-start | bytes 110600 | tf_op jit(solution)/shard_map/ppermute | solution.py:22
  24.3 5.5 %collective-permute-start.5 = (bf16[144,128]{1,0:T(8,128)(2,1)S(1)}, bf16[144,128]{1,0:T(8,128)(2,1)S(1)}, u32[]{:S(2)}, u32[]{:S(2)}) collective-permute-start(bf16[144,128]{1,0:T(8,128)(2,1)S(1)} %bitcast.46), channel_id=1, source_target_pairs={{0,8},{8,16},{16,24},{24,32},{32,40},{40,48},{48,56},{1,9},{9,17},... | collective-permute-start | bytes 110600 | tf_op jit(solution)/shard_map/ppermute | solution.py:22
  31.4 3.5 %message_round.2 = (bf16[256,128]{1,0:T(8,128)(2,1)S(1)}, bf16[144,128]{1,0:T(8,128)(2,1)S(1)}, bf16[144,128]{1,0:T(8,128)(2,1)S(1)}, bf16[144,128]{1,0:T(8,128)(2,1)S(1)}) custom-call(bf16[256,128]{1,0:T(8,128)(2,1)S(1)} %copy-done.7, bf16[144,128]{1,0:T(8,128)(2,1)S(1)} %collective-permute-done.4.g2, bf16[144,128]{1,0:T(8,128)(2,1)S(1)} %bitcast.29, ...), custom_call_target="tpu_custom_call" | custom-call | tf_op jit(solution)/shard_map/message_round/pallas_call | solution.py:242
  35.6 4.8 %collective-permute-start.7 = (bf16[144,128]{1,0:T(8,128)(2,1)S(1)}, bf16[144,128]{1,0:T(8,128)(2,1)S(1)}, u32[]{:S(2)}, u32[]{:S(2)}) collective-permute-start(bf16[144,128]{1,0:T(8,128)(2,1)S(1)} %get-tuple-element.28), channel_id=1, source_target_pairs={{0,1},{1,0},{2,3},{3,2},{4,5},{5,4},{6,7},{7,6},{8,9},{9,8},{10,11... | collective-permute-start | bytes 110600 | tf_op jit(solution)/shard_map/ppermute | solution.py:290
  41.6 3.3 %collective-permute-start.9 = (bf16[144,128]{1,0:T(8,128)(2,1)S(1)}, bf16[144,128]{1,0:T(8,128)(2,1)S(1)}, u32[]{:S(2)}, u32[]{:S(2)}) collective-permute-start(bf16[144,128]{1,0:T(8,128)(2,1)S(1)} %pad_maximum_fusion.8), channel_id=1, source_target_pairs={{64,0},{128,64},{192,128},{256,192},{320,256},{384,320},{448,384},... | collective-permute-start | bytes 110600 | tf_op jit(solution)/shard_map/ppermute | solution.py:22
  44.9 2.6 %collective-permute-start.8 = (bf16[144,128]{1,0:T(8,128)(2,1)S(1)}, bf16[144,128]{1,0:T(8,128)(2,1)S(1)}, u32[]{:S(2)}, u32[]{:S(2)}) collective-permute-start(bf16[144,128]{1,0:T(8,128)(2,1)S(1)} %pad_maximum_fusion.6), channel_id=1, source_target_pairs={{0,64},{64,128},{128,192},{192,256},{256,320},{320,384},{384,448},... | collective-permute-start | bytes 110600 | tf_op jit(solution)/shard_map/ppermute | solution.py:22
  47.5 3.2 %collective-permute-done.8 = bf16[144,128]{1,0:T(8,128)(2,1)S(1)} collective-permute-done((bf16[144,128]{1,0:T(8,128)(2,1)S(1)}, bf16[144,128]{1,0:T(8,128)(2,1)S(1)}, u32[]{:S(2)}, u32[]{:S(2)}) %collective-permute-start.8) | collective-permute-done | bytes 36896 | tf_op jit(solution)/shard_map/ppermute | solution.py:22
  52.7 5.4 %collective-permute-start.11 = (bf16[144,128]{1,0:T(8,128)(2,1)S(1)}, bf16[144,128]{1,0:T(8,128)(2,1)S(1)}, u32[]{:S(2)}, u32[]{:S(2)}) collective-permute-start(bf16[144,128]{1,0:T(8,128)(2,1)S(1)} %bitcast.47), channel_id=1, source_target_pairs={{0,8},{8,16},{16,24},{24,32},{32,40},{40,48},{48,56},{1,9},{9,17},... | collective-permute-start | bytes 110600 | tf_op jit(solution)/shard_map/ppermute | solution.py:22
  59.8 3.7 %message_round.3 = (bf16[256,128]{1,0:T(8,128)(2,1)S(1)}, bf16[144,128]{1,0:T(8,128)(2,1)S(1)}, bf16[144,128]{1,0:T(8,128)(2,1)S(1)}, bf16[144,128]{1,0:T(8,128)(2,1)S(1)}) custom-call(bf16[256,128]{1,0:T(8,128)(2,1)S(1)} %get-tuple-element.26.latent_ref, bf16[144,128]{1,0:T(8,128)(2,1)S(1)} %collective-permute-done.10.g2, bf16[144,128]{1,0:T(8,128)(2,1)S(1)} %bitcast.30, ...), custom_call_target="tpu_custom_call" | custom-call | tf_op jit(solution)/shard_map/message_round/pallas_call | solution.py:242
  64.1 4.5 %collective-permute-start.13 = (bf16[144,128]{1,0:T(8,128)(2,1)S(1)}, bf16[144,128]{1,0:T(8,128)(2,1)S(1)}, u32[]{:S(2)}, u32[]{:S(2)}) collective-permute-start(bf16[144,128]{1,0:T(8,128)(2,1)S(1)} %get-tuple-element.32), channel_id=1, source_target_pairs={{0,1},{1,0},{2,3},{3,2},{4,5},{5,4},{6,7},{7,6},{8,9},{9,8},{10,11... | collective-permute-start | bytes 110600 | tf_op jit(solution)/shard_map/ppermute | solution.py:290
  69.9 3.5 %collective-permute-start.15 = (bf16[144,128]{1,0:T(8,128)(2,1)S(1)}, bf16[144,128]{1,0:T(8,128)(2,1)S(1)}, u32[]{:S(2)}, u32[]{:S(2)}) collective-permute-start(bf16[144,128]{1,0:T(8,128)(2,1)S(1)} %pad_maximum_fusion.14), channel_id=1, source_target_pairs={{64,0},{128,64},{192,128},{256,192},{320,256},{384,320},{448,384},... | collective-permute-start | bytes 110600 | tf_op jit(solution)/shard_map/ppermute | solution.py:22
  73.4 2.4 %collective-permute-start.14 = (bf16[144,128]{1,0:T(8,128)(2,1)S(1)}, bf16[144,128]{1,0:T(8,128)(2,1)S(1)}, u32[]{:S(2)}, u32[]{:S(2)}) collective-permute-start(bf16[144,128]{1,0:T(8,128)(2,1)S(1)} %pad_maximum_fusion.12), channel_id=1, source_target_pairs={{0,64},{64,128},{128,192},{192,256},{256,320},{320,384},{384,448},... | collective-permute-start | bytes 110600 | tf_op jit(solution)/shard_map/ppermute | solution.py:22
  75.8 4.1 %collective-permute-done.14 = bf16[144,128]{1,0:T(8,128)(2,1)S(1)} collective-permute-done((bf16[144,128]{1,0:T(8,128)(2,1)S(1)}, bf16[144,128]{1,0:T(8,128)(2,1)S(1)}, u32[]{:S(2)}, u32[]{:S(2)}) %collective-permute-start.14) | collective-permute-done | bytes 36896 | tf_op jit(solution)/shard_map/ppermute | solution.py:22
  81.9 5.4 %collective-permute-start.17 = (bf16[144,128]{1,0:T(8,128)(2,1)S(1)}, bf16[144,128]{1,0:T(8,128)(2,1)S(1)}, u32[]{:S(2)}, u32[]{:S(2)}) collective-permute-start(bf16[144,128]{1,0:T(8,128)(2,1)S(1)} %bitcast.48), channel_id=1, source_target_pairs={{0,8},{8,16},{16,24},{24,32},{32,40},{40,48},{48,56},{1,9},{9,17},... | collective-permute-start | bytes 110600 | tf_op jit(solution)/shard_map/ppermute | solution.py:22
  88.9 4.6 %last_round.1 = (f32[18,256]{1,0:T(8,128)}, f32[36,18]{1,0:T(8,128)S(1)}, f32[36,18]{1,0:T(8,128)S(1)}, f32[36,18]{1,0:T(8,128)S(1)}) custom-call(bf16[256,128]{1,0:T(8,128)(2,1)S(1)} %get-tuple-element.30.latent_ref, bf16[144,128]{1,0:T(8,128)(2,1)S(1)} %collective-permute-done.16.g2, bf16[144,128]{1,0:T(8,128)(2,1)S(1)} %bitcast.28, ...), custom_call_target="tpu_custom_call" | custom-call | tf_op jit(solution)/shard_map/last_round/pallas_call | solution.py:242
  94.2 3.4 %collective-permute-start.19 = (f32[36,18]{1,0:T(8,128)S(1)}, f32[36,18]{1,0:T(8,128)S(1)}, u32[]{:S(2)}, u32[]{:S(2)}) collective-permute-start(f32[36,18]{1,0:T(8,128)S(1)} %get-tuple-element.36), channel_id=1, source_target_pairs={{0,1},{1,0},{2,3},{3,2},{4,5},{5,4},{6,7},{7,6},{8,9},{9,8},{10,11... | collective-permute-start | bytes 7784 | tf_op jit(solution)/shard_map/ppermute | solution.py:290
  98.6 3.9 %collective-permute-start.21 = (f32[36,18]{1,0:T(8,128)S(1)}, f32[36,18]{1,0:T(8,128)S(1)}, u32[]{:S(2)}, u32[]{:S(2)}) collective-permute-start(f32[36,18]{1,0:T(8,128)S(1)} %pad_maximum_fusion.20), channel_id=1, source_target_pairs={{64,0},{128,64},{192,128},{256,192},{320,256},{384,320},{448,384},... | collective-permute-start | bytes 7784 | tf_op jit(solution)/shard_map/ppermute | solution.py:22
  104.5 3.7 %collective-permute-done.20 = f32[36,18]{1,0:T(8,128)S(1)} collective-permute-done((f32[36,18]{1,0:T(8,128)S(1)}, f32[36,18]{1,0:T(8,128)S(1)}, u32[]{:S(2)}, u32[]{:S(2)}) %collective-permute-start.20) | collective-permute-done | bytes 2624 | tf_op jit(solution)/shard_map/ppermute | solution.py:22
  108.3 1.9 %collective-permute-start.23 = (f32[36,18]{1,0:T(8,128)S(1)}, f32[36,18]{1,0:T(8,128)S(1)}, u32[]{:S(2)}, u32[]{:S(2)}) collective-permute-start(f32[36,18]{1,0:T(8,128)S(1)} %reshape.201), channel_id=1, source_target_pairs={{8,0},{16,8},{24,16},{32,24},{40,32},{48,40},{56,48},{9,1},{17,9},... | collective-permute-start | bytes 7784 | tf_op jit(solution)/shard_map/ppermute | solution.py:22
  110.2 5.4 %collective-permute-start.22 = (f32[36,18]{1,0:T(8,128)S(1)}, f32[36,18]{1,0:T(8,128)S(1)}, u32[]{:S(2)}, u32[]{:S(2)}) collective-permute-start(f32[36,18]{1,0:T(8,128)S(1)} %reshape.200), channel_id=1, source_target_pairs={{0,8},{8,16},{16,24},{24,32},{32,40},{40,48},{48,56},{1,9},{9,17},... | collective-permute-start | bytes 7784 | tf_op jit(solution)/shard_map/ppermute | solution.py:22
  (124 shorter events, 24.9 us)
Async XLA Ops:
  3.1 9.9 %collective-permute-start = (bf16[144,128]{1,0:T(8,128)(2,1)}, bf16[144,128]{1,0:T(8,128)(2,1)S(1)}, u32[]{:S(2)}, u32[]{:S(2)}) collective-permute-start(bf16[144,128]{1,0:T(8,128)(2,1)} %get-tuple-element.21), channel_id=1, source_target_pairs={{1,2},{2,1},{3,4},{4,3},{5,6},{6,5},{9,10},{10,9},{11,12},{12,11},... | collective-permute-start | bytes 110600 | tf_op jit(solution)/shard_map/ppermute | solution.py:290
  3.9 9.1 %collective-permute-start.1 = (bf16[144,128]{1,0:T(8,128)(2,1)}, bf16[144,128]{1,0:T(8,128)(2,1)S(1)}, u32[]{:S(2)}, u32[]{:S(2)}) collective-permute-start(bf16[144,128]{1,0:T(8,128)(2,1)} %get-tuple-element.22), channel_id=1, source_target_pairs={{0,1},{1,0},{2,3},{3,2},{4,5},{5,4},{6,7},{7,6},{8,9},{9,8},{10,11... | collective-permute-start | bytes 110600 | tf_op jit(solution)/shard_map/ppermute | solution.py:290
  13.1 9.2 %collective-permute-start.3 = (bf16[144,128]{1,0:T(8,128)(2,1)S(1)}, bf16[144,128]{1,0:T(8,128)(2,1)S(1)}, u32[]{:S(2)}, u32[]{:S(2)}) collective-permute-start(bf16[144,128]{1,0:T(8,128)(2,1)S(1)} %pad_maximum_fusion.2), channel_id=1, source_target_pairs={{64,0},{128,64},{192,128},{256,192},{320,256},{384,320},{448,384},... | collective-permute-start | bytes 110600 | tf_op jit(solution)/shard_map/ppermute | solution.py:22
  16.4 5.9 %collective-permute-start.2 = (bf16[144,128]{1,0:T(8,128)(2,1)S(1)}, bf16[144,128]{1,0:T(8,128)(2,1)S(1)}, u32[]{:S(2)}, u32[]{:S(2)}) collective-permute-start(bf16[144,128]{1,0:T(8,128)(2,1)S(1)} %pad_maximum_fusion), channel_id=1, source_target_pairs={{0,64},{64,128},{128,192},{192,256},{256,320},{320,384},{384,448},... | collective-permute-start | bytes 110600 | tf_op jit(solution)/shard_map/ppermute | solution.py:22
  22.3 7.5 %collective-permute-start.4 = (bf16[144,128]{1,0:T(8,128)(2,1)S(1)}, bf16[144,128]{1,0:T(8,128)(2,1)S(1)}, u32[]{:S(2)}, u32[]{:S(2)}) collective-permute-start(bf16[144,128]{1,0:T(8,128)(2,1)S(1)} %bitcast.40), channel_id=1, source_target_pairs={{8,0},{16,8},{24,16},{32,24},{40,32},{48,40},{56,48},{9,1},{17,9},... | collective-permute-start | bytes 110600 | tf_op jit(solution)/shard_map/ppermute | solution.py:22
  24.3 7.1 %collective-permute-start.5 = (bf16[144,128]{1,0:T(8,128)(2,1)S(1)}, bf16[144,128]{1,0:T(8,128)(2,1)S(1)}, u32[]{:S(2)}, u32[]{:S(2)}) collective-permute-start(bf16[144,128]{1,0:T(8,128)(2,1)S(1)} %bitcast.46), channel_id=1, source_target_pairs={{0,8},{8,16},{16,24},{24,32},{32,40},{40,48},{48,56},{1,9},{9,17},... | collective-permute-start | bytes 110600 | tf_op jit(solution)/shard_map/ppermute | solution.py:22
  34.9 6.6 %collective-permute-start.6 = (bf16[144,128]{1,0:T(8,128)(2,1)S(1)}, bf16[144,128]{1,0:T(8,128)(2,1)S(1)}, u32[]{:S(2)}, u32[]{:S(2)}) collective-permute-start(bf16[144,128]{1,0:T(8,128)(2,1)S(1)} %get-tuple-element.27), channel_id=1, source_target_pairs={{1,2},{2,1},{3,4},{4,3},{5,6},{6,5},{9,10},{10,9},{11,12},{12,11},... | collective-permute-start | bytes 110600 | tf_op jit(solution)/shard_map/ppermute | solution.py:290
  35.6 5.9 %collective-permute-start.7 = (bf16[144,128]{1,0:T(8,128)(2,1)S(1)}, bf16[144,128]{1,0:T(8,128)(2,1)S(1)}, u32[]{:S(2)}, u32[]{:S(2)}) collective-permute-start(bf16[144,128]{1,0:T(8,128)(2,1)S(1)} %get-tuple-element.28), channel_id=1, source_target_pairs={{0,1},{1,0},{2,3},{3,2},{4,5},{5,4},{6,7},{7,6},{8,9},{9,8},{10,11... | collective-permute-start | bytes 110600 | tf_op jit(solution)/shard_map/ppermute | solution.py:290
  41.6 5.9 %collective-permute-start.9 = (bf16[144,128]{1,0:T(8,128)(2,1)S(1)}, bf16[144,128]{1,0:T(8,128)(2,1)S(1)}, u32[]{:S(2)}, u32[]{:S(2)}) collective-permute-start(bf16[144,128]{1,0:T(8,128)(2,1)S(1)} %pad_maximum_fusion.8), channel_id=1, source_target_pairs={{64,0},{128,64},{192,128},{256,192},{320,256},{384,320},{448,384},... | collective-permute-start | bytes 110600 | tf_op jit(solution)/shard_map/ppermute | solution.py:22
  44.9 5.9 %collective-permute-start.8 = (bf16[144,128]{1,0:T(8,128)(2,1)S(1)}, bf16[144,128]{1,0:T(8,128)(2,1)S(1)}, u32[]{:S(2)}, u32[]{:S(2)}) collective-permute-start(bf16[144,128]{1,0:T(8,128)(2,1)S(1)} %pad_maximum_fusion.6), channel_id=1, source_target_pairs={{0,64},{64,128},{128,192},{192,256},{256,320},{320,384},{384,448},... | collective-permute-start | bytes 110600 | tf_op jit(solution)/shard_map/ppermute | solution.py:22
  50.8 7.4 %collective-permute-start.10 = (bf16[144,128]{1,0:T(8,128)(2,1)S(1)}, bf16[144,128]{1,0:T(8,128)(2,1)S(1)}, u32[]{:S(2)}, u32[]{:S(2)}) collective-permute-start(bf16[144,128]{1,0:T(8,128)(2,1)S(1)} %bitcast.41), channel_id=1, source_target_pairs={{8,0},{16,8},{24,16},{32,24},{40,32},{48,40},{56,48},{9,1},{17,9},... | collective-permute-start | bytes 110600 | tf_op jit(solution)/shard_map/ppermute | solution.py:22
  52.7 7.1 %collective-permute-start.11 = (bf16[144,128]{1,0:T(8,128)(2,1)S(1)}, bf16[144,128]{1,0:T(8,128)(2,1)S(1)}, u32[]{:S(2)}, u32[]{:S(2)}) collective-permute-start(bf16[144,128]{1,0:T(8,128)(2,1)S(1)} %bitcast.47), channel_id=1, source_target_pairs={{0,8},{8,16},{16,24},{24,32},{32,40},{40,48},{48,56},{1,9},{9,17},... | collective-permute-start | bytes 110600 | tf_op jit(solution)/shard_map/ppermute | solution.py:22
  63.5 6.3 %collective-permute-start.12 = (bf16[144,128]{1,0:T(8,128)(2,1)S(1)}, bf16[144,128]{1,0:T(8,128)(2,1)S(1)}, u32[]{:S(2)}, u32[]{:S(2)}) collective-permute-start(bf16[144,128]{1,0:T(8,128)(2,1)S(1)} %get-tuple-element.31), channel_id=1, source_target_pairs={{1,2},{2,1},{3,4},{4,3},{5,6},{6,5},{9,10},{10,9},{11,12},{12,11},... | collective-permute-start | bytes 110600 | tf_op jit(solution)/shard_map/ppermute | solution.py:290
  64.1 5.7 %collective-permute-start.13 = (bf16[144,128]{1,0:T(8,128)(2,1)S(1)}, bf16[144,128]{1,0:T(8,128)(2,1)S(1)}, u32[]{:S(2)}, u32[]{:S(2)}) collective-permute-start(bf16[144,128]{1,0:T(8,128)(2,1)S(1)} %get-tuple-element.32), channel_id=1, source_target_pairs={{0,1},{1,0},{2,3},{3,2},{4,5},{5,4},{6,7},{7,6},{8,9},{9,8},{10,11... | collective-permute-start | bytes 110600 | tf_op jit(solution)/shard_map/ppermute | solution.py:290
  69.9 5.9 %collective-permute-start.15 = (bf16[144,128]{1,0:T(8,128)(2,1)S(1)}, bf16[144,128]{1,0:T(8,128)(2,1)S(1)}, u32[]{:S(2)}, u32[]{:S(2)}) collective-permute-start(bf16[144,128]{1,0:T(8,128)(2,1)S(1)} %pad_maximum_fusion.14), channel_id=1, source_target_pairs={{64,0},{128,64},{192,128},{256,192},{320,256},{384,320},{448,384},... | collective-permute-start | bytes 110600 | tf_op jit(solution)/shard_map/ppermute | solution.py:22
  73.4 6.5 %collective-permute-start.14 = (bf16[144,128]{1,0:T(8,128)(2,1)S(1)}, bf16[144,128]{1,0:T(8,128)(2,1)S(1)}, u32[]{:S(2)}, u32[]{:S(2)}) collective-permute-start(bf16[144,128]{1,0:T(8,128)(2,1)S(1)} %pad_maximum_fusion.12), channel_id=1, source_target_pairs={{0,64},{64,128},{128,192},{192,256},{256,320},{320,384},{384,448},... | collective-permute-start | bytes 110600 | tf_op jit(solution)/shard_map/ppermute | solution.py:22
  79.9 7.4 %collective-permute-start.16 = (bf16[144,128]{1,0:T(8,128)(2,1)S(1)}, bf16[144,128]{1,0:T(8,128)(2,1)S(1)}, u32[]{:S(2)}, u32[]{:S(2)}) collective-permute-start(bf16[144,128]{1,0:T(8,128)(2,1)S(1)} %bitcast.42), channel_id=1, source_target_pairs={{8,0},{16,8},{24,16},{32,24},{40,32},{48,40},{56,48},{9,1},{17,9},... | collective-permute-start | bytes 110600 | tf_op jit(solution)/shard_map/ppermute | solution.py:22
  81.9 7.1 %collective-permute-start.17 = (bf16[144,128]{1,0:T(8,128)(2,1)S(1)}, bf16[144,128]{1,0:T(8,128)(2,1)S(1)}, u32[]{:S(2)}, u32[]{:S(2)}) collective-permute-start(bf16[144,128]{1,0:T(8,128)(2,1)S(1)} %bitcast.48), channel_id=1, source_target_pairs={{0,8},{8,16},{16,24},{24,32},{32,40},{40,48},{48,56},{1,9},{9,17},... | collective-permute-start | bytes 110600 | tf_op jit(solution)/shard_map/ppermute | solution.py:22
  93.5 4.1 %collective-permute-start.18 = (f32[36,18]{1,0:T(8,128)S(1)}, f32[36,18]{1,0:T(8,128)S(1)}, u32[]{:S(2)}, u32[]{:S(2)}) collective-permute-start(f32[36,18]{1,0:T(8,128)S(1)} %get-tuple-element.35), channel_id=1, source_target_pairs={{1,2},{2,1},{3,4},{4,3},{5,6},{6,5},{9,10},{10,9},{11,12},{12,11},... | collective-permute-start | bytes 7784 | tf_op jit(solution)/shard_map/ppermute | solution.py:290
  94.2 4.3 %collective-permute-start.19 = (f32[36,18]{1,0:T(8,128)S(1)}, f32[36,18]{1,0:T(8,128)S(1)}, u32[]{:S(2)}, u32[]{:S(2)}) collective-permute-start(f32[36,18]{1,0:T(8,128)S(1)} %get-tuple-element.36), channel_id=1, source_target_pairs={{0,1},{1,0},{2,3},{3,2},{4,5},{5,4},{6,7},{7,6},{8,9},{9,8},{10,11... | collective-permute-start | bytes 7784 | tf_op jit(solution)/shard_map/ppermute | solution.py:290
  98.6 5.9 %collective-permute-start.21 = (f32[36,18]{1,0:T(8,128)S(1)}, f32[36,18]{1,0:T(8,128)S(1)}, u32[]{:S(2)}, u32[]{:S(2)}) collective-permute-start(f32[36,18]{1,0:T(8,128)S(1)} %pad_maximum_fusion.20), channel_id=1, source_target_pairs={{64,0},{128,64},{192,128},{256,192},{320,256},{384,320},{448,384},... | collective-permute-start | bytes 7784 | tf_op jit(solution)/shard_map/ppermute | solution.py:22
  102.5 5.7 %collective-permute-start.20 = (f32[36,18]{1,0:T(8,128)S(1)}, f32[36,18]{1,0:T(8,128)S(1)}, u32[]{:S(2)}, u32[]{:S(2)}) collective-permute-start(f32[36,18]{1,0:T(8,128)S(1)} %pad_maximum_fusion.18), channel_id=1, source_target_pairs={{0,64},{64,128},{128,192},{192,256},{256,320},{320,384},{384,448},... | collective-permute-start | bytes 7784 | tf_op jit(solution)/shard_map/ppermute | solution.py:22
  108.3 7.4 %collective-permute-start.23 = (f32[36,18]{1,0:T(8,128)S(1)}, f32[36,18]{1,0:T(8,128)S(1)}, u32[]{:S(2)}, u32[]{:S(2)}) collective-permute-start(f32[36,18]{1,0:T(8,128)S(1)} %reshape.201), channel_id=1, source_target_pairs={{8,0},{16,8},{24,16},{32,24},{40,32},{48,40},{56,48},{9,1},{17,9},... | collective-permute-start | bytes 7784 | tf_op jit(solution)/shard_map/ppermute | solution.py:22
  110.2 6.9 %collective-permute-start.22 = (f32[36,18]{1,0:T(8,128)S(1)}, f32[36,18]{1,0:T(8,128)S(1)}, u32[]{:S(2)}, u32[]{:S(2)}) collective-permute-start(f32[36,18]{1,0:T(8,128)S(1)} %reshape.200), channel_id=1, source_target_pairs={{0,8},{8,16},{16,24},{24,32},{32,40},{40,48},{48,56},{1,9},{9,17},... | collective-permute-start | bytes 7784 | tf_op jit(solution)/shard_map/ppermute | solution.py:22
  (15 other events, 199.5 us)

commit v5 on v4

--- a/solution.py
+++ b/solution.py
@@ -8,7 +8,7 @@
 from jax.sharding import PartitionSpec as P
 
 MIG = 4
-BLOCK = 8
+BLOCK = 16
 EPS = 1e-05
 F32 = jnp.float32
 BF16 = jnp.bfloat16
@@ -309,12 +309,13 @@
     hold = parts[0]
     parts = [part.reshape(3, 3 * rows, tail) for part in parts]
     parts = moved(*(jnp.concatenate([part[x] for part in parts], axis=0) for x in range(3)), "gx")
+    held = (hold, parts[0])
     parts = [part.reshape(3, 3, rows, tail) for part in parts]
     low, mid, high = (
         jnp.stack([part[:, y] for part in parts], axis=1).reshape(9 * rows, tail)
         for y in range(3)
     )
-    return moved(low, mid, high, "gy"), hold
+    return moved(low, mid, high, "gy"), held
 
 
 def on_device(
@@ -367,12 +368,12 @@
     )
     leaving = [migrate_dir.reshape(1, particles), migrate_slot.reshape(1, particles)]
     for r in range(rounds):
-        ghosts, hold = exchanged(low, mid, high, ghost_rows)
+        ghosts, held = exchanged(low, mid, high, ghost_rows)
 
         def of_round(array):
             return pl.BlockSpec((1,) + array.shape[1:], lambda i: (r, 0, 0))
 
-        held = (hold,) if r == 0 else ()
+        held = (held[min(r, 1)],)
         (part_sum,) = call(
             local_kernel,
             (latent, edges, columns, edge_w1) + held,

time: 119 us -> 117 us (0.983)
  Pallas kernels: 21.1 us -> 19.7 us
    ppermute x16, waiting for transfers between devices: 17.2 us -> 14.8 us  [shifted(): lax.ppermute(value, axis, [(source, source + steps) for source in range(f...]
    ppermute x8, waiting for transfers between devices: 0.82 us -> 2.45 us  [swapped(): return lax.ppermute(value, axis, pairs)]
    pallas_call x6, Pallas kernels: 15.1 us -> 13.8 us  [call(): pl.pallas_call(body, grid=(1,), in_specs=[spec if spec is not None else w...]
  transfers between devices with their start and end apart: 24 -> 24, of which waited for: 8 -> 10; matrix products, arithmetic and copies ran while one was open for 1% -> 1% of each run, Pallas kernels for 6% -> 6%
where the time goes in v5:
time: 117 us; the launch traced here: 116 us
  starting transfers between devices  73.7 us (63%)
  Pallas kernels  19.7 us (17%)
  waiting for transfers between devices  17.2 us (15%)
  local copies, waits for them, and re-layouts  3.84 us (3%)
  between operations  1.52 us (1%)
    ppermute x16, starting transfers between devices, shifted(): lax.ppermute(value, axis, [(source, source + steps) for source in range(f...  53.2 us
    ppermute x8, starting transfers between devices, swapped(): return lax.ppermute(value, axis, pairs)  20.5 us
    ppermute x16, waiting for transfers between devices, shifted(): lax.ppermute(value, axis, [(source, source + steps) for source in range(f...  14.8 us
    pallas_call x6, Pallas kernels, call(): pl.pallas_call(body, grid=(1,), in_specs=[spec if spec is not None else w...  13.8 us
    pallas_call x2, Pallas kernels, call_fetching(): pl.pallas_call(functools.partial(fetching, body, len(args)), in_specs=[pl...  5.99 us
    unnamed x31, local copies, waits for them, and re-layouts  2.87 us
    ppermute x8, waiting for transfers between devices, swapped(): return lax.ppermute(value, axis, pairs)  2.45 us
  transfers between devices with their start and end apart: 24, of which 10 were waited for; matrix products, arithmetic and copies ran while one was open for 1% of the time, Pallas kernels for 6%

profile of v5, /device:TPU:240, one launch (start us, length us, event | category | flops | bytes accessed | tf_op | source)
XLA Modules:
  0.0 116.2 jit_solution(17279167499188851756)
XLA Ops:
  0.6 2.5 %node_encoder.1 = (bf16[256,128]{1,0:T(8,128)(2,1)}, bf16[144,128]{1,0:T(8,128)(2,1)}, bf16[144,128]{1,0:T(8,128)(2,1)}, bf16[144,128]{1,0:T(8,128)(2,1)}) custom-call(f32[18,256]{1,0:T(8,128)} %refs_6_.1, f32[15,128]{1,0:T(8,128)} %refs_1_.5, bf16[128,128]{1,0:T(8,128)(2,1)} %refs_2_.4, s32[16,27]{1,0:T(8,128)} %bitcast.31), custom_call_target="tpu_custom_call" | custom-call | tf_op jit(solution)/shard_map/node_encoder/pallas_call | solution.py:269
  3.9 4.8 %collective-permute-start.1 = (bf16[144,128]{1,0:T(8,128)(2,1)}, bf16[144,128]{1,0:T(8,128)(2,1)S(1)}, u32[]{:S(2)}, u32[]{:S(2)}) collective-permute-start(bf16[144,128]{1,0:T(8,128)(2,1)} %get-tuple-element.22), channel_id=1, source_target_pairs={{0,1},{1,0},{2,3},{3,2},{4,5},{5,4},{6,7},{7,6},{8,9},{9,8},{10,11... | collective-permute-start | bytes 110600 | tf_op jit(solution)/shard_map/ppermute | solution.py:290
  9.4 3.5 %edge_encoder.1 = (bf16[16,256,128]{2,1,0:T(8,128)(2,1)}, s32[256,128]{1,0:T(8,128)}) custom-call(f32[3,16,256]{2,1,0:T(8,128)} %refs_0_.6, s32[16,256]{1,0:T(8,128)} %refs_1_.6, s32[1,256]{1,0:T(1,128)} %bitcast.51, f32[4,128]{1,0:T(4,128)} %refs_3_.4, bf16[128,128]{1,0:T(8,128)(2,1)} %refs_4_.4), custom_call_target="tpu_custom_call" | custom-call | flops 805306368 | bytes 2097152 | tf_op jit(solution)/shard_map/edge_encoder/pallas_call | solution.py:269
  13.1 3.3 %collective-permute-start.3 = (bf16[144,128]{1,0:T(8,128)(2,1)S(1)}, bf16[144,128]{1,0:T(8,128)(2,1)S(1)}, u32[]{:S(2)}, u32[]{:S(2)}) collective-permute-start(bf16[144,128]{1,0:T(8,128)(2,1)S(1)} %pad_maximum_fusion.2), channel_id=1, source_target_pairs={{64,0},{128,64},{192,128},{256,192},{320,256},{384,320},{448,384},... | collective-permute-start | bytes 110600 | tf_op jit(solution)/shard_map/ppermute | solution.py:22
  16.4 2.6 %collective-permute-start.2 = (bf16[144,128]{1,0:T(8,128)(2,1)S(1)}, bf16[144,128]{1,0:T(8,128)(2,1)S(1)}, u32[]{:S(2)}, u32[]{:S(2)}) collective-permute-start(bf16[144,128]{1,0:T(8,128)(2,1)S(1)} %pad_maximum_fusion), channel_id=1, source_target_pairs={{0,64},{64,128},{128,192},{192,256},{256,320},{320,384},{384,448},... | collective-permute-start | bytes 110600 | tf_op jit(solution)/shard_map/ppermute | solution.py:22
  24.3 5.5 %collective-permute-start.5 = (bf16[144,128]{1,0:T(8,128)(2,1)S(1)}, bf16[144,128]{1,0:T(8,128)(2,1)S(1)}, u32[]{:S(2)}, u32[]{:S(2)}) collective-permute-start(bf16[144,128]{1,0:T(8,128)(2,1)S(1)} %bitcast.50), channel_id=1, source_target_pairs={{0,8},{8,16},{16,24},{24,32},{32,40},{40,48},{48,56},{1,9},{9,17},... | collective-permute-start | bytes 110600 | tf_op jit(solution)/shard_map/ppermute | solution.py:22
  31.4 3.0 %message_round.2 = (bf16[256,128]{1,0:T(8,128)(2,1)S(1)}, bf16[144,128]{1,0:T(8,128)(2,1)S(1)}, bf16[144,128]{1,0:T(8,128)(2,1)S(1)}, bf16[144,128]{1,0:T(8,128)(2,1)S(1)}) custom-call(bf16[256,128]{1,0:T(8,128)(2,1)S(1)} %copy-done.7, bf16[144,128]{1,0:T(8,128)(2,1)S(1)} %collective-permute-done.4.g2, bf16[144,128]{1,0:T(8,128)(2,1)S(1)} %bitcast.30, ...), custom_call_target="tpu_custom_call" | custom-call | tf_op jit(solution)/shard_map/message_round/pallas_call | solution.py:242
  35.2 4.8 %collective-permute-start.7 = (bf16[144,128]{1,0:T(8,128)(2,1)S(1)}, bf16[144,128]{1,0:T(8,128)(2,1)S(1)}, u32[]{:S(2)}, u32[]{:S(2)}) collective-permute-start(bf16[144,128]{1,0:T(8,128)(2,1)S(1)} %get-tuple-element.28), channel_id=1, source_target_pairs={{0,1},{1,0},{2,3},{3,2},{4,5},{5,4},{6,7},{7,6},{8,9},{9,8},{10,11... | collective-permute-start | bytes 110600 | tf_op jit(solution)/shard_map/ppermute | solution.py:290
  40.8 3.3 %collective-permute-start.9 = (bf16[144,128]{1,0:T(8,128)(2,1)S(1)}, bf16[144,128]{1,0:T(8,128)(2,1)S(1)}, u32[]{:S(2)}, u32[]{:S(2)}) collective-permute-start(bf16[144,128]{1,0:T(8,128)(2,1)S(1)} %pad_maximum_fusion.8), channel_id=1, source_target_pairs={{64,0},{128,64},{192,128},{256,192},{320,256},{384,320},{448,384},... | collective-permute-start | bytes 110600 | tf_op jit(solution)/shard_map/ppermute | solution.py:22
  44.1 2.6 %collective-permute-start.8 = (bf16[144,128]{1,0:T(8,128)(2,1)S(1)}, bf16[144,128]{1,0:T(8,128)(2,1)S(1)}, u32[]{:S(2)}, u32[]{:S(2)}) collective-permute-start(bf16[144,128]{1,0:T(8,128)(2,1)S(1)} %pad_maximum_fusion.6), channel_id=1, source_target_pairs={{0,64},{64,128},{128,192},{192,256},{256,320},{320,384},{384,448},... | collective-permute-start | bytes 110600 | tf_op jit(solution)/shard_map/ppermute | solution.py:22
  46.7 3.2 %collective-permute-done.8.refs_0_ = bf16[144,128]{1,0:T(8,128)(2,1)S(1)} collective-permute-done((bf16[144,128]{1,0:T(8,128)(2,1)S(1)}, bf16[144,128]{1,0:T(8,128)(2,1)S(1)}, u32[]{:S(2)}, u32[]{:S(2)}) %collective-permute-start.8) | collective-permute-done | bytes 36896 | tf_op jit(solution)/shard_map/ppermute | solution.py:22
  51.9 5.4 %collective-permute-start.11 = (bf16[144,128]{1,0:T(8,128)(2,1)S(1)}, bf16[144,128]{1,0:T(8,128)(2,1)S(1)}, u32[]{:S(2)}, u32[]{:S(2)}) collective-permute-start(bf16[144,128]{1,0:T(8,128)(2,1)S(1)} %bitcast.47), channel_id=1, source_target_pairs={{0,8},{8,16},{16,24},{24,32},{32,40},{40,48},{48,56},{1,9},{9,17},... | collective-permute-start | bytes 110600 | tf_op jit(solution)/shard_map/ppermute | solution.py:22
  59.0 3.0 %message_round.3 = (bf16[256,128]{1,0:T(8,128)(2,1)S(1)}, bf16[144,128]{1,0:T(8,128)(2,1)S(1)}, bf16[144,128]{1,0:T(8,128)(2,1)S(1)}, bf16[144,128]{1,0:T(8,128)(2,1)S(1)}) custom-call(bf16[256,128]{1,0:T(8,128)(2,1)S(1)} %get-tuple-element.26.latent_ref, bf16[144,128]{1,0:T(8,128)(2,1)S(1)} %collective-permute-done.10.g2, bf16[144,128]{1,0:T(8,128)(2,1)S(1)} %bitcast.29, ...), custom_call_target="tpu_custom_call" | custom-call | tf_op jit(solution)/shard_map/message_round/pallas_call | solution.py:242
  62.7 4.5 %collective-permute-start.13 = (bf16[144,128]{1,0:T(8,128)(2,1)S(1)}, bf16[144,128]{1,0:T(8,128)(2,1)S(1)}, u32[]{:S(2)}, u32[]{:S(2)}) collective-permute-start(bf16[144,128]{1,0:T(8,128)(2,1)S(1)} %get-tuple-element.32), channel_id=1, source_target_pairs={{0,1},{1,0},{2,3},{3,2},{4,5},{5,4},{6,7},{7,6},{8,9},{9,8},{10,11... | collective-permute-start | bytes 110600 | tf_op jit(solution)/shard_map/ppermute | solution.py:290
  68.1 3.4 %collective-permute-start.15 = (bf16[144,128]{1,0:T(8,128)(2,1)S(1)}, bf16[144,128]{1,0:T(8,128)(2,1)S(1)}, u32[]{:S(2)}, u32[]{:S(2)}) collective-permute-start(bf16[144,128]{1,0:T(8,128)(2,1)S(1)} %pad_maximum_fusion.14), channel_id=1, source_target_pairs={{64,0},{128,64},{192,128},{256,192},{320,256},{384,320},{448,384},... | collective-permute-start | bytes 110600 | tf_op jit(solution)/shard_map/ppermute | solution.py:22
  71.6 2.4 %collective-permute-start.14 = (bf16[144,128]{1,0:T(8,128)(2,1)S(1)}, bf16[144,128]{1,0:T(8,128)(2,1)S(1)}, u32[]{:S(2)}, u32[]{:S(2)}) collective-permute-start(bf16[144,128]{1,0:T(8,128)(2,1)S(1)} %pad_maximum_fusion.12), channel_id=1, source_target_pairs={{0,64},{64,128},{128,192},{192,256},{256,320},{320,384},{384,448},... | collective-permute-start | bytes 110600 | tf_op jit(solution)/shard_map/ppermute | solution.py:22
  74.0 4.1 %collective-permute-done.14.refs_0_ = bf16[144,128]{1,0:T(8,128)(2,1)S(1)} collective-permute-done((bf16[144,128]{1,0:T(8,128)(2,1)S(1)}, bf16[144,128]{1,0:T(8,128)(2,1)S(1)}, u32[]{:S(2)}, u32[]{:S(2)}) %collective-permute-start.14) | collective-permute-done | bytes 36896 | tf_op jit(solution)/shard_map/ppermute | solution.py:22
  78.2 2.1 %collective-permute-start.16 = (bf16[144,128]{1,0:T(8,128)(2,1)S(1)}, bf16[144,128]{1,0:T(8,128)(2,1)S(1)}, u32[]{:S(2)}, u32[]{:S(2)}) collective-permute-start(bf16[144,128]{1,0:T(8,128)(2,1)S(1)} %bitcast.41), channel_id=1, source_target_pairs={{8,0},{16,8},{24,16},{32,24},{40,32},{48,40},{56,48},{9,1},{17,9},... | collective-permute-start | bytes 110600 | tf_op jit(solution)/shard_map/ppermute | solution.py:22
  80.2 5.6 %collective-permute-start.17 = (bf16[144,128]{1,0:T(8,128)(2,1)S(1)}, bf16[144,128]{1,0:T(8,128)(2,1)S(1)}, u32[]{:S(2)}, u32[]{:S(2)}) collective-permute-start(bf16[144,128]{1,0:T(8,128)(2,1)S(1)} %bitcast.45), channel_id=1, source_target_pairs={{0,8},{8,16},{16,24},{24,32},{32,40},{40,48},{48,56},{1,9},{9,17},... | collective-permute-start | bytes 110600 | tf_op jit(solution)/shard_map/ppermute | solution.py:22
  87.3 4.3 %last_round.1 = (f32[18,256]{1,0:T(8,128)}, f32[36,18]{1,0:T(8,128)S(1)}, f32[36,18]{1,0:T(8,128)S(1)}, f32[36,18]{1,0:T(8,128)S(1)}) custom-call(bf16[256,128]{1,0:T(8,128)(2,1)S(1)} %get-tuple-element.30.latent_ref, bf16[144,128]{1,0:T(8,128)(2,1)S(1)} %collective-permute-done.16.g2, bf16[144,128]{1,0:T(8,128)(2,1)S(1)} %bitcast.28, ...), custom_call_target="tpu_custom_call" | custom-call | tf_op jit(solution)/shard_map/last_round/pallas_call | solution.py:242
  92.2 3.8 %collective-permute-start.19 = (f32[36,18]{1,0:T(8,128)S(1)}, f32[36,18]{1,0:T(8,128)S(1)}, u32[]{:S(2)}, u32[]{:S(2)}) collective-permute-start(f32[36,18]{1,0:T(8,128)S(1)} %get-tuple-element.36), channel_id=1, source_target_pairs={{0,1},{1,0},{2,3},{3,2},{4,5},{5,4},{6,7},{7,6},{8,9},{9,8},{10,11... | collective-permute-start | bytes 7784 | tf_op jit(solution)/shard_map/ppermute | solution.py:290
  96.9 3.9 %collective-permute-start.21 = (f32[36,18]{1,0:T(8,128)S(1)}, f32[36,18]{1,0:T(8,128)S(1)}, u32[]{:S(2)}, u32[]{:S(2)}) collective-permute-start(f32[36,18]{1,0:T(8,128)S(1)} %pad_maximum_fusion.20), channel_id=1, source_target_pairs={{64,0},{128,64},{192,128},{256,192},{320,256},{384,320},{448,384},... | collective-permute-start | bytes 7784 | tf_op jit(solution)/shard_map/ppermute | solution.py:22
  102.8 3.7 %collective-permute-done.20 = f32[36,18]{1,0:T(8,128)S(1)} collective-permute-done((f32[36,18]{1,0:T(8,128)S(1)}, f32[36,18]{1,0:T(8,128)S(1)}, u32[]{:S(2)}, u32[]{:S(2)}) %collective-permute-start.20) | collective-permute-done | bytes 2624 | tf_op jit(solution)/shard_map/ppermute | solution.py:22
  108.6 5.4 %collective-permute-start.22 = (f32[36,18]{1,0:T(8,128)S(1)}, f32[36,18]{1,0:T(8,128)S(1)}, u32[]{:S(2)}, u32[]{:S(2)}) collective-permute-start(f32[36,18]{1,0:T(8,128)S(1)} %reshape.200), channel_id=1, source_target_pairs={{0,8},{8,16},{16,24},{24,32},{32,40},{40,48},{48,56},{1,9},{9,17},... | collective-permute-start | bytes 7784 | tf_op jit(solution)/shard_map/ppermute | solution.py:22
  (124 shorter events, 24.1 us)
Async XLA Ops:
  3.1 9.9 %collective-permute-start = (bf16[144,128]{1,0:T(8,128)(2,1)}, bf16[144,128]{1,0:T(8,128)(2,1)S(1)}, u32[]{:S(2)}, u32[]{:S(2)}) collective-permute-start(bf16[144,128]{1,0:T(8,128)(2,1)} %get-tuple-element.21), channel_id=1, source_target_pairs={{1,2},{2,1},{3,4},{4,3},{5,6},{6,5},{9,10},{10,9},{11,12},{12,11},... | collective-permute-start | bytes 110600 | tf_op jit(solution)/shard_map/ppermute | solution.py:290
  3.9 9.1 %collective-permute-start.1 = (bf16[144,128]{1,0:T(8,128)(2,1)}, bf16[144,128]{1,0:T(8,128)(2,1)S(1)}, u32[]{:S(2)}, u32[]{:S(2)}) collective-permute-start(bf16[144,128]{1,0:T(8,128)(2,1)} %get-tuple-element.22), channel_id=1, source_target_pairs={{0,1},{1,0},{2,3},{3,2},{4,5},{5,4},{6,7},{7,6},{8,9},{9,8},{10,11... | collective-permute-start | bytes 110600 | tf_op jit(solution)/shard_map/ppermute | solution.py:290
  13.1 9.2 %collective-permute-start.3 = (bf16[144,128]{1,0:T(8,128)(2,1)S(1)}, bf16[144,128]{1,0:T(8,128)(2,1)S(1)}, u32[]{:S(2)}, u32[]{:S(2)}) collective-permute-start(bf16[144,128]{1,0:T(8,128)(2,1)S(1)} %pad_maximum_fusion.2), channel_id=1, source_target_pairs={{64,0},{128,64},{192,128},{256,192},{320,256},{384,320},{448,384},... | collective-permute-start | bytes 110600 | tf_op jit(solution)/shard_map/ppermute | solution.py:22
  16.4 6.0 %collective-permute-start.2 = (bf16[144,128]{1,0:T(8,128)(2,1)S(1)}, bf16[144,128]{1,0:T(8,128)(2,1)S(1)}, u32[]{:S(2)}, u32[]{:S(2)}) collective-permute-start(bf16[144,128]{1,0:T(8,128)(2,1)S(1)} %pad_maximum_fusion), channel_id=1, source_target_pairs={{0,64},{64,128},{128,192},{192,256},{256,320},{320,384},{384,448},... | collective-permute-start | bytes 110600 | tf_op jit(solution)/shard_map/ppermute | solution.py:22
  22.3 7.5 %collective-permute-start.4 = (bf16[144,128]{1,0:T(8,128)(2,1)S(1)}, bf16[144,128]{1,0:T(8,128)(2,1)S(1)}, u32[]{:S(2)}, u32[]{:S(2)}) collective-permute-start(bf16[144,128]{1,0:T(8,128)(2,1)S(1)} %bitcast.44), channel_id=1, source_target_pairs={{8,0},{16,8},{24,16},{32,24},{40,32},{48,40},{56,48},{9,1},{17,9},... | collective-permute-start | bytes 110600 | tf_op jit(solution)/shard_map/ppermute | solution.py:22
  24.3 7.1 %collective-permute-start.5 = (bf16[144,128]{1,0:T(8,128)(2,1)S(1)}, bf16[144,128]{1,0:T(8,128)(2,1)S(1)}, u32[]{:S(2)}, u32[]{:S(2)}) collective-permute-start(bf16[144,128]{1,0:T(8,128)(2,1)S(1)} %bitcast.50), channel_id=1, source_target_pairs={{0,8},{8,16},{16,24},{24,32},{32,40},{40,48},{48,56},{1,9},{9,17},... | collective-permute-start | bytes 110600 | tf_op jit(solution)/shard_map/ppermute | solution.py:22
  34.5 5.5 %collective-permute-start.6 = (bf16[144,128]{1,0:T(8,128)(2,1)S(1)}, bf16[144,128]{1,0:T(8,128)(2,1)S(1)}, u32[]{:S(2)}, u32[]{:S(2)}) collective-permute-start(bf16[144,128]{1,0:T(8,128)(2,1)S(1)} %get-tuple-element.27), channel_id=1, source_target_pairs={{1,2},{2,1},{3,4},{4,3},{5,6},{6,5},{9,10},{10,9},{11,12},{12,11},... | collective-permute-start | bytes 110600 | tf_op jit(solution)/shard_map/ppermute | solution.py:290
  35.2 5.6 %collective-permute-start.7 = (bf16[144,128]{1,0:T(8,128)(2,1)S(1)}, bf16[144,128]{1,0:T(8,128)(2,1)S(1)}, u32[]{:S(2)}, u32[]{:S(2)}) collective-permute-start(bf16[144,128]{1,0:T(8,128)(2,1)S(1)} %get-tuple-element.28), channel_id=1, source_target_pairs={{0,1},{1,0},{2,3},{3,2},{4,5},{5,4},{6,7},{7,6},{8,9},{9,8},{10,11... | collective-permute-start | bytes 110600 | tf_op jit(solution)/shard_map/ppermute | solution.py:290
  40.8 5.9 %collective-permute-start.9 = (bf16[144,128]{1,0:T(8,128)(2,1)S(1)}, bf16[144,128]{1,0:T(8,128)(2,1)S(1)}, u32[]{:S(2)}, u32[]{:S(2)}) collective-permute-start(bf16[144,128]{1,0:T(8,128)(2,1)S(1)} %pad_maximum_fusion.8), channel_id=1, source_target_pairs={{64,0},{128,64},{192,128},{256,192},{320,256},{384,320},{448,384},... | collective-permute-start | bytes 110600 | tf_op jit(solution)/shard_map/ppermute | solution.py:22
  44.1 5.9 %collective-permute-start.8 = (bf16[144,128]{1,0:T(8,128)(2,1)S(1)}, bf16[144,128]{1,0:T(8,128)(2,1)S(1)}, u32[]{:S(2)}, u32[]{:S(2)}) collective-permute-start(bf16[144,128]{1,0:T(8,128)(2,1)S(1)} %pad_maximum_fusion.6), channel_id=1, source_target_pairs={{0,64},{64,128},{128,192},{192,256},{256,320},{320,384},{384,448},... | collective-permute-start | bytes 110600 | tf_op jit(solution)/shard_map/ppermute | solution.py:22
  50.0 8.6 %collective-permute-start.10 = (bf16[144,128]{1,0:T(8,128)(2,1)S(1)}, bf16[144,128]{1,0:T(8,128)(2,1)S(1)}, u32[]{:S(2)}, u32[]{:S(2)}) collective-permute-start(bf16[144,128]{1,0:T(8,128)(2,1)S(1)} %bitcast.42), channel_id=1, source_target_pairs={{8,0},{16,8},{24,16},{32,24},{40,32},{48,40},{56,48},{9,1},{17,9},... | collective-permute-start | bytes 110600 | tf_op jit(solution)/shard_map/ppermute | solution.py:22
  51.9 7.1 %collective-permute-start.11 = (bf16[144,128]{1,0:T(8,128)(2,1)S(1)}, bf16[144,128]{1,0:T(8,128)(2,1)S(1)}, u32[]{:S(2)}, u32[]{:S(2)}) collective-permute-start(bf16[144,128]{1,0:T(8,128)(2,1)S(1)} %bitcast.47), channel_id=1, source_target_pairs={{0,8},{8,16},{16,24},{24,32},{32,40},{40,48},{48,56},{1,9},{9,17},... | collective-permute-start | bytes 110600 | tf_op jit(solution)/shard_map/ppermute | solution.py:22
  62.0 5.2 %collective-permute-start.12 = (bf16[144,128]{1,0:T(8,128)(2,1)S(1)}, bf16[144,128]{1,0:T(8,128)(2,1)S(1)}, u32[]{:S(2)}, u32[]{:S(2)}) collective-permute-start(bf16[144,128]{1,0:T(8,128)(2,1)S(1)} %get-tuple-element.31), channel_id=1, source_target_pairs={{1,2},{2,1},{3,4},{4,3},{5,6},{6,5},{9,10},{10,9},{11,12},{12,11},... | collective-permute-start | bytes 110600 | tf_op jit(solution)/shard_map/ppermute | solution.py:290
  62.7 5.3 %collective-permute-start.13 = (bf16[144,128]{1,0:T(8,128)(2,1)S(1)}, bf16[144,128]{1,0:T(8,128)(2,1)S(1)}, u32[]{:S(2)}, u32[]{:S(2)}) collective-permute-start(bf16[144,128]{1,0:T(8,128)(2,1)S(1)} %get-tuple-element.32), channel_id=1, source_target_pairs={{0,1},{1,0},{2,3},{3,2},{4,5},{5,4},{6,7},{7,6},{8,9},{9,8},{10,11... | collective-permute-start | bytes 110600 | tf_op jit(solution)/shard_map/ppermute | solution.py:290
  68.1 5.9 %collective-permute-start.15 = (bf16[144,128]{1,0:T(8,128)(2,1)S(1)}, bf16[144,128]{1,0:T(8,128)(2,1)S(1)}, u32[]{:S(2)}, u32[]{:S(2)}) collective-permute-start(bf16[144,128]{1,0:T(8,128)(2,1)S(1)} %pad_maximum_fusion.14), channel_id=1, source_target_pairs={{64,0},{128,64},{192,128},{256,192},{320,256},{384,320},{448,384},... | collective-permute-start | bytes 110600 | tf_op jit(solution)/shard_map/ppermute | solution.py:22
  71.6 6.5 %collective-permute-start.14 = (bf16[144,128]{1,0:T(8,128)(2,1)S(1)}, bf16[144,128]{1,0:T(8,128)(2,1)S(1)}, u32[]{:S(2)}, u32[]{:S(2)}) collective-permute-start(bf16[144,128]{1,0:T(8,128)(2,1)S(1)} %pad_maximum_fusion.12), channel_id=1, source_target_pairs={{0,64},{64,128},{128,192},{192,256},{256,320},{320,384},{384,448},... | collective-permute-start | bytes 110600 | tf_op jit(solution)/shard_map/ppermute | solution.py:22
  78.2 8.9 %collective-permute-start.16 = (bf16[144,128]{1,0:T(8,128)(2,1)S(1)}, bf16[144,128]{1,0:T(8,128)(2,1)S(1)}, u32[]{:S(2)}, u32[]{:S(2)}) collective-permute-start(bf16[144,128]{1,0:T(8,128)(2,1)S(1)} %bitcast.41), channel_id=1, source_target_pairs={{8,0},{16,8},{24,16},{32,24},{40,32},{48,40},{56,48},{9,1},{17,9},... | collective-permute-start | bytes 110600 | tf_op jit(solution)/shard_map/ppermute | solution.py:22
  80.2 7.1 %collective-permute-start.17 = (bf16[144,128]{1,0:T(8,128)(2,1)S(1)}, bf16[144,128]{1,0:T(8,128)(2,1)S(1)}, u32[]{:S(2)}, u32[]{:S(2)}) collective-permute-start(bf16[144,128]{1,0:T(8,128)(2,1)S(1)} %bitcast.45), channel_id=1, source_target_pairs={{0,8},{8,16},{16,24},{24,32},{32,40},{40,48},{48,56},{1,9},{9,17},... | collective-permute-start | bytes 110600 | tf_op jit(solution)/shard_map/ppermute | solution.py:22
  91.6 4.4 %collective-permute-start.18 = (f32[36,18]{1,0:T(8,128)S(1)}, f32[36,18]{1,0:T(8,128)S(1)}, u32[]{:S(2)}, u32[]{:S(2)}) collective-permute-start(f32[36,18]{1,0:T(8,128)S(1)} %get-tuple-element.35), channel_id=1, source_target_pairs={{1,2},{2,1},{3,4},{4,3},{5,6},{6,5},{9,10},{10,9},{11,12},{12,11},... | collective-permute-start | bytes 7784 | tf_op jit(solution)/shard_map/ppermute | solution.py:290
  92.2 4.6 %collective-permute-start.19 = (f32[36,18]{1,0:T(8,128)S(1)}, f32[36,18]{1,0:T(8,128)S(1)}, u32[]{:S(2)}, u32[]{:S(2)}) collective-permute-start(f32[36,18]{1,0:T(8,128)S(1)} %get-tuple-element.36), channel_id=1, source_target_pairs={{0,1},{1,0},{2,3},{3,2},{4,5},{5,4},{6,7},{7,6},{8,9},{9,8},{10,11... | collective-permute-start | bytes 7784 | tf_op jit(solution)/shard_map/ppermute | solution.py:290
  96.9 5.9 %collective-permute-start.21 = (f32[36,18]{1,0:T(8,128)S(1)}, f32[36,18]{1,0:T(8,128)S(1)}, u32[]{:S(2)}, u32[]{:S(2)}) collective-permute-start(f32[36,18]{1,0:T(8,128)S(1)} %pad_maximum_fusion.20), channel_id=1, source_target_pairs={{64,0},{128,64},{192,128},{256,192},{320,256},{384,320},{448,384},... | collective-permute-start | bytes 7784 | tf_op jit(solution)/shard_map/ppermute | solution.py:22
  100.9 5.7 %collective-permute-start.20 = (f32[36,18]{1,0:T(8,128)S(1)}, f32[36,18]{1,0:T(8,128)S(1)}, u32[]{:S(2)}, u32[]{:S(2)}) collective-permute-start(f32[36,18]{1,0:T(8,128)S(1)} %pad_maximum_fusion.18), channel_id=1, source_target_pairs={{0,64},{64,128},{128,192},{192,256},{256,320},{320,384},{384,448},... | collective-permute-start | bytes 7784 | tf_op jit(solution)/shard_map/ppermute | solution.py:22
  106.6 7.4 %collective-permute-start.23 = (f32[36,18]{1,0:T(8,128)S(1)}, f32[36,18]{1,0:T(8,128)S(1)}, u32[]{:S(2)}, u32[]{:S(2)}) collective-permute-start(f32[36,18]{1,0:T(8,128)S(1)} %reshape.201), channel_id=1, source_target_pairs={{8,0},{16,8},{24,16},{32,24},{40,32},{48,40},{56,48},{9,1},{17,9},... | collective-permute-start | bytes 7784 | tf_op jit(solution)/shard_map/ppermute | solution.py:22
  108.6 6.9 %collective-permute-start.22 = (f32[36,18]{1,0:T(8,128)S(1)}, f32[36,18]{1,0:T(8,128)S(1)}, u32[]{:S(2)}, u32[]{:S(2)}) collective-permute-start(f32[36,18]{1,0:T(8,128)S(1)} %reshape.200), channel_id=1, source_target_pairs={{0,8},{8,16},{16,24},{24,32},{32,40},{40,48},{48,56},{1,9},{9,17},... | collective-permute-start | bytes 7784 | tf_op jit(solution)/shard_map/ppermute | solution.py:22
  (15 other events, 144.1 us)
